TPU v7x, 32 devices: a whole 2x2x4 slice. The times are simulated.
32 devices in a mesh: seg: 2 (over x), rad: 4 (over y, core), ax: 4 (over z).
Axes of the slice: x: 2, y: 2, z: 4, core: 2. Of those that a mesh axis runs over, the one named last changes fastest.
Arguments:
- start_states: float32 [4, 3, 16, 192, 384], P('seg', None, 'ax', 'rad'), may hold values from -4.2 to 4.2
- radial_inverse: float32 [192, 192, 192], P('ax'), may hold values from 0 to 1.2, as said below
- offsets: int32 [4], P('seg'), may hold values from 0 to 15
- mode_count: int32 [1], replicated, may hold values from 128 to 192
Outputs:
- residual: float32 [4, 3, 16, 192, 384], P('seg', None, 'ax', 'rad')
Inputs may be any that keep to these rules, and one draw needn't show every extreme that they name: `radial_inverse`: for each mode, a dense matrix with positive entries.
All inputs are finite; a program needn't handle non-finite values.
Results may differ from a plain program's by a relative error of at most 0.0001.
Values sent between devices are 32-bit elements; how exact they have to be, the bound alone decides.
No kernel may reach another device: no remote copies, remote signals or barrier semaphores. Data moves between devices by JAX's collectives and lax.ppermute only.
A program may use at most 128 MiB of HBM per device.

v0:
```python
import math

import jax
import jax.numpy as jnp
from jax import lax
from jax.sharding import PartitionSpec as P

STEPS = 2


highest = lax.Precision.HIGHEST


def passed_along(value, axis, steps):
    count = lax.axis_size(axis)
    pairs = [(source, (source + steps) % count) for source in range(count)]
    return lax.ppermute(value, axis, pairs)


def padded_2(array, sides, width):
    for axis, dim in sides:
        peers, length = (lax.axis_size(axis), array.shape[dim])
        up = [(i, (i + 1) % peers) for i in range(peers)]
        down = [(j, i) for i, j in up]
        last = lax.slice_in_dim(array, length - width, length, axis=dim)
        leading = lax.slice_in_dim(array, 0, width, axis=dim)
        before = lax.ppermute(last, axis, up)
        after = lax.ppermute(leading, axis, down)
        array = jnp.concatenate([before, array, after], axis=dim)
    return array


def fourier_tables(columns, kept_modes):
    modes_total = columns // 2
    row_index = lax.broadcasted_iota(jnp.int32, (columns, columns), 0)
    point_index = lax.broadcasted_iota(jnp.int32, (columns, columns), 1)
    mode_index = row_index // 2
    phase = (mode_index * point_index % columns).astype(jnp.float32) * (2.0 * math.pi / columns)
    even_rows = row_index % 2 == 0
    cosine = jnp.cos(phase)
    sine = jnp.sin(phase)
    root = math.sqrt(modes_total)
    synthesis = jnp.where(even_rows, cosine, sine) / root
    weights = jnp.where(mode_index == 0, 1.0, 2.0)
    analysis = jnp.where(even_rows, weights * cosine, 2.0 * sine) * (root / columns)
    analysis = jnp.where(mode_index < kept_modes, analysis, 0.0)
    return (synthesis, analysis)


def radial_solve(pencils, radial_inverse, radial_rows):
    local_modes = radial_inverse.shape[0]
    local_columns, members, axial_cells, ignored = pencils.shape
    own_rows = lax.dynamic_slice_in_dim(
        radial_inverse, lax.axis_index("rad") * radial_rows, radial_rows, 1
    )
    piece = lax.all_gather(pencils, "rad", axis=3, tiled=True)
    piece_rows = piece.shape[3]
    grouped = piece.reshape(local_modes, 2, members, axial_cells, piece_rows)
    product = jnp.einsum("mrs,mkqzs->mkqzr", own_rows, grouped, precision=highest)
    return product.reshape(local_columns, members, axial_cells, radial_rows)


def body(start_states, radial_inverse, offsets, mode_count):
    groups, components, axial_rows, radial_rows, columns = start_states.shape
    synthesis, analysis = fourier_tables(columns, mode_count[0])
    radius = (
        (lax.axis_index("rad") * radial_rows + jnp.arange(radial_rows)).astype(jnp.float32) + 0.5
    ) / (radial_rows * lax.axis_size("rad"))
    profile = (1.0 - radius * radius).reshape(1, 1, 1, radial_rows, 1)
    following = passed_along(start_states[0], "seg", -1)
    current = start_states
    for step_index in range(STEPS):
        if step_index == 0:
            physical = jnp.einsum("gczrj,jp->gczrp", current, synthesis, precision=highest)
        else:
            physical = jnp.einsum("jgczr,jp->gczrp", current, synthesis, precision=highest)
        padded = padded_2(physical, (("ax", 2),), 1)
        gradient = (padded[:, :, 2:] - padded[:, :, :-2]) * 20.0
        advecting = profile + padded[:, 2:3, 1:-1]
        forcing = physical - 0.02 * advecting * gradient
        spectral = jnp.einsum("gczrp,jp->jgczr", forcing, analysis, precision=highest)
        pencils = lax.all_to_all(spectral, "ax", split_axis=0, concat_axis=3, tiled=True)
        local_columns = pencils.shape[0]
        axial_cells = pencils.shape[3]
        pencils = pencils.reshape(local_columns, groups * components, axial_cells, radial_rows)
        solved = radial_solve(pencils, radial_inverse, radial_rows)
        if step_index == STEPS - 1:
            blocks = solved.reshape(local_columns, groups, components, axial_cells, radial_rows)
            shifted = [
                jnp.roll(blocks[:, member], offsets[member], axis=2) for member in range(groups)
            ]
            solved = jnp.stack(shifted, axis=1).reshape(
                local_columns, groups * components, axial_cells, radial_rows
            )
        returned = lax.all_to_all(solved, "ax", split_axis=2, concat_axis=0, tiled=True)
        current = returned.reshape(columns, groups, components, axial_rows, radial_rows)
    ending = jnp.transpose(current, (1, 2, 3, 4, 0))
    upcoming = jnp.concatenate([start_states[1:], following[None]], axis=0)
    return ending - upcoming


def solution(mesh):
    placed = (P("seg", None, "ax", "rad", None), P("ax", None, None), P("seg"), P())
    return jax.shard_map(
        body,
        mesh=mesh,
        in_specs=placed,
        out_specs=P("seg", None, "ax", "rad", None),
        check_vma=False,
    )
```

profile of v0, /device:TPU:1, one launch (start us, length us, event | category | flops | bytes accessed | tf_op | source)
XLA Modules:
  0.0 550.8 jit_solution(4344185242859229900)
XLA Ops:
  6.6 7.4 %convolution_bitcast_fusion = f32[2,3,4,48,384]{4,3,2,1,0:T(8,128)S(1)} fusion(f32[2,3,4,48,384]{4,3,2,1,0:T(8,128)} %param.6, s32[384]{0:T(512)S(1)} %get-tuple-element.19, s32[384]{0:T(512)S(1)} %get-tuple-element.20, s32[384]{0:T(512)S(1)} %get-tuple-element.18, s32[384]{0:T(512)S(1)} %get-tuple-element.21, pred[384]{0:T(512)(128)(4,1)S(1)} %get-tuple-element.17, ...), kind=kOutput, calls=%fused_computation.33 | convolution fusion | flops 2040496128 | bytes 3545856 | tf_op jit(solution)/shard_map/gczrj,jp->gczrp/dot_general | solution.py:74
  14.1 4.2 collective-permute-start
  19.4 7.8 %collective-permute-done = f32[2,3,1,48,384]{4,3,2,1,0:T(8,128)S(1)} collective-permute-done((f32[2,3,1,48,384]{4,3,2,1,0:T(8,128)S(1)}, f32[2,3,1,48,384]{4,3,2,1,0:T(8,128)S(1)}, u32[]{:S(2)}, u32[]{:S(2)}) %collective-permute-start) | collective-permute-done | bytes 442400 | tf_op jit(solution)/shard_map/ppermute | solution.py:28
  27.2 10.3 %collective-permute-done.1 = f32[2,3,1,48,384]{4,3,2,1,0:T(8,128)S(1)} collective-permute-done((f32[2,3,1,48,384]{4,3,2,1,0:T(8,128)S(1)}, f32[2,3,1,48,384]{4,3,2,1,0:T(8,128)S(1)}, u32[]{:S(2)}, u32[]{:S(2)}) %collective-permute-start.1) | collective-permute-done | bytes 442400 | tf_op jit(solution)/shard_map/ppermute | solution.py:27
  37.5 0.8 copy-done.4
  38.3 7.2 %fusion.18 = f32[384,2,3,4,48]{0,4,3,2,1:T(8,128)S(1)} fusion(f32[2,3,4,48,384]{4,3,2,1,0:T(8,128)S(1)} %convolution_bitcast_fusion, f32[2,3,1,48,384]{4,3,2,1,0:T(8,128)} %copy-done.4, f32[2,3,1,48,384]{4,3,2,1,0:T(8,128)} %copy-done.3, f32[2,4,48,384]{3,2,1,0:T(8,128)S(1)} %fusion.30, s32[384]{0:T(512)S(1)} %get-tuple-element.19, ...), kind=kOutput, calls=%fused_computation.28 | convolution fusion | flops 2043592704 | bytes 5020420 | tf_op jit(solution)/shard_map/gczrp,jp->jgczr/dot_general | solution.py:81
  45.5 4.0 copy.32
  49.6 6.6 %reshape.55 = f32[4,1,110592]{2,1,0:T(1,128)S(1)} reshape(f32[384,2,3,4,48]{4,3,2,1,0:T(4,128)} %copy.32) | data formatting | bytes 3538944
  56.2 42.9 %all_to_all.60 = f32[4,1,110592]{2,1,0:T(1,128)S(1)} all-to-all(f32[4,1,110592]{2,1,0:T(1,128)S(1)} %reshape.55), channel_id=1, replica_groups=mesh['seg'=2,'rad'=4,'ax'=4] {'ax'}, dimensions={0} | all-to-all | bytes 3538944 | tf_op jit(solution)/shard_map/all_to_all | solution.py:82
  99.6 5.8 %reduce = f32[4,110592]{1,0:T(4,128)S(1)} reduce(f32[4,1,110592]{2,1,0:T(1,128)S(1)} %all_to_all.60, f32[]{:T(128)} %broadcast.69), dimensions={1}, to_apply=%all_to_all.44.reduce_sub_computation | reduce | bytes 3538948 | tf_op jit(solution)/shard_map/all_to_all | solution.py:82
  105.3 6.9 %reshape.56 = f32[384,2,3,4,48]{4,3,2,1,0:T(4,128)} reshape(f32[4,110592]{1,0:T(4,128)S(1)} %reduce) | data formatting | bytes 3538944
  112.2 5.0 copy.34
  117.5 65.3 %all-gather.3.cloned.1.call-done = f32[96,6,16,192]{0,3,2,1:T(8,128)} async-done(((f32[96,6,16,48]{0,3,2,1:T(8,128)}), f32[96,6,16,192]{0,3,2,1:T(8,128)}) %all-gather.3.cloned.1.call-update) | async-done | bytes 7077904 | tf_op jit(solution)/shard_map/all_gather | solution.py:56
  182.8 11.5 %copy.35 = f32[96,6,16,192]{3,2,1,0:T(8,128)} copy(f32[96,6,16,192]{0,3,2,1:T(8,128)} %all-gather.3.cloned.1.call-done) | data formatting | bytes 14155776 | tf_op jit(solution)/shard_map/all_gather | solution.py:56
  194.3 13.3 %fusion.4 = f32[48,2,6,16,48]{4,3,2,1,0:T(8,128)} fusion(f32[48,2,6,16,192]{4,3,2,1,0:T(8,128)} %bitcast.74, f32[48,192,192]{2,1,0:T(8,128)} %param.7, s32[]{:T(128)S(6)} %select_n.67), kind=kOutput, calls=%fused_computation.11 | convolution fusion | flops 1019215872 | bytes 13565956 | tf_op jit(solution)/shard_map/mrs,mkqzs->mkqzr/dot_general | solution.py:59
  207.6 4.5 copy.36
  212.1 57.7 %all_to_all.61 = f32[96,6,16,48]{0,3,1,2:T(8,128)S(1)} all-to-all(f32[96,6,16,48]{0,3,1,2:T(8,128)S(1)} %copy.36), channel_id=1, replica_groups=mesh['seg'=2,'rad'=4,'ax'=4] {'ax'}, dimensions={2} | all-to-all | bytes 3538944 | tf_op jit(solution)/shard_map/all_to_all | solution.py:95
  269.8 1.5 copy.56
  271.3 2.4 reshape.47
  273.7 7.6 %fusion.31 = f32[2,3,4,48,384]{4,3,2,1,0:T(8,128)S(1)} fusion(f32[384,2,3,4,48]{0,4,3,2,1:T(8,128)} %reshape.47, s32[384]{0:T(512)S(1)} %get-tuple-element.19, s32[384]{0:T(512)S(1)} %get-tuple-element.20, s32[384]{0:T(512)S(1)} %get-tuple-element.18, s32[384]{0:T(512)S(1)} %copy-done.1, pred[384]{0:T(512)(128)(4,1)S(1)} %copy-done.8, ...), kind=kOutput, calls=%fused_computation.50 | convolution fusion | flops 2040496128 | bytes 3545856 | tf_op jit(solution)/shard_map/jgczr,jp->gczrp/dot_general | solution.py:76
  281.4 1.5 collective-permute-start.2
  283.3 8.4 %collective-permute-done.2 = f32[2,3,1,48,384]{4,3,2,1,0:T(8,128)S(1)} collective-permute-done((f32[2,3,1,48,384]{4,3,2,1,0:T(8,128)S(1)}, f32[2,3,1,48,384]{4,3,2,1,0:T(8,128)S(1)}, u32[]{:S(2)}, u32[]{:S(2)}) %collective-permute-start.2) | collective-permute-done | bytes 442400 | tf_op jit(solution)/shard_map/ppermute | solution.py:28
  291.8 9.9 %collective-permute-done.3 = f32[2,3,1,48,384]{4,3,2,1,0:T(8,128)S(1)} collective-permute-done((f32[2,3,1,48,384]{4,3,2,1,0:T(8,128)S(1)}, f32[2,3,1,48,384]{4,3,2,1,0:T(8,128)S(1)}, u32[]{:S(2)}, u32[]{:S(2)}) %collective-permute-start.3) | collective-permute-done | bytes 442400 | tf_op jit(solution)/shard_map/ppermute | solution.py:27
  301.7 6.1 %fusion.11 = f32[384,2,3,4,48]{0,4,3,2,1:T(8,128)S(1)} fusion(f32[2,3,4,48,384]{4,3,2,1,0:T(8,128)S(1)} %fusion.31, f32[2,3,1,48,384]{4,3,2,1,0:T(8,128)S(1)} %collective-permute-done.3, f32[2,3,1,48,384]{4,3,2,1,0:T(8,128)S(1)} %collective-permute-done.2, f32[2,4,48,384]{3,2,1,0:T(8,128)S(1)} %fusion.28, s32[384]{0:T(512)S(1)} %get-tuple-element.19, ...), kind=kOutput, calls=%fused_computation.20 | convolution fusion | flops 2043592704 | bytes 5020420 | tf_op jit(solution)/shard_map/gczrp,jp->jgczr/dot_general | solution.py:81
  307.8 4.0 copy.38
  311.9 6.6 %reshape.57 = f32[4,1,110592]{2,1,0:T(1,128)S(1)} reshape(f32[384,2,3,4,48]{4,3,2,1,0:T(4,128)} %copy.38) | data formatting | bytes 3538944
  318.4 43.2 %all_to_all.62 = f32[4,1,110592]{2,1,0:T(1,128)S(1)} all-to-all(f32[4,1,110592]{2,1,0:T(1,128)S(1)} %reshape.57), channel_id=1, replica_groups=mesh['seg'=2,'rad'=4,'ax'=4] {'ax'}, dimensions={0} | all-to-all | bytes 3538944 | tf_op jit(solution)/shard_map/all_to_all | solution.py:82
  361.6 5.8 %reduce.1 = f32[4,110592]{1,0:T(4,128)S(1)} reduce(f32[4,1,110592]{2,1,0:T(1,128)S(1)} %all_to_all.62, f32[]{:T(128)} %broadcast.69), dimensions={1}, to_apply=%all_to_all.50.reduce_sub_computation | reduce | bytes 3538948 | tf_op jit(solution)/shard_map/all_to_all | solution.py:82
  367.4 6.9 %reshape.58 = f32[384,2,3,4,48]{4,3,2,1,0:T(4,128)} reshape(f32[4,110592]{1,0:T(4,128)S(1)} %reduce.1) | data formatting | bytes 3538944
  374.3 5.0 copy.40
  379.3 0.6 copy-done.2
  384.2 59.7 %all-gather.5.cloned.1.call-done = f32[96,6,16,192]{0,3,2,1:T(8,128)} async-done(((f32[96,6,16,48]{0,3,2,1:T(8,128)}), f32[96,6,16,192]{0,3,2,1:T(8,128)}) %all-gather.5.cloned.1.call-update) | async-done | bytes 7077904 | tf_op jit(solution)/shard_map/all_gather | solution.py:56
  443.8 11.5 %copy.41 = f32[96,6,16,192]{3,2,1,0:T(8,128)} copy(f32[96,6,16,192]{0,3,2,1:T(8,128)} %all-gather.5.cloned.1.call-done) | data formatting | bytes 14155776 | tf_op jit(solution)/shard_map/all_gather | solution.py:56
  455.4 11.9 %fusion.2 = f32[48,2,6,16,48]{4,3,2,1,0:T(8,128)S(1)} fusion(f32[48,2,6,16,192]{4,3,2,1,0:T(8,128)} %bitcast.73, f32[48,192,192]{2,1,0:T(8,128)} %param.7, s32[]{:T(128)S(6)} %select_n.67), kind=kOutput, calls=%fused_computation.9 | convolution fusion | flops 1019215872 | bytes 13565956 | tf_op jit(solution)/shard_map/mrs,mkqzs->mkqzr/dot_general | solution.py:59
  467.3 1.8 slice_bitcast_fusion.1
  469.1 0.8 fusion.1
  469.9 0.9 copy.42
  470.8 2.5 fusion
  473.2 1.7 copy.43
  475.0 1.5 pad_maximum_fusion
  476.4 1.7 copy.44
  478.1 4.3 all-to-all-start.3
  482.4 2.5 fusion.75
  484.9 1.5 collective-permute-start.4
  486.4 49.4 %all-to-all-done.3 = f32[96,6,16,48]{0,3,1,2:T(8,128)S(1)} async-done(((f32[96,6,16,48]{0,3,1,2:T(8,128)}), f32[96,6,16,48]{0,3,1,2:T(8,128)S(1)}, u32[]{:S(2)}, u32[]{:S(2)}) %all-to-all-start.3) | async-done | bytes 1769504 | tf_op jit(solution)/shard_map/all_to_all | solution.py:95
  535.8 3.0 copy.46
  538.8 2.4 reshape.51
  541.2 2.6 maximum_subtract_fusion
  (33 shorter events, 2.3 us)
Async XLA Ops:
  6.5 176.3 %all-gather.3.cloned.1.call-start = ((), (), s32[]{:S(2)}) async-start(), calls=%async_computation.4 | async-start | bytes 11796480 | tf_op jit(solution)/shard_map/all_gather | solution.py:56
  6.5 7.4 %copy-start = (s32[384]{0:T(512)}, s32[384]{0:T(512)S(1)}, u32[]{:S(2)}) copy-start(s32[384]{0:T(512)S(1)} %get-tuple-element.21) | copy-start | bytes 4612
  6.6 7.4 %copy-start.5 = (pred[384]{0:T(512)(128)(4,1)}, pred[384]{0:T(512)(128)(4,1)S(1)}, u32[]{:S(2)}) copy-start(pred[384]{0:T(512)(128)(4,1)S(1)} %get-tuple-element.16) | copy-start | bytes 1156
  6.6 7.4 %copy-start.7 = (pred[384]{0:T(512)(128)(4,1)}, pred[384]{0:T(512)(128)(4,1)S(1)}, u32[]{:S(2)}) copy-start(pred[384]{0:T(512)(128)(4,1)S(1)} %get-tuple-element.17) | copy-start | bytes 1156
  14.1 13.1 %collective-permute-start = (f32[2,3,1,48,384]{4,3,2,1,0:T(8,128)S(1)}, f32[2,3,1,48,384]{4,3,2,1,0:T(8,128)S(1)}, u32[]{:S(2)}, u32[]{:S(2)}) collective-permute-start(f32[2,3,1,48,384]{4,3,2,1,0:T(8,128)S(1)} %get-tuple-element.10), channel_id=1, source_target_pairs={{1,0},{2,1},{3,2},{0,3},{5,4},{6,5},{7,6},{4,7},{9,8},{10,9},{11,1... | collective-permute-start | bytes 1327112 | tf_op jit(solution)/shard_map/ppermute | solution.py:28
  18.3 19.2 %collective-permute-start.1 = (f32[2,3,1,48,384]{4,3,2,1,0:T(8,128)S(1)}, f32[2,3,1,48,384]{4,3,2,1,0:T(8,128)S(1)}, u32[]{:S(2)}, u32[]{:S(2)}) collective-permute-start(f32[2,3,1,48,384]{4,3,2,1,0:T(8,128)S(1)} %get-tuple-element.11), channel_id=1, source_target_pairs={{0,1},{1,2},{2,3},{3,0},{4,5},{5,6},{6,7},{7,4},{8,9},{9,10},{10,1... | collective-permute-start | bytes 1327112 | tf_op jit(solution)/shard_map/ppermute | solution.py:27
  27.2 10.3 %copy-start.3 = (f32[2,3,1,48,384]{4,3,2,1,0:T(8,128)}, f32[2,3,1,48,384]{4,3,2,1,0:T(8,128)S(1)}, u32[]{:S(2)}) copy-start(f32[2,3,1,48,384]{4,3,2,1,0:T(8,128)S(1)} %collective-permute-done) | copy-start | bytes 1327108
  37.5 0.8 copy-start.4
  117.2 326.6 %all-gather.5.cloned.1.call-start = ((), (), s32[]{:S(2)}) async-start(), calls=%async_computation.5 | async-start | bytes 11796480 | tf_op jit(solution)/shard_map/all_gather | solution.py:56
  271.3 2.4 copy-start.1
  271.3 2.4 copy-start.6
  271.3 2.4 copy-start.8
  281.4 10.3 %collective-permute-start.2 = (f32[2,3,1,48,384]{4,3,2,1,0:T(8,128)S(1)}, f32[2,3,1,48,384]{4,3,2,1,0:T(8,128)S(1)}, u32[]{:S(2)}, u32[]{:S(2)}) collective-permute-start(f32[2,3,1,48,384]{4,3,2,1,0:T(8,128)S(1)} %get-tuple-element.8), channel_id=1, source_target_pairs={{1,0},{2,1},{3,2},{0,3},{5,4},{6,5},{7,6},{4,7},{9,8},{10,9},{11,1... | collective-permute-start | bytes 1327112 | tf_op jit(solution)/shard_map/ppermute | solution.py:28
  283.0 18.7 %collective-permute-start.3 = (f32[2,3,1,48,384]{4,3,2,1,0:T(8,128)S(1)}, f32[2,3,1,48,384]{4,3,2,1,0:T(8,128)S(1)}, u32[]{:S(2)}, u32[]{:S(2)}) collective-permute-start(f32[2,3,1,48,384]{4,3,2,1,0:T(8,128)S(1)} %get-tuple-element.9), channel_id=1, source_target_pairs={{0,1},{1,2},{2,3},{3,0},{4,5},{5,6},{6,7},{7,4},{8,9},{9,10},{10,1... | collective-permute-start | bytes 1327112 | tf_op jit(solution)/shard_map/ppermute | solution.py:27
  379.3 0.7 copy-start.2
  478.1 57.7 %all-to-all-start.3 = ((f32[96,6,16,48]{0,3,1,2:T(8,128)}), f32[96,6,16,48]{0,3,1,2:T(8,128)S(1)}, u32[]{:S(2)}, u32[]{:S(2)}) async-start(f32[96,6,16,48]{0,3,1,2:T(8,128)} %copy.44), calls=%async_computation.3 | async-start | bytes 4718592 | tf_op jit(solution)/shard_map/all_to_all | solution.py:95
  484.9 56.3 %collective-permute-start.4 = (f32[3,4,48,384]{3,2,1,0:T(8,128)}, f32[3,4,48,384]{3,2,1,0:T(8,128)}, u32[]{:S(2)}, u32[]{:S(2)}) collective-permute-start(f32[3,4,48,384]{3,2,1,0:T(8,128)} %get-tuple-element.13), channel_id=1, source_target_pairs={{0,16},{16,0},{1,17},{17,1},{2,18},{18,2},{3,19},{19,3},{4,20},{20... | collective-permute-start | bytes 2654216 | tf_op jit(solution)/shard_map/ppermute | solution.py:17
Sparse Core Ops, SparseCore 0:
  117.4 65.3 all-gather.2
  379.4 64.3 all-gather.4
where the time goes:
time: 558 us; the launch traced here: 551 us
  waiting for transfers between devices  211 us (38%)
  blocking collectives  144 us (26%)
  local copies, waits for them, and re-layouts  93 us (17%)
  matrix products  53.6 us (10%)
  other arithmetic  19.1 us (3%)
  between operations  18.1 us (3%)
  starting transfers between devices  12.3 us (2%)
    all_gather x2, waiting for transfers between devices, radial_solve(): piece = lax.all_gather(pencils, 'rad', axis=3, tiled=True)  125 us
    all_to_all x2, blocking collectives, body(): lax.all_to_all(spectral, 'ax', split_axis=0, concat_axis=3, tiled=True)  86 us
    all_to_all x1, blocking collectives, body(): lax.all_to_all(solved, 'ax', split_axis=2, concat_axis=0, tiled=True)  57.7 us
    all_to_all x1, waiting for transfers between devices, body(): lax.all_to_all(solved, 'ax', split_axis=2, concat_axis=0, tiled=True)  49.4 us
    unnamed x22, local copies, waits for them, and re-layouts  28.3 us
    dot_general x2, matrix products, radial_solve(): jnp.einsum('mrs,mkqzs->mkqzr', own_rows, grouped, precision=highest)  25.2 us
    all_gather x2, local copies, waits for them, and re-layouts, radial_solve(): piece = lax.all_gather(pencils, 'rad', axis=3, tiled=True)  23 us
    ppermute x2, waiting for transfers between devices, padded_2(): before = lax.ppermute(last, axis, up)  20.2 us
  transfers between devices with their start and end apart: 8, of which 7 were waited for; matrix products, arithmetic and copies ran while one was open for 2% of the time, Pallas kernels for 0%

commit v1 on v0

--- a/solution.py
+++ b/solution.py
@@ -1,12 +1,18 @@
+import functools
 import math
 
 import jax
 import jax.numpy as jnp
+import ml_dtypes
+import numpy as np
 from jax import lax
+from jax.experimental import pallas as pl
+from jax.experimental.pallas import tpu as pltpu
 from jax.sharding import PartitionSpec as P
 
 STEPS = 2
-
+MESH_AXES = ("seg", "rad", "ax")
+VMEM_LIMIT = 48 * 1024 * 1024
 
 highest = lax.Precision.HIGHEST
 
@@ -60,7 +66,7 @@
     return product.reshape(local_columns, members, axial_cells, radial_rows)
 
 
-def body(start_states, radial_inverse, offsets, mode_count):
+def general_body(start_states, radial_inverse, offsets, mode_count):
     groups, components, axial_rows, radial_rows, columns = start_states.shape
     synthesis, analysis = fourier_tables(columns, mode_count[0])
     radius = (
@@ -99,7 +105,436 @@
     return ending - upcoming
 
 
+def halves(high):
+    top = high.astype(jnp.bfloat16)
+    return top, (high - top.astype(jnp.float32)).astype(jnp.bfloat16)
+
+
+def product(left, right, contract):
+    return lax.dot_general(
+        left, right, ((contract[:1], contract[1:]), ((), ())), preferred_element_type=jnp.float32
+    )
+
+
+def stacked_table(table):
+    top = table.astype(ml_dtypes.bfloat16)
+    rest = (table - top.astype(np.float64)).astype(ml_dtypes.bfloat16)
+    return np.concatenate([top, top, rest], axis=1)
+
+
+def column_order(columns, quarter_modes, shares):
+    each = quarter_modes // shares
+    order = []
+    for share in range(shares):
+        for low in range(2):
+            for high in range(2):
+                first = (2 * high + low) * quarter_modes + share * each
+                order.extend(range(2 * first, 2 * (first + each)))
+    assert sorted(order) == list(range(columns))
+    return np.array(order)
+
+
+def tables(columns, order):
+    modes_total = columns // 2
+    rows = np.arange(columns)
+    mode = rows // 2
+    phase = (mode[:, None] * np.arange(columns)[None, :]) % columns * (2.0 * np.pi / columns)
+    even = (rows % 2 == 0)[:, None]
+    root = math.sqrt(modes_total)
+    synthesis = np.where(even, np.cos(phase), np.sin(phase)) / root
+    weights = np.where(mode == 0, 1.0, 2.0)[:, None]
+    analysis = np.where(even, weights * np.cos(phase), 2.0 * np.sin(phase)) * (root / columns)
+    return (
+        stacked_table(np.ascontiguousarray(synthesis.T)),
+        stacked_table(np.ascontiguousarray(synthesis.T[:, order])),
+        stacked_table(analysis[order]),
+        mode[order].astype(np.int32),
+    )
+
+
+def lane_index():
+    return lax.broadcasted_iota(jnp.int32, (1, 128), 1)
+
+
+def physical_to_spectral(physical, profile, analysis):
+    lane = lane_index()
+    z = lane % 16
+    forcing = []
+    for tile in range(3):
+        field = physical[tile]
+        above = jnp.where(z == 15, pltpu.roll(field, 15, 1), pltpu.roll(field, 127, 1))
+        below = jnp.where(z == 0, pltpu.roll(field, 113, 1), pltpu.roll(field, 1, 1))
+        speed = jnp.where(lane < 32, pltpu.roll(field, 64, 1), pltpu.roll(field, 96, 1))
+        speed = jnp.where(lane < 64, speed, field)
+        speed = jnp.where(lane < 96, speed, physical[2])
+        forcing.append(field - 0.4 * (profile[tile : tile + 1] + speed) * (above - below))
+    forcing = jnp.concatenate(forcing, axis=1)
+    top, rest = halves(forcing)
+    return product(analysis, jnp.concatenate([top, rest, top], axis=0), (1, 0))
+
+
+def write_spectral(spectral, out_ref):
+    members, tiles, width, ignored = out_ref.shape
+    for tile in range(tiles):
+        block = spectral[:, tile * 128 : (tile + 1) * 128]
+        out_ref[:, tile] = block.reshape(members, width, 128)
+
+
+def first_phase_a(rows_ref, synthesis_ref, analysis_ref, profile_ref, out_ref):
+    parts = []
+    for tile in range(3):
+        parts.append(rows_ref[tile])
+        parts.append(rows_ref[3, tile * 32 : (tile + 1) * 32])
+    top, rest = halves(jnp.concatenate(parts, axis=0))
+    physical = product(synthesis_ref[...], jnp.concatenate([top, rest, top], axis=1), (1, 1))
+    physical = [physical[:, tile * 128 : (tile + 1) * 128] for tile in range(3)]
+    write_spectral(physical_to_spectral(physical, profile_ref[0], analysis_ref[...]), out_ref)
+
+
+def later_phase_a(wire_ref, synthesis_ref, analysis_ref, profile_ref, out_ref):
+    members, tiles, width, ignored = wire_ref.shape
+    state = jnp.concatenate(
+        [wire_ref[:, tile].reshape(members * width, 128) for tile in range(tiles)], axis=1
+    )
+    top, rest = halves(state)
+    physical = product(synthesis_ref[...], jnp.concatenate([top, rest, top], axis=0), (1, 0))
+    physical = [physical[:, tile * 128 : (tile + 1) * 128] for tile in range(3)]
+    write_spectral(physical_to_spectral(physical, profile_ref[0], analysis_ref[...]), out_ref)
+
+
+def unpack_radii(wire_ref, held_ref, places):
+    members, tiles, width, ignored = wire_ref.shape
+    lane = lane_index()
+    for member in range(members):
+        for group in range(tiles // 3):
+            waves = [wire_ref[member, 3 * group + tile] for tile in range(3)]
+            fourth = jnp.where(lane < 32, pltpu.roll(waves[0], 32, 1), pltpu.roll(waves[1], 64, 1))
+            fourth = jnp.where(lane < 64, fourth, pltpu.roll(waves[2], 96, 1))
+            base = (places[member] + 4 * group) * width
+            for index, block in enumerate(waves + [fourth]):
+                held_ref[base + index * width : base + (index + 1) * width, :] = block
+
+
+def solved_modes(half_ref, own_ref, other_ref, held_ref, transposed, store):
+    each, radii, ignored = own_ref.shape
+    width = 4 * each
+    first_half = half_ref[0] == 0
+    for mode in range(2 * each):
+        index = mode % each
+        here, there = own_ref[index], other_ref[index]
+        if mode < each:
+            matrix = jnp.where(first_half, here, there)
+        else:
+            matrix = jnp.where(first_half, there, here)
+        state = jnp.concatenate(
+            [held_ref[pl.ds(2 * mode + part, radii, stride=width), :] for part in range(2)], axis=1
+        )
+        matrix_top, matrix_rest = halves(matrix)
+        if transposed:
+            top, rest = halves(state.T)
+            solved = product(top, matrix_top, (1, 1))
+            solved += product(rest, matrix_top, (1, 1)) + product(top, matrix_rest, (1, 1))
+        else:
+            top, rest = halves(state)
+            solved = product(matrix_top, top, (1, 0))
+            solved += product(matrix_top, rest, (1, 0)) + product(matrix_rest, top, (1, 0))
+        store(mode, solved)
+
+
+def phase_b(places, half_ref, own_ref, other_ref, wire_ref, out_ref, held_ref, solved_ref):
+    members, tiles, width, ignored = wire_ref.shape
+    radii = own_ref.shape[1]
+    unpack_radii(wire_ref, held_ref, places)
+
+    def store(mode, solved):
+        for part in range(2):
+            solved_ref[pl.ds(2 * mode + part, radii, stride=width), :] = solved[
+                :, part * 128 : (part + 1) * 128
+            ]
+
+    solved_modes(half_ref, own_ref, other_ref, held_ref, False, store)
+    lane = lane_index()
+    for member in range(members):
+        for group in range(tiles // 3):
+            base = (places[member] + 4 * group) * width
+            blocks = [solved_ref[base + i * width : base + (i + 1) * width, :] for i in range(4)]
+            for tile in range(3):
+                fourth = pltpu.roll(blocks[3], 96 - 32 * tile, 1)
+                out_ref[member, 3 * group + tile] = jnp.where(lane < 96, blocks[tile], fourth)
+
+
+def last_phase_b(
+    places, peers, half_ref, offset_ref, own_ref, other_ref, wire_ref, out_ref, held_ref, solved_ref
+):
+    members, tiles, width, ignored = wire_ref.shape
+    radii = own_ref.shape[1]
+    seg_places, rad_places, ax_places = peers
+    planes = 16 // ax_places
+    each = radii // rad_places
+    unpack_radii(wire_ref, held_ref, places)
+
+    def store(mode, solved):
+        for part in range(2):
+            rows = pl.ds(2 * mode + part, 96, stride=width)
+            block = solved[part * 128 : part * 128 + 96]
+            solved_ref[0, rows, :] = block[:, :128]
+            solved_ref[1, rows, 0 : radii - 128] = block[:, 128:]
+
+    solved_modes(half_ref, own_ref, other_ref, held_ref, True, store)
+    lane = lane_index()
+
+    def radial_piece(low, high, rad, at):
+        first = rad * each
+        if first + each <= 128:
+            return pltpu.roll(low, (at - first) % 128, 1)
+        if first >= 128:
+            return pltpu.roll(high, (at - first) % 128, 1)
+        return pltpu.roll(jnp.where(lane >= first, low, high), (at - first) % 128, 1)
+
+    for seg in range(seg_places):
+        for ax in range(ax_places):
+            blocks = {}
+            for component in range(3):
+                for plane in range(planes):
+                    source = lax.rem(ax * planes + plane - offset_ref[seg] + 16, 16)
+                    row = ((component * seg_places + seg) * 16 + source) * width
+                    row = pl.multiple_of(row, 8)
+                    blocks[component, plane] = (
+                        solved_ref[0, pl.ds(row, width), :],
+                        solved_ref[1, pl.ds(row, width), :],
+                    )
+            for rad in range(rad_places):
+                pairs = []
+                for component in range(3):
+                    for pair in range(planes // 2):
+                        left = radial_piece(*blocks[component, 2 * pair], rad, 0)
+                        right = radial_piece(*blocks[component, 2 * pair + 1], rad, each)
+                        pairs.append(jnp.where(lane < each, left, right))
+                split = [
+                    block[8 * part : 8 * part + 8] for part in range(width // 8) for block in pairs
+                ]
+                target = (seg * rad_places + rad) * ax_places + ax
+                for group in range(len(split) // 4):
+                    for tile in range(3):
+                        fourth = pltpu.roll(split[4 * group + 3], 96 - 32 * tile, 1)
+                        out_ref[target, 3 * group + tile] = jnp.where(
+                            lane < 96, split[4 * group + tile], fourth
+                        )
+                whole = len(split) // 4
+                for index in range(4 * whole, len(split)):
+                    out_ref[target, 3 * whole + index - 4 * whole] = split[index]
+
+
+def residual_end(peers, wire_ref, start_ref, following_ref, out_ref, held_ref):
+    seg_places, rad_places, ax_places = peers
+    groups, components, planes, each, columns = out_ref.shape
+    lane = lane_index()
+    shares = seg_places * rad_places
+    width = columns // (2 * shares)
+    chunk = width // 2
+    count = (width // 8) * components * (planes // 2)
+    for half in range(2):
+        for share in range(shares):
+            for low in range(2):
+                source = share * ax_places + 2 * half + low
+                split = []
+                for group in range(count // 4):
+                    waves = [wire_ref[source, 3 * group + tile] for tile in range(3)]
+                    fourth = jnp.where(
+                        lane < 32, pltpu.roll(waves[0], 32, 1), pltpu.roll(waves[1], 64, 1)
+                    )
+                    split += waves + [jnp.where(lane < 64, fourth, pltpu.roll(waves[2], 96, 1))]
+                for index in range(count % 4):
+                    split.append(wire_ref[source, 3 * (count // 4) + index])
+                per_part = components * (planes // 2)
+                for slot in range(per_part):
+                    rows = jnp.concatenate(
+                        [split[part * per_part + slot] for part in range(width // 8)], axis=0
+                    )
+                    for high in range(2):
+                        at = (2 * high + low) * (columns // 4) + share * chunk
+                        held_ref[slot, at : at + chunk, :] = rows[high * chunk : (high + 1) * chunk]
+        for component in range(components):
+            for pair in range(planes // 2):
+                ending = held_ref[component * (planes // 2) + pair].T
+                for side in range(2):
+                    plane = 2 * pair + side
+                    if half + 1 < groups:
+                        upcoming = start_ref[half + 1, component, plane]
+                    else:
+                        upcoming = following_ref[component, plane]
+                    out_ref[half, component, plane] = (
+                        ending[side * each : (side + 1) * each] - upcoming
+                    )
+
+
+def whole_blocks(count):
+    return [pl.BlockSpec(memory_space=pltpu.VMEM)] * count
+
+
+def fits(shape, peers):
+    groups, components, axial_rows, radial_rows, columns = shape
+    seg_places, rad_places, ax_places = peers
+    members = seg_places * rad_places * 2
+    return (
+        (groups, components, seg_places, ax_places) == (2, 3, 2, 4)
+        and axial_rows * ax_places == 16
+        and radial_rows == 48
+        and rad_places * radial_rows == 192
+        and columns == 384
+        and members == 16
+    )
+
+
+def half_body(peers, start_states, radial_inverse, offsets, mode_count):
+    groups, components, axial_rows, radial_rows, columns = start_states.shape
+    seg_places, rad_places, ax_places = peers
+    axial = axial_rows * ax_places
+    radii = radial_rows * rad_places
+    shares = seg_places * rad_places
+    members = 2 * shares
+    own_radii = radii // members
+    own_modes = radial_inverse.shape[0] // shares
+    width = columns // members
+    tiles = own_radii * 3 // 4
+    order = column_order(columns, radial_inverse.shape[0], shares)
+    synthesis_natural, synthesis, analysis, mode_of_row = tables(columns, order)
+
+    seg, rad, ax = (lax.axis_index(name) for name in MESH_AXES)
+    half, low = ax // 2, ax % 2
+
+    def device(s, r, a):
+        return (s * rad_places + r) * ax_places + a
+
+    half_groups = [
+        [
+            device(s, r, 2 * h + l)
+            for s in range(seg_places)
+            for r in range(rad_places)
+            for l in range(2)
+        ]
+        for h in range(2)
+    ]
+    mirror = [(a, (a + 2) % 4) for a in range(4)]
+    places = [
+        r * radial_rows + (s * 2 + l) * own_radii
+        for s in range(seg_places)
+        for r in range(rad_places)
+        for l in range(2)
+    ]
+
+    split = start_states.reshape(
+        groups, components, axial_rows, seg_places, 2, own_radii, columns
+    )
+    split = jnp.transpose(split, (3, 0, 4, 5, 1, 2, 6))
+    split = split.reshape(seg_places * ax_places, own_radii * components * axial_rows, columns)
+    arrived = lax.all_to_all(split, ("seg", "ax"), 0, 0, tiled=True)
+    arrived = arrived.reshape(
+        seg_places, ax_places, own_radii, components, axial_rows, columns
+    )
+    rows = jnp.transpose(arrived, (2, 3, 0, 1, 4, 5))
+    rows = rows.reshape(own_radii, components * seg_places * axial, columns)
+
+    share = seg * rad_places + rad
+    own_inverse = lax.dynamic_slice_in_dim(radial_inverse, share * own_modes, own_modes, 0)
+    other_inverse = lax.ppermute(own_inverse, "ax", mirror)
+    following = passed_along(start_states[0], "seg", -1)
+    swapped = passed_along(offsets, "seg", 1)
+    low_offsets = jnp.where(seg == 0, offsets, swapped)
+    high_offsets = jnp.where(seg == 0, swapped, offsets)
+    half_offsets = jnp.stack([low_offsets[half], high_offsets[half]])
+    half_index = half.reshape(1).astype(jnp.int32)
+
+    kept = (jnp.asarray(mode_of_row) < mode_count[0])[:, None]
+    analysis = jnp.where(kept, jnp.asarray(analysis), jnp.zeros((), jnp.bfloat16))
+    synthesis_natural = jnp.asarray(synthesis_natural)
+    synthesis = jnp.asarray(synthesis)
+    first = rad * radial_rows + (seg * 2 + low) * own_radii
+    tile_index = np.arange(tiles)[:, None]
+    lane = np.arange(128)[None, :]
+    local = 4 * (tile_index // 3) + np.where(lane < 96, tile_index % 3, 3)
+    radius = ((first + jnp.asarray(local)).astype(jnp.float32) + 0.5) / radii
+    profile = (1.0 - radius * radius).reshape(tiles // 3, 3, 128)
+
+    params = pltpu.CompilerParams(vmem_limit_bytes=VMEM_LIMIT)
+    wire = jax.ShapeDtypeStruct((members, tiles, width, 128), jnp.float32)
+    wire_spec = pl.BlockSpec((members, 3, width, 128), lambda g: (0, g, 0, 0))
+    table_spec = pl.BlockSpec((columns, 3 * columns), lambda g: (0, 0))
+    profile_spec = pl.BlockSpec((1, 3, 128), lambda g: (g, 0, 0))
+    held = pltpu.VMEM((radii * width, 128), jnp.float32)
+
+    def exchanged(value):
+        return lax.all_to_all(
+            value, MESH_AXES, 0, 0, axis_index_groups=half_groups, tiled=True
+        )
+
+    with jax.named_scope("phase_a_first"):
+        spectral = pl.pallas_call(
+            first_phase_a,
+            grid=(tiles // 3,),
+            in_specs=[
+                pl.BlockSpec((4,) + rows.shape[1:], lambda g: (g, 0, 0)),
+                table_spec,
+                table_spec,
+                profile_spec,
+            ],
+            out_specs=wire_spec,
+            out_shape=wire,
+            compiler_params=params,
+        )(rows, synthesis_natural, analysis, profile)
+    lines = exchanged(spectral)
+    with jax.named_scope("phase_b_first"):
+        solved = pl.pallas_call(
+            functools.partial(phase_b, places),
+            in_specs=[pl.BlockSpec(memory_space=pltpu.SMEM)] + whole_blocks(3),
+            out_specs=pl.BlockSpec(memory_space=pltpu.VMEM),
+            out_shape=wire,
+            scratch_shapes=[held, held],
+            compiler_params=params,
+        )(half_index, own_inverse, other_inverse, lines)
+    state = exchanged(solved)
+    with jax.named_scope("phase_a_later"):
+        spectral = pl.pallas_call(
+            later_phase_a,
+            grid=(tiles // 3,),
+            in_specs=[wire_spec, table_spec, table_spec, profile_spec],
+            out_specs=wire_spec,
+            out_shape=wire,
+            compiler_params=params,
+        )(state, synthesis, analysis, profile)
+    lines = exchanged(spectral)
+    count = (width // 8) * components * (axial_rows // 2)
+    end_tiles = (count // 4) * 3 + count % 4
+    everyone = seg_places * rad_places * ax_places
+    with jax.named_scope("phase_b_last"):
+        ending = pl.pallas_call(
+            functools.partial(last_phase_b, places, peers),
+            in_specs=[pl.BlockSpec(memory_space=pltpu.SMEM)] * 2 + whole_blocks(3),
+            out_specs=pl.BlockSpec(memory_space=pltpu.VMEM),
+            out_shape=jax.ShapeDtypeStruct((everyone, end_tiles, 8, 128), jnp.float32),
+            scratch_shapes=[held, pltpu.VMEM((2, 96 * width, 128), jnp.float32)],
+            compiler_params=params,
+        )(half_index, half_offsets, own_inverse, other_inverse, lines)
+    ending = lax.all_to_all(ending, MESH_AXES, 0, 0, tiled=True)
+    with jax.named_scope("residual_end"):
+        return pl.pallas_call(
+            functools.partial(residual_end, peers),
+            in_specs=whole_blocks(3),
+            out_specs=pl.BlockSpec(memory_space=pltpu.VMEM),
+            out_shape=jax.ShapeDtypeStruct(start_states.shape, jnp.float32),
+            scratch_shapes=[pltpu.VMEM((components * (axial_rows // 2), columns, 128), jnp.float32)],
+            compiler_params=params,
+        )(ending, start_states, following)
+
+
 def solution(mesh):
+    peers = tuple(mesh.shape[name] for name in MESH_AXES)
+
+    def body(start_states, radial_inverse, offsets, mode_count):
+        if fits(start_states.shape, peers):
+            return half_body(peers, start_states, radial_inverse, offsets, mode_count)
+        return general_body(start_states, radial_inverse, offsets, mode_count)
+
     placed = (P("seg", None, "ax", "rad", None), P("ax", None, None), P("seg"), P())
     return jax.shard_map(
         body,

time: 558 us -> 258 us (0.46); the launches traced: 551 us -> 257 us
  blocking collectives: 144 us -> 27.5 us
  local copies, waits for them, and re-layouts: 93 us -> 22.3 us
  waiting for transfers between devices: 211 us -> 155 us
  matrix products: 53.6 us -> 0 us
  Pallas kernels: 0 us -> 26.4 us
  other arithmetic: 19.1 us -> 1.57 us
  between operations: 18.1 us -> 0.85 us
  starting transfers between devices: 12.3 us -> 23.7 us
    all_gather x2 -> x0, waiting for transfers between devices: 125 us -> none  [radial_solve(): piece = lax.all_gather(pencils, 'rad', axis=3, tiled=True)]
    all_to_all x3 -> x1, blocking collectives: 144 us -> 27.5 us  [exchanged(): lax.all_to_all(value, MESH_AXES, 0, 0, axis_index_groups=half_groups, til...]
    ppermute x1 -> x2, waiting for transfers between devices: 0.01 us -> 57.9 us  [passed_along(): return lax.ppermute(value, axis, pairs)]
    dot_general x6 -> x0, matrix products: 53.6 us -> none  [the longest x2 25.2 us: radial_solve(): jnp.einsum('mrs,mkqzs->mkqzr', own_rows, grouped, precision=highest)]
    pallas_call x0 -> x5, Pallas kernels: none -> 26.4 us  [the longest x1 6.44 us: half_body(): pl.pallas_call(later_phase_a, grid=(tiles // 3,), in_specs=[wire_spec, ta...]
    all_gather x2 -> x0, local copies, waits for them, and re-layouts: 23 us -> none  [radial_solve(): piece = lax.all_gather(pencils, 'rad', axis=3, tiled=True)]
    unnamed x22 -> x27, local copies, waits for them, and re-layouts: 28.3 us -> 8.57 us
    ppermute x4 -> x1, waiting for transfers between devices: 36.5 us -> 53.5 us  [half_body(): other_inverse = lax.ppermute(own_inverse, 'ax', mirror)]
  transfers between devices with their start and end apart: 8 -> 7, of which waited for: 7 -> 5; matrix products, arithmetic and copies ran while one was open for 2% -> 2% of each run, Pallas kernels for 0% -> 0%
where the time goes in v1:
time: 258 us; the launch traced here: 257 us
  waiting for transfers between devices  155 us (60%)
  blocking collectives  27.5 us (11%)
  Pallas kernels  26.4 us (10%)
  starting transfers between devices  23.7 us (9%)
  local copies, waits for them, and re-layouts  22.3 us (9%)
    ppermute x2, waiting for transfers between devices, passed_along(): return lax.ppermute(value, axis, pairs)  57.9 us
    ppermute x1, waiting for transfers between devices, half_body(): other_inverse = lax.ppermute(own_inverse, 'ax', mirror)  53.5 us
    all_to_all x1, waiting for transfers between devices, half_body(): arrived = lax.all_to_all(split, ('seg', 'ax'), 0, 0, tiled=True)  40.4 us
    all_to_all x1, blocking collectives, exchanged(): lax.all_to_all(value, MESH_AXES, 0, 0, axis_index_groups=half_groups, til...  27.5 us
    all_to_all x2, starting transfers between devices, exchanged(): lax.all_to_all(value, MESH_AXES, 0, 0, axis_index_groups=half_groups, til...  10.1 us
    unnamed x27, local copies, waits for them, and re-layouts  8.57 us
    all_to_all x1, starting transfers between devices, half_body(): arrived = lax.all_to_all(split, ('seg', 'ax'), 0, 0, tiled=True)  6.49 us
    pallas_call x1, Pallas kernels, half_body(): pl.pallas_call(later_phase_a, grid=(tiles // 3,), in_specs=[wire_spec, ta...  6.44 us
  transfers between devices with their start and end apart: 7, of which 5 were waited for; matrix products, arithmetic and copies ran while one was open for 2% of the time, Pallas kernels for 0%

profile of v1, /device:TPU:1, one launch (start us, length us, event | category | flops | bytes accessed | tf_op | source)
XLA Modules:
  0.0 257.4 jit_solution(7178315292169624134)
XLA Ops:
  0.0 2.2 copy.10
  2.2 0.3 copy.11
  2.5 1.8 reshape.21
  4.3 6.5 %all-to-all-start = ((f32[8,144,384]{2,1,0:T(8,128)}), f32[8,144,384]{2,1,0:T(8,128)}, u32[]{:S(2)}, u32[]{:S(2)}) async-start(f32[8,144,384]{2,1,0:T(8,128)} %reshape.21), calls=%async_computation | async-start | bytes 3538944 | tf_op jit(solution)/shard_map/all_to_all | solution.py:431
  10.8 0.0 copy-done.10
  11.5 0.0 copy-done.11
  11.5 0.0 copy-done.9
  11.5 0.2 broadcast_select_fusion.analysis_ref
  11.7 40.4 %all-to-all-done = f32[8,144,384]{2,1,0:T(8,128)} async-done(((f32[8,144,384]{2,1,0:T(8,128)}), f32[8,144,384]{2,1,0:T(8,128)}, u32[]{:S(2)}, u32[]{:S(2)}) %all-to-all-start) | async-done | bytes 1769504 | tf_op jit(solution)/shard_map/all_to_all | solution.py:431
  52.1 2.8 %reshape.22 = f32[2,4,12,3,4,384]{5,4,3,2,1,0:T(4,128)} reshape(f32[8,144,384]{2,1,0:T(8,128)} %all-to-all-done) | data formatting | bytes 3538944 | tf_op jit(solution)/shard_map/reshape | solution.py:432
  54.8 3.2 %copy.12 = f32[12,3,2,4,4,384]{5,4,3,2,1,0:T(4,128)} copy(f32[12,3,2,4,4,384]{5,4,1,0,3,2:T(4,128)} %bitcast.9) | data formatting | bytes 3538944 | tf_op jit(solution)/shard_map/transpose | solution.py:435
  58.0 2.9 %reshape.23.rows_ref = f32[12,96,384]{2,1,0:T(8,128)} reshape(f32[12,3,2,4,4,384]{5,4,3,2,1,0:T(4,128)} %copy.12) | data formatting | bytes 3538944 | tf_op jit(solution)/shard_map/reshape | solution.py:436
  60.9 0.0 copy-done.8
  60.9 1.5 copy-done.4
  62.4 6.3 %phase_a_first.1 = f32[16,9,24,128]{3,2,1,0:T(8,128)S(1)} custom-call(f32[12,96,384]{2,1,0:T(8,128)S(1)} %copy-done.4, bf16[384,1152]{1,0:T(8,128)(2,1)S(1)} %copy-done.8, bf16[384,1152]{1,0:T(8,128)(2,1)S(1)} %broadcast_select_fusion.analysis_ref, f32[3,3,128]{2,1,0:T(4,128)S(1)} %reshape.24.profile_ref), custom_call_target="tpu_custom_call" | custom-call | tf_op jit(solution)/shard_map/phase_a_first/pallas_call | solution.py:472
  68.7 0.0 copy-start.2
  68.8 1.2 copy-done.2
  69.9 6.0 %all-to-all-start.1 = ((f32[16,9,24,128]{3,2,1,0:T(8,128)}), f32[16,9,24,128]{3,2,1,0:T(8,128)}, u32[]{:S(2)}, u32[]{:S(2)}) async-start(f32[16,9,24,128]{3,2,1,0:T(8,128)} %copy-done.2), calls=%async_computation.1 | async-start | bytes 3538944 | tf_op jit(solution)/shard_map/all_to_all | solution.py:467
  76.0 1.4 constant_dynamic-slice_fusion.own_ref
  77.4 0.1 collective-permute-start.1
  77.5 53.5 %collective-permute-done.1.other_ref = f32[6,192,192]{2,1,0:T(8,128)S(1)} collective-permute-done((f32[6,192,192]{2,1,0:T(8,128)S(1)}, f32[6,192,192]{2,1,0:T(8,128)S(1)}, u32[]{:S(2)}, u32[]{:S(2)}) %collective-permute-start.1) | collective-permute-done | bytes 884768 | tf_op jit(solution)/shard_map/ppermute | solution.py:440
  130.9 0.0 all-to-all-done.1.wire_ref
  131.0 4.0 %phase_b_first.1 = f32[16,9,24,128]{3,2,1,0:T(8,128)S(1)} custom-call(s32[1]{0:T(128)} %bitcast.half_ref, f32[6,192,192]{2,1,0:T(8,128)S(1)} %constant_dynamic-slice_fusion.own_ref, f32[6,192,192]{2,1,0:T(8,128)S(1)} %collective-permute-done.1.other_ref, f32[16,9,24,128]{3,2,1,0:T(8,128)} %all-to-all-done.1.wire_ref), custom_call_target="tpu_custom_call" | custom-call | tf_op jit(solution)/shard_map/phase_b_first/pallas_call | solution.py:487
  135.0 0.0 copy-done.5
  135.0 0.0 copy-start.7
  135.0 27.5 %all_to_all.25.wire_ref = f32[16,9,24,128]{3,2,1,0:T(8,128)S(1)} all-to-all(f32[16,9,24,128]{3,2,1,0:T(8,128)S(1)} %phase_b_first.1), channel_id=1, replica_groups={{0,1,4,5,8,9,12,13,16,17,20,21,24,25,28,29},{2,3,6,7,10,11,14,15,18,19,..., dimensions={0} | all-to-all | bytes 3538944 | tf_op jit(solution)/shard_map/all_to_all | solution.py:467
  162.6 0.0 copy-done.7
  162.6 6.4 %phase_a_later.1 = f32[16,9,24,128]{3,2,1,0:T(8,128)S(1)} custom-call(f32[16,9,24,128]{3,2,1,0:T(8,128)S(1)} %all_to_all.25.wire_ref, bf16[384,1152]{1,0:T(8,128)(2,1)S(1)} %copy-done.7, bf16[384,1152]{1,0:T(8,128)(2,1)S(1)} %broadcast_select_fusion.analysis_ref, f32[3,3,128]{2,1,0:T(4,128)S(1)} %reshape.24.profile_ref), custom_call_target="tpu_custom_call" | custom-call | tf_op jit(solution)/shard_map/phase_a_later/pallas_call | solution.py:497
  169.0 0.0 copy-start.3
  169.0 1.2 copy-done.3
  170.2 4.1 %all-to-all-start.3 = ((f32[16,9,24,128]{3,2,1,0:T(8,128)}), f32[16,9,24,128]{3,2,1,0:T(8,128)S(1)}, u32[]{:S(2)}, u32[]{:S(2)}) async-start(f32[16,9,24,128]{3,2,1,0:T(8,128)} %copy-done.3), calls=%async_computation.3 | async-start | bytes 3538944 | tf_op jit(solution)/shard_map/all_to_all | solution.py:467
  174.3 0.0 copy-done.12
  174.3 1.5 collective-permute-start
  175.8 19.8 %collective-permute-done = s32[2]{0:T(128)S(1)} collective-permute-done((s32[2]{0:T(128)S(1)}, s32[2]{0:T(128)S(1)}, u32[]{:S(2)}, u32[]{:S(2)}) %collective-permute-start) | collective-permute-done | bytes 40 | tf_op jit(solution)/shard_map/ppermute | solution.py:23
  195.7 0.7 dynamic_slice.9
  196.4 0.6 dynamic_slice.10
  196.9 1.4 pad_add_fusion.offset_ref
  198.3 0.0 all-to-all-done.3.wire_ref
  198.3 1.3 copy-done.6
  199.6 5.7 %phase_b_last.1 = f32[32,14,8,128]{3,2,1,0:T(8,128)S(1)} custom-call(s32[1]{0:T(128)} %bitcast.half_ref, s32[2]{0:T(128)S(1)} %pad_add_fusion.offset_ref, f32[6,192,192]{2,1,0:T(8,128)S(1)} %constant_dynamic-slice_fusion.own_ref, f32[6,192,192]{2,1,0:T(8,128)S(1)} %copy-done.6, f32[16,9,24,128]{3,2,1,0:T(8,128)S(1)} %all-to-all-done.3.wire_ref), custom_call_target="tpu_custom_call" | custom-call | tf_op jit(solution)/shard_map/phase_b_last/pallas_call | solution.py:510
  205.3 0.0 copy-start.1
  205.3 1.2 copy-done.1
  206.6 4.1 %all-to-all-start.4 = ((f32[32,14,8,128]{3,2,1,0:T(8,128)}), f32[32,14,8,128]{3,2,1,0:T(8,128)}, u32[]{:S(2)}, u32[]{:S(2)}) async-start(f32[32,14,8,128]{3,2,1,0:T(8,128)} %copy-done.1), calls=%async_computation.4 | async-start | bytes 3670016 | tf_op jit(solution)/shard_map/all_to_all | solution.py:518
  210.7 0.1 slice_bitcast_fusion
  210.7 1.5 collective-permute-start.2
  212.2 38.0 %collective-permute-done.2.following_ref = f32[3,4,48,384]{3,2,1,0:T(8,128)S(1)} collective-permute-done((f32[3,4,48,384]{3,2,1,0:T(8,128)S(1)}, f32[3,4,48,384]{3,2,1,0:T(8,128)S(1)}, u32[]{:S(2)}, u32[]{:S(2)}) %collective-permute-start.2) | collective-permute-done | bytes 884768 | tf_op jit(solution)/shard_map/ppermute | solution.py:23
  250.2 3.3 %all-to-all-done.4.wire_ref = f32[32,14,8,128]{3,2,1,0:T(8,128)} async-done(((f32[32,14,8,128]{3,2,1,0:T(8,128)}), f32[32,14,8,128]{3,2,1,0:T(8,128)}, u32[]{:S(2)}, u32[]{:S(2)}) %all-to-all-start.4) | async-done | bytes 1835040 | tf_op jit(solution)/shard_map/all_to_all | solution.py:518
  253.6 3.8 %residual_end.1 = f32[2,3,4,48,384]{4,3,2,1,0:T(8,128)} custom-call(f32[32,14,8,128]{3,2,1,0:T(8,128)} %all-to-all-done.4.wire_ref, f32[2,3,4,48,384]{4,3,2,1,0:T(8,128)S(1)} %copy-done, f32[3,4,48,384]{3,2,1,0:T(8,128)S(1)} %collective-permute-done.2.following_ref), custom_call_target="tpu_custom_call" | custom-call | tf_op jit(solution)/shard_map/residual_end/pallas_call | solution.py:520
  (14 shorter events, 0.0 us)
Async XLA Ops:
  4.3 6.5 %copy-start.10 = (s32[9,128]{1,0:T(8,128)S(1)}, s32[9,128]{1,0:T(8,128)}, u32[]{:S(2)}) copy-start(s32[9,128]{1,0:T(8,128)} %constant.69.clone) | copy-start | bytes 13828
  4.3 7.2 %copy-start.11 = (s32[384]{0:T(512)S(1)}, s32[384]{0:T(512)}, u32[]{:S(2)}) copy-start(s32[384]{0:T(512)} %constant.65.clone) | copy-start | bytes 4612
  4.3 7.2 %copy-start.9 = (bf16[384,1152]{1,0:T(8,128)(2,1)S(1)}, bf16[384,1152]{1,0:T(8,128)(2,1)}, u32[]{:S(2)}) copy-start(bf16[384,1152]{1,0:T(8,128)(2,1)} %constant.66.clone) | copy-start | bytes 2654212
  4.3 47.8 %all-to-all-start = ((f32[8,144,384]{2,1,0:T(8,128)}), f32[8,144,384]{2,1,0:T(8,128)}, u32[]{:S(2)}, u32[]{:S(2)}) async-start(f32[8,144,384]{2,1,0:T(8,128)} %reshape.21), calls=%async_computation | async-start | bytes 3538944 | tf_op jit(solution)/shard_map/all_to_all | solution.py:431
  58.0 2.9 %copy-start.8 = (bf16[384,1152]{1,0:T(8,128)(2,1)S(1)}, bf16[384,1152]{1,0:T(8,128)(2,1)}, u32[]{:S(2)}) copy-start(bf16[384,1152]{1,0:T(8,128)(2,1)} %constant.67.clone.synthesis_ref) | copy-start | bytes 2654212
  60.9 1.5 copy-start.4
  68.7 1.2 copy-start.2
  69.9 61.0 %all-to-all-start.1 = ((f32[16,9,24,128]{3,2,1,0:T(8,128)}), f32[16,9,24,128]{3,2,1,0:T(8,128)}, u32[]{:S(2)}, u32[]{:S(2)}) async-start(f32[16,9,24,128]{3,2,1,0:T(8,128)} %copy-done.2), calls=%async_computation.1 | async-start | bytes 3538944 | tf_op jit(solution)/shard_map/all_to_all | solution.py:467
  77.4 53.6 %collective-permute-start.1 = (f32[6,192,192]{2,1,0:T(8,128)S(1)}, f32[6,192,192]{2,1,0:T(8,128)S(1)}, u32[]{:S(2)}, u32[]{:S(2)}) collective-permute-start(f32[6,192,192]{2,1,0:T(8,128)S(1)} %constant_dynamic-slice_fusion.own_ref), channel_id=1, source_target_pairs={{0,2},{1,3},{2,0},{3,1},{4,6},{5,7},{6,4},{7,5},{8,10},{9,11},{10,... | collective-permute-start | bytes 2654216 | tf_op jit(solution)/shard_map/ppermute | solution.py:440
  130.9 4.1 %copy-start.5 = (f32[6,192,192]{2,1,0:T(8,128)}, f32[6,192,192]{2,1,0:T(8,128)S(1)}, u32[]{:S(2)}) copy-start(f32[6,192,192]{2,1,0:T(8,128)S(1)} %collective-permute-done.1.other_ref) | copy-start | bytes 2654212
  135.0 27.5 %copy-start.7 = (bf16[384,1152]{1,0:T(8,128)(2,1)S(1)}, bf16[384,1152]{1,0:T(8,128)(2,1)}, u32[]{:S(2)}) copy-start(bf16[384,1152]{1,0:T(8,128)(2,1)} %constant.68.clone.synthesis_ref) | copy-start | bytes 2654212
  169.0 1.2 copy-start.3
  170.2 4.1 %copy-start.12 = (s32[2]{0:T(128)S(1)}, s32[2]{0:T(128)}, u32[]{:S(2)}) copy-start(s32[2]{0:T(128)} %param.11) | copy-start | bytes 28
  170.2 28.1 %all-to-all-start.3 = ((f32[16,9,24,128]{3,2,1,0:T(8,128)}), f32[16,9,24,128]{3,2,1,0:T(8,128)S(1)}, u32[]{:S(2)}, u32[]{:S(2)}) async-start(f32[16,9,24,128]{3,2,1,0:T(8,128)} %copy-done.3), calls=%async_computation.3 | async-start | bytes 3538944 | tf_op jit(solution)/shard_map/all_to_all | solution.py:467
  174.3 21.3 %collective-permute-start = (s32[2]{0:T(128)S(1)}, s32[2]{0:T(128)S(1)}, u32[]{:S(2)}, u32[]{:S(2)}) collective-permute-start(s32[2]{0:T(128)S(1)} %copy-done.12), channel_id=1, source_target_pairs={{0,16},{16,0},{1,17},{17,1},{2,18},{18,2},{3,19},{19,3},{4,20},{20... | collective-permute-start | bytes 32 | tf_op jit(solution)/shard_map/ppermute | solution.py:23
  198.3 1.3 copy-start.6
  205.3 1.2 copy-start.1
  206.6 4.1 %copy-start = (f32[2,3,4,48,384]{4,3,2,1,0:T(8,128)S(1)}, f32[2,3,4,48,384]{4,3,2,1,0:T(8,128)}, u32[]{:S(2)}) copy-start(f32[2,3,4,48,384]{4,3,2,1,0:T(8,128)} %start_ref.1) | copy-start | bytes 5308420
  206.6 47.0 %all-to-all-start.4 = ((f32[32,14,8,128]{3,2,1,0:T(8,128)}), f32[32,14,8,128]{3,2,1,0:T(8,128)}, u32[]{:S(2)}, u32[]{:S(2)}) async-start(f32[32,14,8,128]{3,2,1,0:T(8,128)} %copy-done.1), calls=%async_computation.4 | async-start | bytes 3670016 | tf_op jit(solution)/shard_map/all_to_all | solution.py:518
  210.7 39.5 %collective-permute-start.2 = (f32[3,4,48,384]{3,2,1,0:T(8,128)S(1)}, f32[3,4,48,384]{3,2,1,0:T(8,128)S(1)}, u32[]{:S(2)}, u32[]{:S(2)}) collective-permute-start(f32[3,4,48,384]{3,2,1,0:T(8,128)S(1)} %slice_bitcast_fusion), channel_id=1, source_target_pairs={{0,16},{16,0},{1,17},{17,1},{2,18},{18,2},{3,19},{19,3},{4,20},{20... | collective-permute-start | bytes 2654216 | tf_op jit(solution)/shard_map/ppermute | solution.py:23

commit v2 on v1

--- a/solution.py
+++ b/solution.py
@@ -13,6 +13,7 @@
 STEPS = 2
 MESH_AXES = ("seg", "rad", "ax")
 VMEM_LIMIT = 48 * 1024 * 1024
+FLOPS = 40_000_000_000
 
 highest = lax.Precision.HIGHEST
 
@@ -180,12 +181,36 @@
         out_ref[:, tile] = block.reshape(members, width, 128)
 
 
+def pack_start(start_ref, out_ref):
+    ignored, components, planes, each, columns = start_ref.shape
+    seg_places, ignored, lows, strips, rows, ignored = out_ref.shape
+    period = components * planes
+    own = rows // period
+    for component in range(components):
+        for plane in range(planes):
+            for seg in range(seg_places):
+                for low in range(lows):
+                    first = (seg * lows + low) * own
+                    block = start_ref[0, component, plane, first : first + own]
+                    at = pl.ds(component * planes + plane, own, stride=period)
+                    for strip in range(strips):
+                        out_ref[seg, 0, low, strip, at, :] = block[
+                            :, strip * 128 : (strip + 1) * 128
+                        ]
+
+
 def first_phase_a(rows_ref, synthesis_ref, analysis_ref, profile_ref, out_ref):
-    parts = []
-    for tile in range(3):
-        parts.append(rows_ref[tile])
-        parts.append(rows_ref[3, tile * 32 : (tile + 1) * 32])
-    top, rest = halves(jnp.concatenate(parts, axis=0))
+    sources, strips = rows_ref.shape[:2]
+    strip_rows = []
+    for strip in range(strips):
+        parts = []
+        for tile in range(3):
+            for radius, components in ((tile, range(3)), (3, (tile,))):
+                for component in components:
+                    first = 12 * radius + 4 * component
+                    parts += [rows_ref[i, strip, first : first + 4] for i in range(sources)]
+        strip_rows.append(jnp.concatenate(parts, axis=0))
+    top, rest = halves(jnp.concatenate(strip_rows, axis=1))
     physical = product(synthesis_ref[...], jnp.concatenate([top, rest, top], axis=1), (1, 1))
     physical = [physical[:, tile * 128 : (tile + 1) * 128] for tile in range(3)]
     write_spectral(physical_to_spectral(physical, profile_ref[0], analysis_ref[...]), out_ref)
@@ -215,21 +240,26 @@
                 held_ref[base + index * width : base + (index + 1) * width, :] = block
 
 
-def solved_modes(half_ref, own_ref, other_ref, held_ref, transposed, store):
-    each, radii, ignored = own_ref.shape
-    width = 4 * each
+def ordered_inverse(half_ref, own_ref, other_ref, top_ref, rest_ref):
+    each = own_ref.shape[0]
     first_half = half_ref[0] == 0
-    for mode in range(2 * each):
-        index = mode % each
+    for index in range(each):
         here, there = own_ref[index], other_ref[index]
-        if mode < each:
-            matrix = jnp.where(first_half, here, there)
-        else:
-            matrix = jnp.where(first_half, there, here)
+        for at, matrix in (
+            (index, jnp.where(first_half, here, there)),
+            (each + index, jnp.where(first_half, there, here)),
+        ):
+            top_ref[at], rest_ref[at] = halves(matrix)
+
+
+def solved_modes(top_ref, rest_ref, held_ref, transposed, store):
+    modes, radii, ignored = top_ref.shape
+    width = 2 * modes
+    for mode in range(modes):
+        matrix_top, matrix_rest = top_ref[mode], rest_ref[mode]
         state = jnp.concatenate(
             [held_ref[pl.ds(2 * mode + part, radii, stride=width), :] for part in range(2)], axis=1
         )
-        matrix_top, matrix_rest = halves(matrix)
         if transposed:
             top, rest = halves(state.T)
             solved = product(top, matrix_top, (1, 1))
@@ -241,9 +271,9 @@
         store(mode, solved)
 
 
-def phase_b(places, half_ref, own_ref, other_ref, wire_ref, out_ref, held_ref, solved_ref):
+def phase_b(places, top_ref, rest_ref, wire_ref, out_ref, held_ref, solved_ref):
     members, tiles, width, ignored = wire_ref.shape
-    radii = own_ref.shape[1]
+    radii = top_ref.shape[1]
     unpack_radii(wire_ref, held_ref, places)
 
     def store(mode, solved):
@@ -252,7 +282,7 @@
                 :, part * 128 : (part + 1) * 128
             ]
 
-    solved_modes(half_ref, own_ref, other_ref, held_ref, False, store)
+    solved_modes(top_ref, rest_ref, held_ref, False, store)
     lane = lane_index()
     for member in range(members):
         for group in range(tiles // 3):
@@ -264,10 +294,10 @@
 
 
 def last_phase_b(
-    places, peers, half_ref, offset_ref, own_ref, other_ref, wire_ref, out_ref, held_ref, solved_ref
+    places, peers, offset_ref, top_ref, rest_ref, wire_ref, out_ref, held_ref, solved_ref
 ):
     members, tiles, width, ignored = wire_ref.shape
-    radii = own_ref.shape[1]
+    radii = top_ref.shape[1]
     seg_places, rad_places, ax_places = peers
     planes = 16 // ax_places
     each = radii // rad_places
@@ -280,7 +310,7 @@
             solved_ref[0, rows, :] = block[:, :128]
             solved_ref[1, rows, 0 : radii - 128] = block[:, 128:]
 
-    solved_modes(half_ref, own_ref, other_ref, held_ref, True, store)
+    solved_modes(top_ref, rest_ref, held_ref, True, store)
     lane = lane_index()
 
     def radial_piece(low, high, rad, at):
@@ -423,27 +453,50 @@
         for l in range(2)
     ]
 
-    split = start_states.reshape(
-        groups, components, axial_rows, seg_places, 2, own_radii, columns
-    )
-    split = jnp.transpose(split, (3, 0, 4, 5, 1, 2, 6))
-    split = split.reshape(seg_places * ax_places, own_radii * components * axial_rows, columns)
-    arrived = lax.all_to_all(split, ("seg", "ax"), 0, 0, tiled=True)
-    arrived = arrived.reshape(
-        seg_places, ax_places, own_radii, components, axial_rows, columns
-    )
-    rows = jnp.transpose(arrived, (2, 3, 0, 1, 4, 5))
-    rows = rows.reshape(own_radii, components * seg_places * axial, columns)
+    params = pltpu.CompilerParams(vmem_limit_bytes=VMEM_LIMIT)
+
+    row_count = own_radii * components * axial_rows
+    strips = columns // 128
+    with jax.named_scope("pack_start"):
+        split = pl.pallas_call(
+            pack_start,
+            grid=(groups,),
+            in_specs=[pl.BlockSpec((1,) + start_states.shape[1:], lambda b: (b, 0, 0, 0, 0))],
+            out_specs=pl.BlockSpec(
+                (seg_places, 1, 2, strips, row_count, 128), lambda b: (0, b, 0, 0, 0, 0)
+            ),
+            out_shape=jax.ShapeDtypeStruct(
+                (seg_places, groups, 2, strips, row_count, 128), jnp.float32
+            ),
+            compiler_params=params,
+        )(start_states)
+    split = split.reshape(seg_places * ax_places, strips, row_count, 128)
+    rows = lax.all_to_all(split, ("seg", "ax"), 0, 0, tiled=True)
 
     share = seg * rad_places + rad
     own_inverse = lax.dynamic_slice_in_dim(radial_inverse, share * own_modes, own_modes, 0)
-    other_inverse = lax.ppermute(own_inverse, "ax", mirror)
     following = passed_along(start_states[0], "seg", -1)
     swapped = passed_along(offsets, "seg", 1)
     low_offsets = jnp.where(seg == 0, offsets, swapped)
     high_offsets = jnp.where(seg == 0, swapped, offsets)
     half_offsets = jnp.stack([low_offsets[half], high_offsets[half]])
     half_index = half.reshape(1).astype(jnp.int32)
+    rows, own_inverse, half_offsets, following = lax.optimization_barrier(
+        (rows, own_inverse, half_offsets, following)
+    )
+    other_inverse = lax.ppermute(own_inverse, "ax", mirror)
+    matrices = jax.ShapeDtypeStruct((2 * own_modes, radii, radii), jnp.bfloat16)
+    with jax.named_scope("ordered_inverse"):
+        inverse = pl.pallas_call(
+            ordered_inverse,
+            in_specs=[pl.BlockSpec(memory_space=pltpu.SMEM)] + whole_blocks(2),
+            out_specs=whole_blocks(2),
+            out_shape=[matrices, matrices],
+            compiler_params=params,
+            cost_estimate=pl.CostEstimate(
+                flops=FLOPS, bytes_accessed=16 * own_modes * radii * radii, transcendentals=0
+            ),
+        )(half_index, own_inverse, other_inverse)
 
     kept = (jnp.asarray(mode_of_row) < mode_count[0])[:, None]
     analysis = jnp.where(kept, jnp.asarray(analysis), jnp.zeros((), jnp.bfloat16))
@@ -456,7 +509,6 @@
     radius = ((first + jnp.asarray(local)).astype(jnp.float32) + 0.5) / radii
     profile = (1.0 - radius * radius).reshape(tiles // 3, 3, 128)
 
-    params = pltpu.CompilerParams(vmem_limit_bytes=VMEM_LIMIT)
     wire = jax.ShapeDtypeStruct((members, tiles, width, 128), jnp.float32)
     wire_spec = pl.BlockSpec((members, 3, width, 128), lambda g: (0, g, 0, 0))
     table_spec = pl.BlockSpec((columns, 3 * columns), lambda g: (0, 0))
@@ -473,7 +525,7 @@
             first_phase_a,
             grid=(tiles // 3,),
             in_specs=[
-                pl.BlockSpec((4,) + rows.shape[1:], lambda g: (g, 0, 0)),
+                pl.BlockSpec((rows.shape[0], strips, 48, 128), lambda g: (0, 0, g, 0)),
                 table_spec,
                 table_spec,
                 profile_spec,
@@ -486,12 +538,12 @@
     with jax.named_scope("phase_b_first"):
         solved = pl.pallas_call(
             functools.partial(phase_b, places),
-            in_specs=[pl.BlockSpec(memory_space=pltpu.SMEM)] + whole_blocks(3),
+            in_specs=whole_blocks(3),
             out_specs=pl.BlockSpec(memory_space=pltpu.VMEM),
             out_shape=wire,
             scratch_shapes=[held, held],
             compiler_params=params,
-        )(half_index, own_inverse, other_inverse, lines)
+        )(*inverse, lines)
     state = exchanged(solved)
     with jax.named_scope("phase_a_later"):
         spectral = pl.pallas_call(
@@ -509,12 +561,12 @@
     with jax.named_scope("phase_b_last"):
         ending = pl.pallas_call(
             functools.partial(last_phase_b, places, peers),
-            in_specs=[pl.BlockSpec(memory_space=pltpu.SMEM)] * 2 + whole_blocks(3),
+            in_specs=[pl.BlockSpec(memory_space=pltpu.SMEM)] + whole_blocks(3),
             out_specs=pl.BlockSpec(memory_space=pltpu.VMEM),
             out_shape=jax.ShapeDtypeStruct((everyone, end_tiles, 8, 128), jnp.float32),
             scratch_shapes=[held, pltpu.VMEM((2, 96 * width, 128), jnp.float32)],
             compiler_params=params,
-        )(half_index, half_offsets, own_inverse, other_inverse, lines)
+        )(half_offsets, *inverse, lines)
     ending = lax.all_to_all(ending, MESH_AXES, 0, 0, tiled=True)
     with jax.named_scope("residual_end"):
         return pl.pallas_call(

time: 258 us -> 239 us (0.926)
  waiting for transfers between devices: 155 us -> 72.3 us
  blocking collectives: 27.5 us -> 99.8 us
  starting transfers between devices: 23.7 us -> 17.8 us
  local copies, waits for them, and re-layouts: 22.3 us -> 16.8 us
    all_to_all x0 -> x1, blocking collectives: none -> 46.5 us  [half_body(): ending = lax.all_to_all(ending, MESH_AXES, 0, 0, tiled=True)]
    all_to_all x2 -> x1, waiting for transfers between devices: 43.7 us -> 3.26 us  [half_body(): rows = lax.all_to_all(split, ('seg', 'ax'), 0, 0, tiled=True)]
    ppermute x2, waiting for transfers between devices: 57.9 us -> 29.8 us  [passed_along(): return lax.ppermute(value, axis, pairs)]
    all_to_all x1 -> x2, blocking collectives: 27.5 us -> 53.2 us  [exchanged(): lax.all_to_all(value, MESH_AXES, 0, 0, axis_index_groups=half_groups, til...]
    ppermute x1, waiting for transfers between devices: 53.5 us -> 32.7 us  [half_body(): other_inverse = lax.ppermute(own_inverse, 'ax', mirror)]
    reshape x3 -> x0, local copies, waits for them, and re-layouts: 7.46 us -> none  [the longest x1 2.88 us: half_body(): rows = rows.reshape(own_radii, components * seg_places * axial, columns)]
    all_to_all x2 -> x1, waiting for transfers between devices: 0.01 us -> 6.58 us  [exchanged(): lax.all_to_all(value, MESH_AXES, 0, 0, axis_index_groups=half_groups, til...]
    all_to_all x2 -> x1, starting transfers between devices: 10.6 us -> 6.49 us  [half_body(): rows = lax.all_to_all(split, ('seg', 'ax'), 0, 0, tiled=True)]
  transfers between devices with their start and end apart: 7 -> 5, of which waited for: 5 -> 4; matrix products, arithmetic and copies ran while one was open for 2% -> 3% of each run, Pallas kernels for 0% -> 3%
where the time goes in v2:
time: 239 us
  blocking collectives  99.8 us (42%)
  waiting for transfers between devices  72.3 us (30%)
  Pallas kernels  27.5 us (12%)
  starting transfers between devices  17.8 us (7%)
  local copies, waits for them, and re-layouts  16.8 us (7%)
  other arithmetic  3.37 us (1%)
    all_to_all x2, blocking collectives, exchanged(): lax.all_to_all(value, MESH_AXES, 0, 0, axis_index_groups=half_groups, til...  53.2 us
    all_to_all x1, blocking collectives, half_body(): ending = lax.all_to_all(ending, MESH_AXES, 0, 0, tiled=True)  46.5 us
    ppermute x1, waiting for transfers between devices, half_body(): other_inverse = lax.ppermute(own_inverse, 'ax', mirror)  32.7 us
    ppermute x2, waiting for transfers between devices, passed_along(): return lax.ppermute(value, axis, pairs)  29.8 us
    unnamed x36, local copies, waits for them, and re-layouts  12.1 us
    all_to_all x1, waiting for transfers between devices, exchanged(): lax.all_to_all(value, MESH_AXES, 0, 0, axis_index_groups=half_groups, til...  6.58 us
    all_to_all x1, starting transfers between devices, half_body(): rows = lax.all_to_all(split, ('seg', 'ax'), 0, 0, tiled=True)  6.49 us
    pallas_call x1, Pallas kernels, half_body(): pl.pallas_call(first_phase_a, grid=(tiles // 3,), in_specs=[pl.BlockSpec(...  6.48 us
  transfers between devices with their start and end apart: 5, of which 4 were waited for; matrix products, arithmetic and copies ran while one was open for 3% of the time, Pallas kernels for 3%

profile of v2, /device:TPU:1, one launch (start us, length us, event | category | flops | bytes accessed | tf_op | source)
XLA Modules:
  0.0 238.5 jit_solution(1184970547444850686)
XLA Ops:
  0.0 1.5 copy-done
  1.5 0.4 pack_start.1
  1.9 0.0 copy-start.4
  1.9 1.2 copy-done.4
  3.1 6.5 %all-to-all-start = ((f32[8,3,144,128]{3,2,1,0:T(8,128)}), f32[8,3,144,128]{3,2,1,0:T(8,128)S(1)}, u32[]{:S(2)}, u32[]{:S(2)}) async-start(f32[8,3,144,128]{3,2,1,0:T(8,128)} %bitcast.6), calls=%async_computation | async-start | bytes 3538944 | tf_op jit(solution)/shard_map/all_to_all | solution.py:474
  9.6 0.0 copy-done.1
  9.6 0.0 copy-start.17
  9.6 0.0 copy-start.15
  9.6 0.0 copy-start.16
  9.6 1.0 slice_bitcast_fusion
  10.6 1.4 collective-permute-start.1
  12.0 0.0 copy-done.17
  12.0 0.0 collective-permute-start
  12.1 2.4 %constant_dynamic-slice_fusion.own_ref = f32[6,192,192]{2,1,0:T(8,128)} fusion(f32[48,192,192]{2,1,0:T(8,128)} %param.10, s32[]{:T(128)S(6)} %select_n.34), kind=kLoop, calls=%fused_computation.7 | loop fusion | bytes 1769476 | tf_op jit(solution)/shard_map/dynamic_slice | solution.py:477
  14.5 29.8 %collective-permute-done = s32[2]{0:T(128)} collective-permute-done((s32[2]{0:T(128)S(1)}, s32[2]{0:T(128)}, u32[]{:S(2)}, u32[]{:S(2)}) %collective-permute-start) | collective-permute-done | bytes 40 | tf_op jit(solution)/shard_map/ppermute | solution.py:24
  44.3 0.7 broadcast_select_fusion.2
  45.0 0.6 dynamic_slice.10
  45.6 0.6 dynamic_slice.11
  46.2 1.4 pad_add_fusion.offset_ref
  47.6 0.0 collective-permute-done.1.following_ref
  47.6 3.3 %all-to-all-done.rows_ref = f32[8,3,144,128]{3,2,1,0:T(8,128)S(1)} async-done(((f32[8,3,144,128]{3,2,1,0:T(8,128)}), f32[8,3,144,128]{3,2,1,0:T(8,128)S(1)}, u32[]{:S(2)}, u32[]{:S(2)}) %all-to-all-start) | async-done | bytes 1769504 | tf_op jit(solution)/shard_map/all_to_all | solution.py:474
  50.8 1.2 copy-done.2
  52.1 3.6 %collective-permute-start.2 = (f32[6,192,192]{2,1,0:T(8,128)}, f32[6,192,192]{2,1,0:T(8,128)}, u32[]{:S(2)}, u32[]{:S(2)}) collective-permute-start(f32[6,192,192]{2,1,0:T(8,128)} %constant_dynamic-slice_fusion.own_ref), channel_id=1, source_target_pairs={{0,2},{1,3},{2,0},{3,1},{4,6},{5,7},{6,4},{7,5},{8,10},{9,11},{10,... | collective-permute-start | bytes 2654216 | tf_op jit(solution)/shard_map/ppermute | solution.py:487
  56.4 1.3 broadcast_select_fusion.analysis_ref
  57.8 0.0 copy-start.14
  57.8 1.2 copy-done.14
  59.0 6.5 %phase_a_first.1 = f32[16,9,24,128]{3,2,1,0:T(8,128)S(1)} custom-call(f32[8,3,144,128]{3,2,1,0:T(8,128)S(1)} %copy-done.3, bf16[384,1152]{1,0:T(8,128)(2,1)S(1)} %copy-done.14, bf16[384,1152]{1,0:T(8,128)(2,1)S(1)} %broadcast_select_fusion.analysis_ref, f32[3,3,128]{2,1,0:T(4,128)S(1)} %reshape.12.profile_ref), custom_call_target="tpu_custom_call" | custom-call | tf_op jit(solution)/shard_map/phase_a_first/pallas_call | solution.py:524
  65.5 0.0 copy-start.5
  65.5 1.2 copy-done.5
  66.7 6.3 %all-to-all-start.1 = ((f32[16,9,24,128]{3,2,1,0:T(8,128)}), f32[16,9,24,128]{3,2,1,0:T(8,128)}, u32[]{:S(2)}, u32[]{:S(2)}) async-start(f32[16,9,24,128]{3,2,1,0:T(8,128)} %copy-done.5), calls=%async_computation.1 | async-start | bytes 3538944 | tf_op jit(solution)/shard_map/all_to_all | solution.py:519
  73.0 32.7 %collective-permute-done.2.other_ref = f32[6,192,192]{2,1,0:T(8,128)} collective-permute-done((f32[6,192,192]{2,1,0:T(8,128)}, f32[6,192,192]{2,1,0:T(8,128)}, u32[]{:S(2)}, u32[]{:S(2)}) %collective-permute-start.2) | collective-permute-done | bytes 884768 | tf_op jit(solution)/shard_map/ppermute | solution.py:487
  105.7 1.3 copy-done.12
  106.9 1.7 ordered_inverse.1
  108.7 1.0 copy-done.6
  109.7 1.0 copy-done.9
  110.7 6.6 %all-to-all-done.1.wire_ref = f32[16,9,24,128]{3,2,1,0:T(8,128)} async-done(((f32[16,9,24,128]{3,2,1,0:T(8,128)}), f32[16,9,24,128]{3,2,1,0:T(8,128)}, u32[]{:S(2)}, u32[]{:S(2)}) %all-to-all-start.1) | async-done | bytes 1769504 | tf_op jit(solution)/shard_map/all_to_all | solution.py:519
  117.3 1.3 copy-done.7
  118.6 1.3 copy-done.10
  119.9 3.3 %phase_b_first.1 = f32[16,9,24,128]{3,2,1,0:T(8,128)S(1)} custom-call(bf16[12,192,192]{2,1,0:T(8,128)(2,1)S(1)} %copy-done.7, bf16[12,192,192]{2,1,0:T(8,128)(2,1)S(1)} %copy-done.10, f32[16,9,24,128]{3,2,1,0:T(8,128)} %all-to-all-done.1.wire_ref), custom_call_target="tpu_custom_call" | custom-call | tf_op jit(solution)/shard_map/phase_b_first/pallas_call | solution.py:539
  123.2 0.0 copy-start.13
  123.2 27.4 %all_to_all.25.wire_ref = f32[16,9,24,128]{3,2,1,0:T(8,128)S(1)} all-to-all(f32[16,9,24,128]{3,2,1,0:T(8,128)S(1)} %phase_b_first.1), channel_id=1, replica_groups={{0,1,4,5,8,9,12,13,16,17,20,21,24,25,28,29},{2,3,6,7,10,11,14,15,18,19,..., dimensions={0} | all-to-all | bytes 3538944 | tf_op jit(solution)/shard_map/all_to_all | solution.py:519
  150.6 0.0 copy-done.13
  150.6 6.4 %phase_a_later.1 = f32[16,9,24,128]{3,2,1,0:T(8,128)S(1)} custom-call(f32[16,9,24,128]{3,2,1,0:T(8,128)S(1)} %all_to_all.25.wire_ref, bf16[384,1152]{1,0:T(8,128)(2,1)S(1)} %copy-done.13, bf16[384,1152]{1,0:T(8,128)(2,1)S(1)} %broadcast_select_fusion.analysis_ref, f32[3,3,128]{2,1,0:T(4,128)S(1)} %reshape.12.profile_ref), custom_call_target="tpu_custom_call" | custom-call | tf_op jit(solution)/shard_map/phase_a_later/pallas_call | solution.py:549
  157.1 25.9 %all_to_all.26.wire_ref = f32[16,9,24,128]{3,2,1,0:T(8,128)S(1)} all-to-all(f32[16,9,24,128]{3,2,1,0:T(8,128)S(1)} %phase_a_later.1), channel_id=1, replica_groups={{0,1,4,5,8,9,12,13,16,17,20,21,24,25,28,29},{2,3,6,7,10,11,14,15,18,19,..., dimensions={0} | all-to-all | bytes 3538944 | tf_op jit(solution)/shard_map/all_to_all | solution.py:519
  182.9 0.0 copy-done.8
  182.9 5.6 %phase_b_last.1 = f32[32,14,8,128]{3,2,1,0:T(8,128)S(1)} custom-call(s32[2]{0:T(128)S(1)} %pad_add_fusion.offset_ref, bf16[12,192,192]{2,1,0:T(8,128)(2,1)S(1)} %copy-done.8, bf16[12,192,192]{2,1,0:T(8,128)(2,1)S(1)} %copy-done.11, f32[16,9,24,128]{3,2,1,0:T(8,128)S(1)} %all_to_all.26.wire_ref), custom_call_target="tpu_custom_call" | custom-call | tf_op jit(solution)/shard_map/phase_b_last/pallas_call | solution.py:562
  188.5 46.5 %all_to_all.27.wire_ref = f32[32,14,8,128]{3,2,1,0:T(8,128)S(1)} all-to-all(f32[32,14,8,128]{3,2,1,0:T(8,128)S(1)} %phase_b_last.1), channel_id=1, replica_groups=mesh['seg'=2,'rad'=4,'ax'=4] {'seg','rad','ax'}, dimensions={0} | all-to-all | bytes 3670016 | tf_op jit(solution)/shard_map/all_to_all | solution.py:570
  235.0 3.5 %residual_end.1 = f32[2,3,4,48,384]{4,3,2,1,0:T(8,128)} custom-call(f32[32,14,8,128]{3,2,1,0:T(8,128)S(1)} %all_to_all.27.wire_ref, f32[2,3,4,48,384]{4,3,2,1,0:T(8,128)S(1)} %copy-done.1, f32[3,4,48,384]{3,2,1,0:T(8,128)} %collective-permute-done.1.following_ref), custom_call_target="tpu_custom_call" | custom-call | tf_op jit(solution)/shard_map/residual_end/pallas_call | solution.py:572
  (18 shorter events, 0.1 us)
Async XLA Ops:
  0.0 1.5 copy-start
  1.9 1.2 copy-start.4
  3.1 6.5 %copy-start.1 = (f32[2,3,4,48,384]{4,3,2,1,0:T(8,128)S(1)}, f32[2,3,4,48,384]{4,3,2,1,0:T(8,128)}, u32[]{:S(2)}) copy-start(f32[2,3,4,48,384]{4,3,2,1,0:T(8,128)} %start_ref.3) | copy-start | bytes 5308420
  3.1 47.8 %all-to-all-start = ((f32[8,3,144,128]{3,2,1,0:T(8,128)}), f32[8,3,144,128]{3,2,1,0:T(8,128)S(1)}, u32[]{:S(2)}, u32[]{:S(2)}) async-start(f32[8,3,144,128]{3,2,1,0:T(8,128)} %bitcast.6), calls=%async_computation | async-start | bytes 3538944 | tf_op jit(solution)/shard_map/all_to_all | solution.py:474
  9.6 2.5 %copy-start.17 = (s32[2]{0:T(128)S(1)}, s32[2]{0:T(128)}, u32[]{:S(2)}) copy-start(s32[2]{0:T(128)} %param.11) | copy-start | bytes 28
  9.6 46.0 %copy-start.15 = (s32[9,128]{1,0:T(8,128)S(1)}, s32[9,128]{1,0:T(8,128)}, u32[]{:S(2)}) copy-start(s32[9,128]{1,0:T(8,128)} %constant.69.clone) | copy-start | bytes 13828
  9.6 46.8 %copy-start.16 = (s32[384]{0:T(512)S(1)}, s32[384]{0:T(512)}, u32[]{:S(2)}) copy-start(s32[384]{0:T(512)} %constant.65.clone) | copy-start | bytes 4612
  10.6 37.0 %collective-permute-start.1 = (f32[3,4,48,384]{3,2,1,0:T(8,128)}, f32[3,4,48,384]{3,2,1,0:T(8,128)}, u32[]{:S(2)}, u32[]{:S(2)}) collective-permute-start(f32[3,4,48,384]{3,2,1,0:T(8,128)} %slice_bitcast_fusion), channel_id=1, source_target_pairs={{0,16},{16,0},{1,17},{17,1},{2,18},{18,2},{3,19},{19,3},{4,20},{20... | collective-permute-start | bytes 2654216 | tf_op jit(solution)/shard_map/ppermute | solution.py:24
  12.0 32.2 %collective-permute-start = (s32[2]{0:T(128)S(1)}, s32[2]{0:T(128)}, u32[]{:S(2)}, u32[]{:S(2)}) collective-permute-start(s32[2]{0:T(128)S(1)} %copy-done.17), channel_id=1, source_target_pairs={{0,16},{16,0},{1,17},{17,1},{2,18},{18,2},{3,19},{19,3},{4,20},{20... | collective-permute-start | bytes 32 | tf_op jit(solution)/shard_map/ppermute | solution.py:24
  50.8 1.2 copy-start.2
  52.1 53.6 %collective-permute-start.2 = (f32[6,192,192]{2,1,0:T(8,128)}, f32[6,192,192]{2,1,0:T(8,128)}, u32[]{:S(2)}, u32[]{:S(2)}) collective-permute-start(f32[6,192,192]{2,1,0:T(8,128)} %constant_dynamic-slice_fusion.own_ref), channel_id=1, source_target_pairs={{0,2},{1,3},{2,0},{3,1},{4,6},{5,7},{6,4},{7,5},{8,10},{9,11},{10,... | collective-permute-start | bytes 2654216 | tf_op jit(solution)/shard_map/ppermute | solution.py:487
  55.6 2.2 copy-start.3
  57.8 1.2 copy-start.14
  65.5 1.2 copy-start.5
  66.7 50.6 %all-to-all-start.1 = ((f32[16,9,24,128]{3,2,1,0:T(8,128)}), f32[16,9,24,128]{3,2,1,0:T(8,128)}, u32[]{:S(2)}, u32[]{:S(2)}) async-start(f32[16,9,24,128]{3,2,1,0:T(8,128)} %copy-done.5), calls=%async_computation.1 | async-start | bytes 3538944 | tf_op jit(solution)/shard_map/all_to_all | solution.py:519
  105.7 1.3 copy-start.12
  108.7 1.0 copy-start.6
  109.7 1.0 copy-start.9
  117.3 1.3 copy-start.7
  118.6 1.3 copy-start.10
  123.2 27.4 %copy-start.13 = (bf16[384,1152]{1,0:T(8,128)(2,1)S(1)}, bf16[384,1152]{1,0:T(8,128)(2,1)}, u32[]{:S(2)}) copy-start(bf16[384,1152]{1,0:T(8,128)(2,1)} %constant.68.clone.synthesis_ref) | copy-start | bytes 2654212
  157.0 25.9 %copy-start.8 = (bf16[12,192,192]{2,1,0:T(8,128)(2,1)S(1)}, bf16[12,192,192]{2,1,0:T(8,128)(2,1)}, u32[]{:S(2)}) copy-start(bf16[12,192,192]{2,1,0:T(8,128)(2,1)} %copy-done.6) | copy-start | bytes 2654212
  157.1 25.9 %copy-start.11 = (bf16[12,192,192]{2,1,0:T(8,128)(2,1)S(1)}, bf16[12,192,192]{2,1,0:T(8,128)(2,1)}, u32[]{:S(2)}) copy-start(bf16[12,192,192]{2,1,0:T(8,128)(2,1)} %copy-done.9) | copy-start | bytes 2654212

commit v3 on v1

v3 whole, which is shorter than its diff:
```python
import functools
import math

import jax
import jax.numpy as jnp
import ml_dtypes
import numpy as np
from jax import lax
from jax.experimental import pallas as pl
from jax.experimental.pallas import tpu as pltpu
from jax.sharding import PartitionSpec as P

STEPS = 2
MESH_AXES = ("seg", "rad", "ax")
UNROLL = [12, 2, 2, 2, 2, 2, 16, 6]
VMEM_LIMIT = 24 * 1024 * 1024
FLOPS = 40_000_000_000

highest = lax.Precision.HIGHEST


def passed_along(value, axis, steps):
    count = lax.axis_size(axis)
    pairs = [(source, (source + steps) % count) for source in range(count)]
    return lax.ppermute(value, axis, pairs)


def padded_2(array, sides, width):
    for axis, dim in sides:
        peers, length = (lax.axis_size(axis), array.shape[dim])
        up = [(i, (i + 1) % peers) for i in range(peers)]
        down = [(j, i) for i, j in up]
        last = lax.slice_in_dim(array, length - width, length, axis=dim)
        leading = lax.slice_in_dim(array, 0, width, axis=dim)
        before = lax.ppermute(last, axis, up)
        after = lax.ppermute(leading, axis, down)
        array = jnp.concatenate([before, array, after], axis=dim)
    return array


def fourier_tables(columns, kept_modes):
    modes_total = columns // 2
    row_index = lax.broadcasted_iota(jnp.int32, (columns, columns), 0)
    point_index = lax.broadcasted_iota(jnp.int32, (columns, columns), 1)
    mode_index = row_index // 2
    phase = (mode_index * point_index % columns).astype(jnp.float32) * (2.0 * math.pi / columns)
    even_rows = row_index % 2 == 0
    cosine = jnp.cos(phase)
    sine = jnp.sin(phase)
    root = math.sqrt(modes_total)
    synthesis = jnp.where(even_rows, cosine, sine) / root
    weights = jnp.where(mode_index == 0, 1.0, 2.0)
    analysis = jnp.where(even_rows, weights * cosine, 2.0 * sine) * (root / columns)
    analysis = jnp.where(mode_index < kept_modes, analysis, 0.0)
    return (synthesis, analysis)


def radial_solve(pencils, radial_inverse, radial_rows):
    local_modes = radial_inverse.shape[0]
    local_columns, members, axial_cells, ignored = pencils.shape
    own_rows = lax.dynamic_slice_in_dim(
        radial_inverse, lax.axis_index("rad") * radial_rows, radial_rows, 1
    )
    piece = lax.all_gather(pencils, "rad", axis=3, tiled=True)
    piece_rows = piece.shape[3]
    grouped = piece.reshape(local_modes, 2, members, axial_cells, piece_rows)
    product = jnp.einsum("mrs,mkqzs->mkqzr", own_rows, grouped, precision=highest)
    return product.reshape(local_columns, members, axial_cells, radial_rows)


def general_body(start_states, radial_inverse, offsets, mode_count):
    groups, components, axial_rows, radial_rows, columns = start_states.shape
    synthesis, analysis = fourier_tables(columns, mode_count[0])
    radius = (
        (lax.axis_index("rad") * radial_rows + jnp.arange(radial_rows)).astype(jnp.float32) + 0.5
    ) / (radial_rows * lax.axis_size("rad"))
    profile = (1.0 - radius * radius).reshape(1, 1, 1, radial_rows, 1)
    following = passed_along(start_states[0], "seg", -1)
    current = start_states
    for step_index in range(STEPS):
        if step_index == 0:
            physical = jnp.einsum("gczrj,jp->gczrp", current, synthesis, precision=highest)
        else:
            physical = jnp.einsum("jgczr,jp->gczrp", current, synthesis, precision=highest)
        padded = padded_2(physical, (("ax", 2),), 1)
        gradient = (padded[:, :, 2:] - padded[:, :, :-2]) * 20.0
        advecting = profile + padded[:, 2:3, 1:-1]
        forcing = physical - 0.02 * advecting * gradient
        spectral = jnp.einsum("gczrp,jp->jgczr", forcing, analysis, precision=highest)
        pencils = lax.all_to_all(spectral, "ax", split_axis=0, concat_axis=3, tiled=True)
        local_columns = pencils.shape[0]
        axial_cells = pencils.shape[3]
        pencils = pencils.reshape(local_columns, groups * components, axial_cells, radial_rows)
        solved = radial_solve(pencils, radial_inverse, radial_rows)
        if step_index == STEPS - 1:
            blocks = solved.reshape(local_columns, groups, components, axial_cells, radial_rows)
            shifted = [
                jnp.roll(blocks[:, member], offsets[member], axis=2) for member in range(groups)
            ]
            solved = jnp.stack(shifted, axis=1).reshape(
                local_columns, groups * components, axial_cells, radial_rows
            )
        returned = lax.all_to_all(solved, "ax", split_axis=2, concat_axis=0, tiled=True)
        current = returned.reshape(columns, groups, components, axial_rows, radial_rows)
    ending = jnp.transpose(current, (1, 2, 3, 4, 0))
    upcoming = jnp.concatenate([start_states[1:], following[None]], axis=0)
    return ending - upcoming


def halves(high):
    top = high.astype(jnp.bfloat16)
    return top, (high - top.astype(jnp.float32)).astype(jnp.bfloat16)


def product(left, right, contract):
    return lax.dot_general(
        left, right, ((contract[:1], contract[1:]), ((), ())), preferred_element_type=jnp.float32
    )


def stacked_table(table):
    top = table.astype(ml_dtypes.bfloat16)
    rest = (table - top.astype(np.float64)).astype(ml_dtypes.bfloat16)
    return np.concatenate([top, top, rest], axis=1)


def column_order(columns, quarter_modes, shares):
    each = quarter_modes // shares
    order = []
    for share in range(shares):
        for low in range(2):
            for high in range(2):
                first = (2 * high + low) * quarter_modes + share * each
                order.extend(range(2 * first, 2 * (first + each)))
    assert sorted(order) == list(range(columns))
    return np.array(order)


def tables(columns, order):
    modes_total = columns // 2
    rows = np.arange(columns)
    mode = rows // 2
    phase = (mode[:, None] * np.arange(columns)[None, :]) % columns * (2.0 * np.pi / columns)
    even = (rows % 2 == 0)[:, None]
    root = math.sqrt(modes_total)
    synthesis = np.where(even, np.cos(phase), np.sin(phase)) / root
    weights = np.where(mode == 0, 1.0, 2.0)[:, None]
    analysis = np.where(even, weights * np.cos(phase), 2.0 * np.sin(phase)) * (root / columns)
    return (
        np.ascontiguousarray(stacked_table(synthesis.T).T),
        stacked_table(np.ascontiguousarray(synthesis.T[:, order])),
        stacked_table(analysis[order]),
        mode[order].astype(np.int32),
    )


def lane_index(block):
    return lax.broadcasted_iota(jnp.int32, block.shape, 1)


def spread(tiles, fourth):
    lane = lane_index(fourth)
    return [
        jnp.where(lane < 96, block, pltpu.roll(fourth, 96 - 32 * index, 1))
        for index, block in enumerate(tiles)
    ]


def gathered(waves):
    lane = lane_index(waves[0])
    fourth = jnp.where(lane < 32, pltpu.roll(waves[0], 32, 1), pltpu.roll(waves[1], 64, 1))
    return waves + [jnp.where(lane < 64, fourth, pltpu.roll(waves[2], 96, 1))]


def every(blocks, first, step):
    return jnp.concatenate(blocks[first::step], axis=0)


def pieces(block):
    return [block[at : at + 8] for at in range(0, block.shape[0], 8)]


def spread_list(blocks):
    whole = len(blocks) // 4 * 4
    quarters = [every(blocks[:whole], first, 4) for first in range(4)]
    full = [pieces(block) for block in spread(quarters[:3], quarters[3])]
    return [block for group in zip(*full) for block in group] + blocks[whole:]


def gathered_list(full, count):
    whole = count // 4 * 3
    blocks = [pieces(block) for block in gathered([every(full[:whole], i, 3) for i in range(3)])]
    return [block for group in zip(*blocks) for block in group] + full[whole:]


def physical_to_spectral(physical, profile, analysis):
    lane = lane_index(physical[0])
    z = lane & 7
    low = lane & 16 == 0
    forcing = []
    for tile in range(3):
        field = physical[tile]
        above = jnp.where(low, pltpu.roll(field, 119, 1), pltpu.roll(field, 23, 1))
        above = jnp.where(z < 7, pltpu.roll(field, 127, 1), above)
        below = jnp.where(low, pltpu.roll(field, 105, 1), pltpu.roll(field, 9, 1))
        below = jnp.where(z > 0, pltpu.roll(field, 1, 1), below)
        speed = jnp.where(lane < 32, pltpu.roll(field, 64, 1), pltpu.roll(field, 96, 1))
        speed = jnp.where(lane < 64, speed, field)
        speed = jnp.where(lane < 96, speed, physical[2])
        forcing.append(field - 0.4 * (profile[tile : tile + 1] + speed) * (above - below))
    forcing = jnp.concatenate(forcing, axis=1)
    top, rest = halves(forcing)
    return product(analysis, jnp.concatenate([top, rest, top], axis=0), (1, 0))


def write_spectral(spectral, count_ref, mode_ref, out_ref):
    members, ignored, width, ignored = out_ref.shape
    kept = mode_ref[...] < count_ref[0]
    for tile in range(3):
        block = jnp.where(kept, spectral[:, tile * 128 : (tile + 1) * 128], 0.0)
        out_ref[:, tile] = block.reshape(members, width, 128)


def first_phase_a(
    count_ref,
    before_ref,
    own_ref,
    after_ref,
    synthesis_ref,
    analysis_ref,
    mode_ref,
    profile_ref,
    out_ref,
    held_ref,
):
    groups, components, planes, radii, columns = own_ref.shape
    strips = columns // 128
    rows = []
    for segment in range(groups):
        for component in range(components):
            rows.append(before_ref[segment, component])
            rows += [own_ref[segment, component, plane] for plane in range(planes)]
            rows.append(after_ref[segment, component])
    top, rest = halves(jnp.concatenate(rows, axis=0))
    physical = product(jnp.concatenate([top, rest, top], axis=1), synthesis_ref[...], (1, 0))
    physical = physical.reshape(groups, components, planes + 2, radii, columns)
    profile = jnp.concatenate([profile_ref[...]] * strips, axis=1)
    for segment in range(groups):
        for plane in range(planes):
            speed = 0.4 * (profile + physical[segment, 2, plane + 1])
            for component in range(components):
                line = physical[segment, component]
                forcing = line[plane + 1] - speed * (line[plane + 2] - line[plane])
                first = (component * groups + segment) * radii * planes
                at = pl.ds(first + plane, radii, stride=planes)
                for strip in range(strips):
                    held_ref[strip, at, :] = forcing[:, strip * 128 : (strip + 1) * 128]
    quad = 4 * planes
    lines = []
    for strip in range(strips):
        parts = []
        for tile in range(3):
            for four, blocks in ((tile, range(6)), (3, (2 * tile, 2 * tile + 1))):
                for block in blocks:
                    at = block * radii * planes + four * quad
                    parts.append(held_ref[strip, at : at + quad, :])
        lines.append(jnp.concatenate(parts, axis=0))
    top, rest = halves(jnp.concatenate(lines, axis=1))
    spectral = product(analysis_ref[...], jnp.concatenate([top, rest, top], axis=1), (1, 1))
    write_spectral(spectral, count_ref, mode_ref, out_ref)


def later_phase_a(
    members,
    count_ref,
    wire_ref,
    synthesis_ref,
    analysis_ref,
    mode_ref,
    profile_ref,
    out_ref,
    state_ref,
):
    sources, tiles, ignored, ignored = wire_ref.shape
    groups, ignored, ignored = state_ref.shape
    parts = out_ref.shape[2] // 8
    pairs = 2 * groups
    group = pl.program_id(0)

    @pl.when(group == 0)
    def _():
        low = lax.broadcasted_iota(jnp.int32, (8 * pairs, 128), 1) & 16 == 0

        @pl.loop(0, members, unroll=UNROLL[5])
        def _(member):
            first = member // 2 * 4 + lax.rem(member, 2)
            both = [
                gathered_list(pieces(wire_ref[source].reshape(tiles * 8, 128)), pairs * parts)
                for source in (first, first + 2)
            ]
            for part in range(parts):
                at = pl.ds(pl.multiple_of((member * parts + part) * 8, 8), 8)
                one, two = (
                    jnp.concatenate(blocks[part * pairs : (part + 1) * pairs], axis=0)
                    for blocks in both
                )
                even = pieces(jnp.where(low, one, pltpu.roll(two, 16, 1)))
                odd = pieces(jnp.where(low, pltpu.roll(one, 112, 1), two))
                radii = [every(even, 0, 2), every(odd, 0, 2), every(even, 1, 2), every(odd, 1, 2)]
                for tile, block in enumerate(spread(radii[:3], radii[3])):
                    for place in range(groups):
                        state_ref[place, at, tile * 128 : (tile + 1) * 128] = block[
                            8 * place : 8 * place + 8
                        ]

    top, rest = halves(state_ref[group])
    physical = product(synthesis_ref[...], jnp.concatenate([top, rest, top], axis=0), (1, 0))
    physical = [physical[:, tile * 128 : (tile + 1) * 128] for tile in range(3)]
    spectral = physical_to_spectral(physical, profile_ref[0], analysis_ref[...])
    write_spectral(spectral, count_ref, mode_ref, out_ref)


def unpack_quads(wire_ref, held_ref, peers):
    members, tiles, width, ignored = wire_ref.shape
    seg_places, rad_places, ignored = peers
    lane = lax.broadcasted_iota(jnp.int32, (4 * width, 128), 1)
    eight, four = lane & 8 == 0, lane & 4 == 0

    def swapped(mask, step, left, right):
        return (
            jnp.where(mask, left, pltpu.roll(right, step, 1)),
            jnp.where(mask, pltpu.roll(left, 128 - step, 1), right),
        )

    groups = tiles // 3

    @pl.loop(0, rad_places * groups, unroll=UNROLL[1])
    def _(index):
        rad, group = index // groups, lax.rem(index, groups)
        sources = [(s * rad_places + rad) * 2 + l for s in range(seg_places) for l in range(2)]
        waves = [
            jnp.concatenate([wire_ref[source, 3 * group + tile] for source in sources], axis=0)
            for tile in range(3)
        ]
        quads = gathered(waves)
        one, two, three, last = (
            jnp.concatenate([quad[at : at + width] for quad in quads], axis=0)
            for at in range(0, 4 * width, width)
        )
        one, three = swapped(eight, 8, one, three)
        two, last = swapped(eight, 8, two, last)
        radii = swapped(four, 4, one, two) + swapped(four, 4, three, last)
        for place, block in enumerate(radii):
            for quad in range(4):
                at = pl.multiple_of((index * 16 + 4 * quad + place) * width, 8)
                held_ref[pl.ds(at, width), :] = block[quad * width : (quad + 1) * width]


def first_radius(member, own):
    rad = lax.rem(member // 2, 4)
    return ((rad * 2 + member // 8) * 2 + lax.rem(member, 2)) * own


def unpack_radii(wire_ref, held_ref):
    members, tiles, width, ignored = wire_ref.shape
    own = tiles * 4 // 3

    @pl.loop(0, members, unroll=UNROLL[2])
    def _(member):
        first = first_radius(member, own)
        waves = [
            jnp.concatenate([wire_ref[member, at] for at in range(tile, tiles, 3)], axis=0)
            for tile in range(3)
        ]
        for index, block in enumerate(gathered(waves)):
            for group in range(tiles // 3):
                at = pl.multiple_of((first + 4 * group + index) * width, 8)
                held_ref[pl.ds(at, width), :] = block[group * width : (group + 1) * width]


def pack_inverse(place_ref, inverse_ref, out_ref, held_ref, sem):
    each, radii, ignored = held_ref.shape
    copy = pltpu.make_async_copy(inverse_ref.at[pl.ds(place_ref[0] * each, each)], held_ref, sem)
    copy.start()
    copy.wait()
    for index in range(each):
        out_ref[index] = held_ref[index, :, :128]
    for index in range(each // 2):
        out_ref[each + index, :, :64] = held_ref[index, :, 128:]
        out_ref[each + index, :, 64:] = held_ref[each // 2 + index, :, 128:]


def ordered_inverse(place_ref, own_ref, other_ref, top_ref, rest_ref):
    each = top_ref.shape[0] // 2
    first_half = place_ref[1] == 0

    def matrix(ref, index):
        side = index // (each // 2) * 64
        tail = ref[each + index % (each // 2), :, side : side + 64]
        return jnp.concatenate([ref[index], tail], axis=1)

    for index in range(each):
        here, there = matrix(own_ref, index), matrix(other_ref, index)
        top_ref[index], rest_ref[index] = halves(jnp.where(first_half, here, there))
        top_ref[each + index], rest_ref[each + index] = halves(jnp.where(first_half, there, here))


def inverse_copies(top_hbm, rest_hbm, top_ref, rest_ref, sems):
    copies = [
        pltpu.make_async_copy(source, target, sems.at[index])
        for index, (source, target) in enumerate(((top_hbm, top_ref), (rest_hbm, rest_ref)))
    ]
    for copy in copies:
        copy.start()
    return copies


def solved_modes(top_ref, rest_ref, held_ref, transposed, store):
    modes, radii, ignored = top_ref.shape
    width = 2 * modes

    @pl.loop(0, modes, unroll=UNROLL[0])
    def _(mode):
        matrix_top, matrix_rest = top_ref[mode], rest_ref[mode]
        state = jnp.concatenate(
            [held_ref[pl.ds(2 * mode + part, radii, stride=width), :] for part in range(2)], axis=1
        )
        if transposed:
            top, rest = halves(state.T)
            solved = product(top, matrix_top, (1, 1))
            solved += product(rest, matrix_top, (1, 1)) + product(top, matrix_rest, (1, 1))
        else:
            top, rest = halves(state)
            solved = product(matrix_top, top, (1, 0))
            solved += product(matrix_top, rest, (1, 0)) + product(matrix_rest, top, (1, 0))
        store(mode, solved)


def phase_b(
    peers, top_hbm, rest_hbm, wire_ref, out_ref, held_ref, solved_ref, top_ref, rest_ref, sems
):
    members, tiles, width, ignored = wire_ref.shape
    radii = top_ref.shape[1]
    ax_places = peers[2]
    copies = inverse_copies(top_hbm, rest_hbm, top_ref, rest_ref, sems)
    unpack_quads(wire_ref, held_ref, peers)
    for copy in copies:
        copy.wait()

    def store(mode, solved):
        for part in range(2):
            solved_ref[pl.ds(2 * mode + part, radii, stride=width), :] = solved[
                :, part * 128 : (part + 1) * 128
            ]

    solved_modes(top_ref, rest_ref, held_ref, False, store)
    own = radii // members
    low = lax.broadcasted_iota(jnp.int32, (own * width // 2, 128), 1) & 16 == 0

    @pl.loop(0, members, unroll=UNROLL[3])
    def _(member):
        place = first_radius(member, own) * width
        for half in range(2):
            one, two = (
                jnp.concatenate(
                    [
                        solved_ref[pl.ds(pl.multiple_of(place + index * width, 8), width), :]
                        for index in range(first, own, 2)
                    ],
                    axis=0,
                )
                for first in range(2)
            )
            if half == 0:
                blocks = pieces(jnp.where(low, one, pltpu.roll(two, 16, 1)))
            else:
                blocks = pieces(jnp.where(low, pltpu.roll(one, 112, 1), two))
            parts = width // 8
            split = [block for part in range(parts) for block in blocks[part::parts]]
            target = member // 2 * ax_places + 2 * half + lax.rem(member, 2)
            for index, block in enumerate(spread_list(split)):
                out_ref[target, index] = block


def last_phase_b(
    peers,
    place_ref,
    own_offset_ref,
    other_offset_ref,
    top_hbm,
    rest_hbm,
    wire_ref,
    out_ref,
    held_ref,
    solved_ref,
    top_ref,
    rest_ref,
    sems,
):
    members, tiles, width, ignored = wire_ref.shape
    radii = top_ref.shape[1]
    seg_places, rad_places, ax_places = peers
    planes = 16 // ax_places
    each = radii // rad_places
    copies = inverse_copies(top_hbm, rest_hbm, top_ref, rest_ref, sems)
    unpack_radii(wire_ref, held_ref)
    for copy in copies:
        copy.wait()

    def store(mode, solved):
        for part in range(2):
            rows = pl.ds(2 * mode + part, 96, stride=width)
            block = solved[part * 128 : part * 128 + 96]
            solved_ref[0, rows, :] = block[:, :128]
            solved_ref[1, rows, 0 : radii - 128] = block[:, 128:]

    solved_modes(top_ref, rest_ref, held_ref, True, store)
    lane = lax.broadcasted_iota(jnp.int32, (planes // 2 * width, 128), 1)

    def radial_piece(low, high, rad, at):
        first = rad * each
        if first + each <= 128:
            return pltpu.roll(low, (at - first) % 128, 1)
        if first >= 128:
            return pltpu.roll(high, (at - first) % 128, 1)
        return pltpu.roll(jnp.where(lane >= first, low, high), (at - first) % 128, 1)

    half = place_ref[1]

    @pl.loop(0, seg_places * ax_places, unroll=UNROLL[4])
    def _(index):
        seg, ax = index // ax_places, lax.rem(index, ax_places)
        offset = jnp.where(place_ref[2] == seg, own_offset_ref[half], other_offset_ref[half])
        blocks = {}
        for component in range(3):
            for plane in range(planes):
                source = lax.rem(ax * planes + plane - offset + 16, 16)
                row = (component * 32 + source // 8 * 16 + seg * 8 + lax.rem(source, 8)) * width
                row = pl.multiple_of(row, 8)
                blocks[component, plane] = row
        for rad in range(rad_places):
            parts = width // 8
            slots = []
            for component in range(3):
                sides = []
                for side in range(2):
                    rows = [
                        pl.ds(blocks[component, plane], width) for plane in range(side, planes, 2)
                    ]
                    low, high = (
                        jnp.concatenate([solved_ref[strip, at, :] for at in rows], axis=0)
                        for strip in range(2)
                    )
                    sides.append(radial_piece(low, high, rad, side * each))
                slots += pieces(jnp.where(lane < each, *sides))
            split = [block for part in range(parts) for block in slots[part::parts]]
            target = (seg * rad_places + rad) * ax_places + ax
            for at, block in enumerate(spread_list(split)):
                out_ref[target, at] = block


def residual_end(peers, wire_ref, start_ref, following_ref, out_ref, held_ref):
    seg_places, rad_places, ax_places = peers
    groups, components, planes, each, columns = out_ref.shape
    shares = seg_places * rad_places
    width = columns // (2 * shares)
    chunk = width // 2
    count = (width // 8) * components * (planes // 2)
    slots = components * (planes // 2)
    for half in range(2):

        @pl.loop(0, 2 * shares, unroll=UNROLL[6])
        def _(member):
            share, low = member // 2, lax.rem(member, 2)
            source = share * ax_places + 2 * half + low
            split = gathered_list(pieces(wire_ref[source].reshape(-1, 128)), count)
            for slot in range(slots):
                parts = [split[part * slots + slot] for part in range(width // 8)]
                rows = jnp.concatenate(parts, axis=0)
                for high in range(2):
                    at = (2 * high + low) * (columns // 4) + share * chunk
                    held_ref[slot, pl.ds(at, chunk), :] = rows[high * chunk : (high + 1) * chunk]

        @pl.loop(0, slots, unroll=UNROLL[7])
        def _(slot):
            component, pair = slot // (planes // 2), lax.rem(slot, planes // 2)
            ending = held_ref[slot].T
            for side in range(2):
                plane = 2 * pair + side
                if half + 1 < groups:
                    upcoming = start_ref[half + 1, component, plane]
                else:
                    upcoming = following_ref[component, plane]
                out_ref[half, component, plane] = ending[side * each : (side + 1) * each] - upcoming


def in_place(value):
    return pltpu.with_memory_space_constraint(value, pltpu.HBM)


def whole_blocks(count):
    return [pl.BlockSpec(memory_space=pltpu.VMEM)] * count


def fits(shape, peers):
    groups, components, axial_rows, radial_rows, columns = shape
    seg_places, rad_places, ax_places = peers
    members = seg_places * rad_places * 2
    return (
        (groups, components, seg_places, ax_places) == (2, 3, 2, 4)
        and axial_rows * ax_places == 16
        and radial_rows == 48
        and rad_places * radial_rows == 192
        and columns == 384
        and members == 16
    )


def half_body(peers, start_states, radial_inverse, offsets, mode_count):
    groups, components, axial_rows, radial_rows, columns = start_states.shape
    seg_places, rad_places, ax_places = peers
    axial = axial_rows * ax_places
    radii = radial_rows * rad_places
    shares = seg_places * rad_places
    members = 2 * shares
    own_radii = radii // members
    own_modes = radial_inverse.shape[0] // shares
    width = columns // members
    tiles = own_radii * 3 // 4
    order = column_order(columns, radial_inverse.shape[0], shares)
    synthesis_natural, synthesis, analysis, mode_of_row = tables(columns, order)

    seg, rad, ax = (lax.axis_index(name) for name in MESH_AXES)
    half, low = ax // 2, ax % 2

    def device(s, r, a):
        return (s * rad_places + r) * ax_places + a

    half_groups = [
        [
            device(s, r, 2 * h + l)
            for s in range(seg_places)
            for r in range(rad_places)
            for l in range(2)
        ]
        for h in range(2)
    ]
    mirror = [(a, (a + 2) % 4) for a in range(4)]
    params = pltpu.CompilerParams(vmem_limit_bytes=VMEM_LIMIT)
    up = [(i, (i + 1) % ax_places) for i in range(ax_places)]
    down = [(j, i) for i, j in up]
    before = lax.ppermute(start_states[:, :, axial_rows - 1], "ax", up)
    after = lax.ppermute(start_states[:, :, 0], "ax", down)

    share = seg * rad_places + rad
    place = jnp.stack([share, half, seg]).astype(jnp.int32)
    with jax.named_scope("pack_inverse"):
        dense_inverse = pl.pallas_call(
            pack_inverse,
            in_specs=[
                pl.BlockSpec(memory_space=pltpu.SMEM),
                pl.BlockSpec(memory_space=pltpu.HBM),
            ],
            out_specs=pl.BlockSpec(memory_space=pltpu.VMEM),
            out_shape=jax.ShapeDtypeStruct((own_modes * 3 // 2, radii, 128), jnp.float32),
            scratch_shapes=[
                pltpu.VMEM((own_modes, radii, radii), jnp.float32),
                pltpu.SemaphoreType.DMA,
            ],
            compiler_params=params,
        )(place, in_place(radial_inverse))
    other_offsets = passed_along(offsets, "seg", 1)
    first = rad * radial_rows + (seg * 2 + low) * own_radii
    tile_index = np.arange(tiles)[:, None]
    lane = np.arange(128)[None, :]
    local = 4 * (tile_index // 3) + np.where(lane < 96, tile_index % 3, 3)
    radius = ((first + jnp.asarray(local)).astype(jnp.float32) + 0.5) / radii
    profile = (1.0 - radius * radius).reshape(tiles // 3, 3, 128)

    own_radius = ((rad * radial_rows + jnp.arange(radial_rows)).astype(jnp.float32) + 0.5) / radii
    own_profile = jnp.broadcast_to((1.0 - own_radius * own_radius)[:, None], (radial_rows, 128))

    following = passed_along(start_states[0], "seg", -1)
    before, after, dense_inverse, following, other_offsets, profile, own_profile = (
        lax.optimization_barrier(
            (before, after, dense_inverse, following, other_offsets, profile, own_profile)
        )
    )
    other_inverse = lax.ppermute(dense_inverse, "ax", mirror)
    matrices = jax.ShapeDtypeStruct((2 * own_modes, radii, radii), jnp.bfloat16)
    in_hbm = [pl.BlockSpec(memory_space=pltpu.HBM)] * 2
    inverse_scratch = [pltpu.VMEM(matrices.shape, matrices.dtype)] * 2
    inverse_scratch += [pltpu.SemaphoreType.DMA((2,))]
    with jax.named_scope("ordered_inverse"):
        inverse = pl.pallas_call(
            ordered_inverse,
            in_specs=[pl.BlockSpec(memory_space=pltpu.SMEM)] + whole_blocks(2),
            out_specs=[pl.BlockSpec(matrices.shape, lambda: (0, 0, 0))] * 2,
            out_shape=[pltpu.HBM(matrices.shape, matrices.dtype)] * 2,
            compiler_params=params,
            cost_estimate=pl.CostEstimate(
                flops=FLOPS, bytes_accessed=16 * own_modes * radii * radii, transcendentals=0
            ),
        )(place, dense_inverse, other_inverse)
    synthesis_natural, synthesis, analysis = (
        jnp.asarray(table) for table in (synthesis_natural, synthesis, analysis)
    )
    mode_rows = jnp.asarray(np.repeat(mode_of_row[:, None], 128, axis=1))
    wire = jax.ShapeDtypeStruct((members, tiles, width, 128), jnp.float32)
    wire_spec = pl.BlockSpec((members, 3, width, 128), lambda g: (0, g, 0, 0))
    held = pltpu.VMEM((radii * width, 128), jnp.float32)
    count = (width // 8) * components * (axial_rows // 2)
    end_tiles = (count // 4) * 3 + count % 4
    everyone = seg_places * rad_places * ax_places
    spread_wire = jax.ShapeDtypeStruct((everyone, end_tiles, 8, 128), jnp.float32)

    def exchanged(value):
        return lax.all_to_all(
            value, MESH_AXES, 0, 0, axis_index_groups=half_groups, tiled=True
        )

    step = radial_rows // 3
    halo_spec = pl.BlockSpec((groups, components, step, columns), lambda g: (0, 0, g, 0))
    with jax.named_scope("phase_a_first"):
        spectral = pl.pallas_call(
            first_phase_a,
            grid=(3,),
            in_specs=[
                pl.BlockSpec(memory_space=pltpu.SMEM),
                halo_spec,
                pl.BlockSpec(
                    (groups, components, axial_rows, step, columns), lambda g: (0, 0, 0, g, 0)
                ),
                halo_spec,
                pl.BlockSpec((3 * columns, columns), lambda g: (0, 0)),
                pl.BlockSpec((columns, 3 * columns), lambda g: (0, 0)),
                pl.BlockSpec((columns, 128), lambda g: (0, 0)),
                pl.BlockSpec((step, 128), lambda g: (g, 0)),
            ],
            out_specs=wire_spec,
            out_shape=wire,
            scratch_shapes=[
                pltpu.VMEM(
                    (columns // 128, groups * components * axial_rows * step, 128), jnp.float32
                )
            ],
            compiler_params=params,
        )(
            mode_count,
            before,
            start_states,
            after,
            synthesis_natural,
            analysis,
            mode_rows,
            own_profile,
        )
    lines = exchanged(spectral)
    with jax.named_scope("phase_b_first"):
        solved = pl.pallas_call(
            functools.partial(phase_b, peers),
            in_specs=in_hbm + whole_blocks(1),
            out_specs=pl.BlockSpec(memory_space=pltpu.VMEM),
            out_shape=spread_wire,
            scratch_shapes=[held, held] + inverse_scratch,
            compiler_params=params,
        )(*map(in_place, inverse), lines)
    state = lax.all_to_all(solved, MESH_AXES, 0, 0, tiled=True)
    with jax.named_scope("phase_a_later"):
        spectral = pl.pallas_call(
            functools.partial(later_phase_a, members),
            grid=(tiles // 3,),
            in_specs=[
                pl.BlockSpec(memory_space=pltpu.SMEM),
                pl.BlockSpec(spread_wire.shape, lambda g: (0, 0, 0, 0)),
                pl.BlockSpec((columns, 3 * columns), lambda g: (0, 0)),
                pl.BlockSpec((columns, 3 * columns), lambda g: (0, 0)),
                pl.BlockSpec((columns, 128), lambda g: (0, 0)),
                pl.BlockSpec((1, 3, 128), lambda g: (g, 0, 0)),
            ],
            out_specs=wire_spec,
            out_shape=wire,
            scratch_shapes=[pltpu.VMEM((tiles // 3, columns, 3 * 128), jnp.float32)],
            compiler_params=params,
        )(mode_count, state, synthesis, analysis, mode_rows, profile)
    lines = exchanged(spectral)
    with jax.named_scope("phase_b_last"):
        ending = pl.pallas_call(
            functools.partial(last_phase_b, peers),
            in_specs=[pl.BlockSpec(memory_space=pltpu.SMEM)] * 3 + in_hbm + whole_blocks(1),
            out_specs=pl.BlockSpec(memory_space=pltpu.VMEM),
            out_shape=spread_wire,
            scratch_shapes=[held, pltpu.VMEM((2, 96 * width, 128), jnp.float32)]
            + inverse_scratch,
            compiler_params=params,
        )(place, offsets, other_offsets, *map(in_place, inverse), lines)
    ending = lax.all_to_all(ending, MESH_AXES, 0, 0, tiled=True)
    with jax.named_scope("residual_end"):
        return pl.pallas_call(
            functools.partial(residual_end, peers),
            in_specs=whole_blocks(3),
            out_specs=pl.BlockSpec(memory_space=pltpu.VMEM),
            out_shape=jax.ShapeDtypeStruct(start_states.shape, jnp.float32),
            scratch_shapes=[pltpu.VMEM((components * (axial_rows // 2), columns, 128), jnp.float32)],
            compiler_params=params,
        )(ending, start_states, following)


def solution(mesh):
    peers = tuple(mesh.shape[name] for name in MESH_AXES)

    def body(start_states, radial_inverse, offsets, mode_count):
        if fits(start_states.shape, peers):
            return half_body(peers, start_states, radial_inverse, offsets, mode_count)
        return general_body(start_states, radial_inverse, offsets, mode_count)

    placed = (P("seg", None, "ax", "rad", None), P("ax", None, None), P("seg"), P())
    return jax.shard_map(
        body,
        mesh=mesh,
        in_specs=placed,
        out_specs=P("seg", None, "ax", "rad", None),
        check_vma=False,
    )
```

time: 258 us -> 229 us (0.89)
  waiting for transfers between devices: 155 us -> 50.2 us
  blocking collectives: 27.5 us -> 121 us
  local copies, waits for them, and re-layouts: 22.3 us -> 5.27 us
  Pallas kernels: 26.4 us -> 37.7 us
  starting transfers between devices: 23.7 us -> 13.3 us
    all_to_all x0 -> x2, blocking collectives: none -> 95.1 us  [the longest x1 48.8 us: half_body(): state = lax.all_to_all(solved, MESH_AXES, 0, 0, tiled=True)]
    ppermute x2, waiting for transfers between devices: 57.9 us -> 10.7 us  [passed_along(): return lax.ppermute(value, axis, pairs)]
    all_to_all x2 -> x0, waiting for transfers between devices: 43.7 us -> none  [the longest x1 40.4 us: half_body(): arrived = lax.all_to_all(split, ('seg', 'ax'), 0, 0, tiled=True)]
    ppermute x1 -> x3, waiting for transfers between devices: 53.5 us -> 29.5 us  [the longest x1 25.7 us: half_body(): other_inverse = lax.ppermute(dense_inverse, 'ax', mirror)]
    pallas_call x4 -> x6, Pallas kernels: 22.6 us -> 35.4 us  [the longest x1 10.5 us: half_body(): pl.pallas_call(functools.partial(later_phase_a, members), grid=(tiles //...]
    all_to_all x2 -> x0, starting transfers between devices: 10.6 us -> none  [the longest x1 6.49 us: half_body(): arrived = lax.all_to_all(split, ('seg', 'ax'), 0, 0, tiled=True)]
    all_to_all x2 -> x1, waiting for transfers between devices: 0.01 us -> 10 us  [exchanged(): lax.all_to_all(value, MESH_AXES, 0, 0, axis_index_groups=half_groups, til...]
    reshape x3 -> x0, local copies, waits for them, and re-layouts: 7.46 us -> none  [the longest x1 2.88 us: half_body(): rows = rows.reshape(own_radii, components * seg_places * axial, columns)]
  transfers between devices with their start and end apart: 7 -> 6, of which waited for: 5 -> 4; matrix products, arithmetic and copies ran while one was open for 2% -> 1% of each run, Pallas kernels for 0% -> 5%
where the time goes in v3:
time: 229 us
  blocking collectives  121 us (53%)
  waiting for transfers between devices  50.2 us (22%)
  Pallas kernels  37.7 us (16%)
  starting transfers between devices  13.3 us (6%)
  local copies, waits for them, and re-layouts  5.27 us (2%)
    all_to_all x1, blocking collectives, half_body(): state = lax.all_to_all(solved, MESH_AXES, 0, 0, tiled=True)  48.8 us
    all_to_all x1, blocking collectives, half_body(): ending = lax.all_to_all(ending, MESH_AXES, 0, 0, tiled=True)  46.4 us
    ppermute x1, waiting for transfers between devices, half_body(): other_inverse = lax.ppermute(dense_inverse, 'ax', mirror)  25.7 us
    all_to_all x1, blocking collectives, exchanged(): lax.all_to_all(value, MESH_AXES, 0, 0, axis_index_groups=half_groups, til...  25.6 us
    ppermute x2, waiting for transfers between devices, passed_along(): return lax.ppermute(value, axis, pairs)  10.7 us
    pallas_call x1, Pallas kernels, half_body(): pl.pallas_call(functools.partial(later_phase_a, members), grid=(tiles //...  10.5 us
    all_to_all x1, waiting for transfers between devices, exchanged(): lax.all_to_all(value, MESH_AXES, 0, 0, axis_index_groups=half_groups, til...  10 us
    all_to_all x1, starting transfers between devices, exchanged(): lax.all_to_all(value, MESH_AXES, 0, 0, axis_index_groups=half_groups, til...  7.33 us
  transfers between devices with their start and end apart: 6, of which 4 were waited for; matrix products, arithmetic and copies ran while one was open for 1% of the time, Pallas kernels for 5%

profile of v3, /device:TPU:1, one launch (start us, length us, event | category | flops | bytes accessed | tf_op | source)
XLA Modules:
  0.0 228.7 jit_solution(4160090703911062214)
XLA Ops:
  0.0 0.0 copy-start
  0.0 0.0 copy-start.11
  0.0 2.3 slice_bitcast_fusion
  2.3 2.0 collective-permute-start.2
  4.3 0.0 collective-permute-start.3
  4.3 0.0 copy-done
  4.3 1.0 slice_bitcast_fusion.1
  5.3 3.5 %collective-permute-start.1 = (f32[2,3,48,384]{3,2,1,0:T(8,128)}, f32[2,3,48,384]{3,2,1,0:T(8,128)S(1)}, u32[]{:S(2)}, u32[]{:S(2)}) collective-permute-start(f32[2,3,48,384]{3,2,1,0:T(8,128)} %get-tuple-element.23), channel_id=1, source_target_pairs={{1,0},{2,1},{3,2},{0,3},{5,4},{6,5},{7,6},{4,7},{9,8},{10,9},{11,1... | collective-permute-start | bytes 1327112 | tf_op jit(solution)/shard_map/ppermute | solution.py:653
  8.9 0.0 collective-permute-start
  8.9 0.0 copy-done.11
  8.9 0.6 multiply_subtract_fusion
  9.5 0.7 reshape.12.profile_ref
  10.2 0.1 pad_add_fusion.place_ref
  10.3 2.9 %pack_inverse.1.own_ref = f32[9,192,128]{2,1,0:T(8,128)} custom-call(s32[3]{0:T(128)S(1)} %pad_add_fusion.place_ref, f32[48,192,192]{2,1,0:T(8,128)} %inverse_ref.1), custom_call_target="tpu_custom_call" | custom-call | tf_op jit(solution)/shard_map/pack_inverse/pallas_call | solution.py:658
  13.2 10.7 %collective-permute-done.3.other_offset_ref = s32[2]{0:T(128)S(1)} collective-permute-done((s32[2]{0:T(128)}, s32[2]{0:T(128)S(1)}, u32[]{:S(2)}, u32[]{:S(2)}) %collective-permute-start.3) | collective-permute-done | bytes 40 | tf_op jit(solution)/shard_map/ppermute | solution.py:25
  23.9 0.0 collective-permute-done.1.after_ref
  23.9 3.8 %collective-permute-done.before_ref = f32[2,3,48,384]{3,2,1,0:T(8,128)S(1)} collective-permute-done((f32[2,3,48,384]{3,2,1,0:T(8,128)}, f32[2,3,48,384]{3,2,1,0:T(8,128)S(1)}, u32[]{:S(2)}, u32[]{:S(2)}) %collective-permute-start) | collective-permute-done | bytes 442400 | tf_op jit(solution)/shard_map/ppermute | solution.py:652
  27.7 0.0 collective-permute-done.2.following_ref
  27.7 0.1 broadcast_in_dim.2.profile_ref
  27.8 0.3 collective-permute-start.4
  28.7 0.0 copy-done.2
  28.7 0.0 copy-done.7
  28.8 0.0 copy-done.8
  28.8 5.3 %phase_a_first.1 = f32[16,9,24,128]{3,2,1,0:T(8,128)S(1)} custom-call(s32[1]{0:T(128)S(6)} %copy.14.count_ref, f32[2,3,48,384]{3,2,1,0:T(8,128)S(1)} %collective-permute-done.before_ref, f32[2,3,4,48,384]{4,3,2,1,0:T(8,128)S(1)} %copy-done, f32[2,3,48,384]{3,2,1,0:T(8,128)S(1)} %collective-permute-done.1.after_ref, bf16[1152,384]{1,0:T(8,128)(2,1)S(1)} %copy-done.7, ...), custom_call_target="tpu_custom_call" | custom-call | tf_op jit(solution)/shard_map/phase_a_first/pallas_call | solution.py:725
  34.1 0.0 copy-done.4
  34.1 0.0 copy-start.1
  34.1 1.2 copy-done.1
  35.3 7.3 %all-to-all-start = ((f32[16,9,24,128]{3,2,1,0:T(8,128)}), f32[16,9,24,128]{3,2,1,0:T(8,128)S(1)}, u32[]{:S(2)}, u32[]{:S(2)}) async-start(f32[16,9,24,128]{3,2,1,0:T(8,128)} %copy-done.1), calls=%async_computation | async-start | bytes 3538944 | tf_op jit(solution)/shard_map/all_to_all | solution.py:718
  42.7 25.7 %collective-permute-done.4.other_ref = f32[9,192,128]{2,1,0:T(8,128)} collective-permute-done((f32[9,192,128]{2,1,0:T(8,128)}, f32[9,192,128]{2,1,0:T(8,128)}, u32[]{:S(2)}, u32[]{:S(2)}) %collective-permute-start.4) | collective-permute-done | bytes 884768 | tf_op jit(solution)/shard_map/ppermute | solution.py:689
  68.4 3.3 %ordered_inverse.1 = (bf16[12,192,192]{2,1,0:T(8,128)(2,1)}, bf16[12,192,192]{2,1,0:T(8,128)(2,1)}) custom-call(s32[3]{0:T(128)S(1)} %pad_add_fusion.place_ref, f32[9,192,128]{2,1,0:T(8,128)} %pack_inverse.1.own_ref, f32[9,192,128]{2,1,0:T(8,128)} %collective-permute-done.4.other_ref), custom_call_target="tpu_custom_call" | custom-call | flops 40000000000 | bytes 3538944 | tf_op jit(solution)/shard_map/ordered_inverse/pallas_call | solution.py:695
  71.7 10.0 %all-to-all-done.wire_ref = f32[16,9,24,128]{3,2,1,0:T(8,128)S(1)} async-done(((f32[16,9,24,128]{3,2,1,0:T(8,128)}), f32[16,9,24,128]{3,2,1,0:T(8,128)S(1)}, u32[]{:S(2)}, u32[]{:S(2)}) %all-to-all-start) | async-done | bytes 1769504 | tf_op jit(solution)/shard_map/all_to_all | solution.py:718
  81.7 6.3 %phase_b_first.1 = f32[32,14,8,128]{3,2,1,0:T(8,128)S(1)} custom-call(bf16[12,192,192]{2,1,0:T(8,128)(2,1)} %get-tuple-element.16.top_hbm, bf16[12,192,192]{2,1,0:T(8,128)(2,1)} %get-tuple-element.17.rest_hbm, f32[16,9,24,128]{3,2,1,0:T(8,128)S(1)} %all-to-all-done.wire_ref), custom_call_target="tpu_custom_call" | custom-call | tf_op jit(solution)/shard_map/phase_b_first/pallas_call | solution.py:760
  88.0 0.0 copy-start.3
  88.1 0.0 copy-start.6
  88.1 0.0 copy-start.9
  88.1 48.8 %all_to_all.20.wire_ref = f32[32,14,8,128]{3,2,1,0:T(8,128)S(1)} all-to-all(f32[32,14,8,128]{3,2,1,0:T(8,128)S(1)} %phase_b_first.1), channel_id=1, replica_groups=mesh['seg'=2,'rad'=4,'ax'=4] {'seg','rad','ax'}, dimensions={0} | all-to-all | bytes 3670016 | tf_op jit(solution)/shard_map/all_to_all | solution.py:768
  136.9 0.0 copy-done.3
  136.9 0.0 copy-done.6
  136.9 0.0 copy-done.9
  136.9 10.5 %phase_a_later.1 = f32[16,9,24,128]{3,2,1,0:T(8,128)S(1)} custom-call(s32[1]{0:T(128)S(6)} %copy.14.count_ref, f32[32,14,8,128]{3,2,1,0:T(8,128)S(1)} %all_to_all.20.wire_ref, bf16[384,1152]{1,0:T(8,128)(2,1)S(1)} %copy-done.6, bf16[384,1152]{1,0:T(8,128)(2,1)S(1)} %copy-done.3, s32[384,128]{1,0:T(8,128)S(1)} %copy-done.9, f32[3,3,128]{2,1,0:T(4,128)S(1)} %reshape.12.profile_ref), custom_call_target="tpu_custom_call" | custom-call | tf_op jit(solution)/shard_map/phase_a_later/pallas_call | solution.py:770
  147.4 0.0 copy-start.10
  147.4 25.6 %all_to_all.21.wire_ref = f32[16,9,24,128]{3,2,1,0:T(8,128)S(1)} all-to-all(f32[16,9,24,128]{3,2,1,0:T(8,128)S(1)} %phase_a_later.1), channel_id=1, replica_groups={{0,1,4,5,8,9,12,13,16,17,20,21,24,25,28,29},{2,3,6,7,10,11,14,15,18,19,..., dimensions={0} | all-to-all | bytes 3538944 | tf_op jit(solution)/shard_map/all_to_all | solution.py:718
  173.0 0.0 copy-done.10
  173.0 6.9 %phase_b_last.1 = f32[32,14,8,128]{3,2,1,0:T(8,128)S(1)} custom-call(s32[3]{0:T(128)S(1)} %pad_add_fusion.place_ref, s32[2]{0:T(128)S(1)} %copy-done.10, s32[2]{0:T(128)S(1)} %collective-permute-done.3.other_offset_ref, bf16[12,192,192]{2,1,0:T(8,128)(2,1)} %get-tuple-element.16.top_hbm, bf16[12,192,192]{2,1,0:T(8,128)(2,1)} %get-tuple-element.17.rest_hbm, ...), custom_call_target="tpu_custom_call" | custom-call | tf_op jit(solution)/shard_map/phase_b_last/pallas_call | solution.py:788
  179.9 0.0 copy-start.5
  180.0 46.4 %all_to_all.22.wire_ref = f32[32,14,8,128]{3,2,1,0:T(8,128)S(1)} all-to-all(f32[32,14,8,128]{3,2,1,0:T(8,128)S(1)} %phase_b_last.1), channel_id=1, replica_groups=mesh['seg'=2,'rad'=4,'ax'=4] {'seg','rad','ax'}, dimensions={0} | all-to-all | bytes 3670016 | tf_op jit(solution)/shard_map/all_to_all | solution.py:797
  226.3 0.0 copy-done.5
  226.3 2.3 %residual_end.1 = f32[2,3,4,48,384]{4,3,2,1,0:T(8,128)} custom-call(f32[32,14,8,128]{3,2,1,0:T(8,128)S(1)} %all_to_all.22.wire_ref, f32[2,3,4,48,384]{4,3,2,1,0:T(8,128)S(1)} %copy-done, f32[3,4,48,384]{3,2,1,0:T(8,128)S(1)} %copy-done.5), custom_call_target="tpu_custom_call" | custom-call | tf_op jit(solution)/shard_map/residual_end/pallas_call | solution.py:799
  (5 shorter events, 0.0 us)
Async XLA Ops:
  0.0 4.3 %copy-start = (f32[2,3,4,48,384]{4,3,2,1,0:T(8,128)S(1)}, f32[2,3,4,48,384]{4,3,2,1,0:T(8,128)}, u32[]{:S(2)}) copy-start(f32[2,3,4,48,384]{4,3,2,1,0:T(8,128)} %start_ref.1) | copy-start | bytes 5308420
  0.0 8.9 %copy-start.11 = (s32[9,128]{1,0:T(8,128)S(1)}, s32[9,128]{1,0:T(8,128)}, u32[]{:S(2)}) copy-start(s32[9,128]{1,0:T(8,128)} %constant.64.clone) | copy-start | bytes 13828
  2.3 25.4 %collective-permute-start.2 = (f32[3,4,48,384]{3,2,1,0:T(8,128)}, f32[3,4,48,384]{3,2,1,0:T(8,128)S(1)}, u32[]{:S(2)}, u32[]{:S(2)}) collective-permute-start(f32[3,4,48,384]{3,2,1,0:T(8,128)} %slice_bitcast_fusion), channel_id=1, source_target_pairs={{0,16},{16,0},{1,17},{17,1},{2,18},{18,2},{3,19},{19,3},{4,20},{20... | collective-permute-start | bytes 2654216 | tf_op jit(solution)/shard_map/ppermute | solution.py:25
  4.3 19.6 %collective-permute-start.3 = (s32[2]{0:T(128)}, s32[2]{0:T(128)S(1)}, u32[]{:S(2)}, u32[]{:S(2)}) collective-permute-start(s32[2]{0:T(128)} %own_offset_ref.1), channel_id=1, source_target_pairs={{0,16},{16,0},{1,17},{17,1},{2,18},{18,2},{3,19},{19,3},{4,20},{20... | collective-permute-start | bytes 32 | tf_op jit(solution)/shard_map/ppermute | solution.py:25
  5.3 18.6 %collective-permute-start.1 = (f32[2,3,48,384]{3,2,1,0:T(8,128)}, f32[2,3,48,384]{3,2,1,0:T(8,128)S(1)}, u32[]{:S(2)}, u32[]{:S(2)}) collective-permute-start(f32[2,3,48,384]{3,2,1,0:T(8,128)} %get-tuple-element.23), channel_id=1, source_target_pairs={{1,0},{2,1},{3,2},{0,3},{5,4},{6,5},{7,6},{4,7},{9,8},{10,9},{11,1... | collective-permute-start | bytes 1327112 | tf_op jit(solution)/shard_map/ppermute | solution.py:653
  8.9 18.8 %collective-permute-start = (f32[2,3,48,384]{3,2,1,0:T(8,128)}, f32[2,3,48,384]{3,2,1,0:T(8,128)S(1)}, u32[]{:S(2)}, u32[]{:S(2)}) collective-permute-start(f32[2,3,48,384]{3,2,1,0:T(8,128)} %get-tuple-element.24), channel_id=1, source_target_pairs={{0,1},{1,2},{2,3},{3,0},{4,5},{5,6},{6,7},{7,4},{8,9},{9,10},{10,1... | collective-permute-start | bytes 1327112 | tf_op jit(solution)/shard_map/ppermute | solution.py:652
  10.3 18.5 %copy-start.2 = (bf16[384,1152]{1,0:T(8,128)(2,1)S(1)}, bf16[384,1152]{1,0:T(8,128)(2,1)}, u32[]{:S(2)}) copy-start(bf16[384,1152]{1,0:T(8,128)(2,1)} %constant.67.clone.analysis_ref) | copy-start | bytes 2654212
  10.3 18.5 %copy-start.7 = (bf16[1152,384]{1,0:T(8,128)(2,1)S(1)}, bf16[1152,384]{1,0:T(8,128)(2,1)}, u32[]{:S(2)}) copy-start(bf16[1152,384]{1,0:T(8,128)(2,1)} %constant.65.clone.synthesis_ref) | copy-start | bytes 2654212
  10.3 18.5 %copy-start.8 = (s32[384,128]{1,0:T(8,128)S(1)}, s32[384,128]{1,0:T(8,128)}, u32[]{:S(2)}) copy-start(s32[384,128]{1,0:T(8,128)} %constant.68.clone.mode_ref) | copy-start | bytes 589828
  27.7 6.4 %copy-start.4 = (f32[3,4,48,384]{3,2,1,0:T(8,128)}, f32[3,4,48,384]{3,2,1,0:T(8,128)S(1)}, u32[]{:S(2)}) copy-start(f32[3,4,48,384]{3,2,1,0:T(8,128)S(1)} %collective-permute-done.2.following_ref) | copy-start | bytes 2654212
  27.8 40.6 %collective-permute-start.4 = (f32[9,192,128]{2,1,0:T(8,128)}, f32[9,192,128]{2,1,0:T(8,128)}, u32[]{:S(2)}, u32[]{:S(2)}) collective-permute-start(f32[9,192,128]{2,1,0:T(8,128)} %pack_inverse.1.own_ref), channel_id=1, source_target_pairs={{0,2},{1,3},{2,0},{3,1},{4,6},{5,7},{6,4},{7,5},{8,10},{9,11},{10,... | collective-permute-start | bytes 2654216 | tf_op jit(solution)/shard_map/ppermute | solution.py:689
  34.1 1.2 copy-start.1
  35.3 46.4 %all-to-all-start = ((f32[16,9,24,128]{3,2,1,0:T(8,128)}), f32[16,9,24,128]{3,2,1,0:T(8,128)S(1)}, u32[]{:S(2)}, u32[]{:S(2)}) async-start(f32[16,9,24,128]{3,2,1,0:T(8,128)} %copy-done.1), calls=%async_computation | async-start | bytes 3538944 | tf_op jit(solution)/shard_map/all_to_all | solution.py:718
  88.0 48.8 %copy-start.3 = (bf16[384,1152]{1,0:T(8,128)(2,1)S(1)}, bf16[384,1152]{1,0:T(8,128)(2,1)}, u32[]{:S(2)}) copy-start(bf16[384,1152]{1,0:T(8,128)(2,1)} %constant.67.clone.analysis_ref) | copy-start | bytes 2654212
  88.1 48.8 %copy-start.6 = (bf16[384,1152]{1,0:T(8,128)(2,1)S(1)}, bf16[384,1152]{1,0:T(8,128)(2,1)}, u32[]{:S(2)}) copy-start(bf16[384,1152]{1,0:T(8,128)(2,1)} %constant.66.clone.synthesis_ref) | copy-start | bytes 2654212
  88.1 48.8 %copy-start.9 = (s32[384,128]{1,0:T(8,128)S(1)}, s32[384,128]{1,0:T(8,128)}, u32[]{:S(2)}) copy-start(s32[384,128]{1,0:T(8,128)} %constant.68.clone.mode_ref) | copy-start | bytes 589828
  147.4 25.6 %copy-start.10 = (s32[2]{0:T(128)S(1)}, s32[2]{0:T(128)}, u32[]{:S(2)}) copy-start(s32[2]{0:T(128)} %own_offset_ref.1) | copy-start | bytes 28
  179.9 46.4 %copy-start.5 = (f32[3,4,48,384]{3,2,1,0:T(8,128)S(1)}, f32[3,4,48,384]{3,2,1,0:T(8,128)}, u32[]{:S(2)}) copy-start(f32[3,4,48,384]{3,2,1,0:T(8,128)} %copy-done.4) | copy-start | bytes 2654212

commit v4 on v3

--- a/solution.py
+++ b/solution.py
@@ -12,7 +12,7 @@
 
 STEPS = 2
 MESH_AXES = ("seg", "rad", "ax")
-UNROLL = [12, 2, 2, 2, 2, 2, 16, 6]
+UNROLL = [12, 2, 16, 2, 8, 4, 16, 6]
 VMEM_LIMIT = 24 * 1024 * 1024
 FLOPS = 40_000_000_000
 
@@ -195,15 +195,12 @@
 
 def physical_to_spectral(physical, profile, analysis):
     lane = lane_index(physical[0])
-    z = lane & 7
-    low = lane & 16 == 0
+    z = lane & 15
     forcing = []
     for tile in range(3):
         field = physical[tile]
-        above = jnp.where(low, pltpu.roll(field, 119, 1), pltpu.roll(field, 23, 1))
-        above = jnp.where(z < 7, pltpu.roll(field, 127, 1), above)
-        below = jnp.where(low, pltpu.roll(field, 105, 1), pltpu.roll(field, 9, 1))
-        below = jnp.where(z > 0, pltpu.roll(field, 1, 1), below)
+        above = jnp.where(z < 15, pltpu.roll(field, 127, 1), pltpu.roll(field, 15, 1))
+        below = jnp.where(z > 0, pltpu.roll(field, 1, 1), pltpu.roll(field, 113, 1))
         speed = jnp.where(lane < 32, pltpu.roll(field, 64, 1), pltpu.roll(field, 96, 1))
         speed = jnp.where(lane < 64, speed, field)
         speed = jnp.where(lane < 96, speed, physical[2])
@@ -219,6 +216,17 @@
     for tile in range(3):
         block = jnp.where(kept, spectral[:, tile * 128 : (tile + 1) * 128], 0.0)
         out_ref[:, tile] = block.reshape(members, width, 128)
+
+
+def synthesized(rows, synthesis):
+    top, rest = halves(jnp.concatenate(rows, axis=0))
+    return product(jnp.concatenate([top, rest, top], axis=1), synthesis, (1, 0))
+
+
+def own_physical(own_ref, synthesis_ref, out_ref):
+    groups, components, planes, radii, columns = own_ref.shape
+    rows = own_ref[...].reshape(groups * components * planes * radii, columns)
+    out_ref[...] = synthesized([rows], synthesis_ref[...]).reshape(out_ref.shape)
 
 
 def first_phase_a(
@@ -235,21 +243,16 @@
 ):
     groups, components, planes, radii, columns = own_ref.shape
     strips = columns // 128
-    rows = []
-    for segment in range(groups):
-        for component in range(components):
-            rows.append(before_ref[segment, component])
-            rows += [own_ref[segment, component, plane] for plane in range(planes)]
-            rows.append(after_ref[segment, component])
-    top, rest = halves(jnp.concatenate(rows, axis=0))
-    physical = product(jnp.concatenate([top, rest, top], axis=1), synthesis_ref[...], (1, 0))
-    physical = physical.reshape(groups, components, planes + 2, radii, columns)
+    count = groups * components
+    sides = [ref[...].reshape(count * radii, columns) for ref in (before_ref, after_ref)]
+    sides = synthesized(sides, synthesis_ref[...]).reshape(2, groups, components, radii, columns)
     profile = jnp.concatenate([profile_ref[...]] * strips, axis=1)
     for segment in range(groups):
         for plane in range(planes):
-            speed = 0.4 * (profile + physical[segment, 2, plane + 1])
+            speed = 0.4 * (profile + own_ref[segment, 2, plane])
             for component in range(components):
-                line = physical[segment, component]
+                line = [own_ref[segment, component, i] for i in range(planes)]
+                line = [sides[0, segment, component], *line, sides[1, segment, component]]
                 forcing = line[plane + 1] - speed * (line[plane + 2] - line[plane])
                 first = (component * groups + segment) * radii * planes
                 at = pl.ds(first + plane, radii, stride=planes)
@@ -260,10 +263,12 @@
     for strip in range(strips):
         parts = []
         for tile in range(3):
-            for four, blocks in ((tile, range(6)), (3, (2 * tile, 2 * tile + 1))):
-                for block in blocks:
-                    at = block * radii * planes + four * quad
-                    parts.append(held_ref[strip, at : at + quad, :])
+            for four, members in ((tile, range(components)), (3, (tile,))):
+                for component in members:
+                    for at in range(four * quad, (four + 1) * quad, quad // 2):
+                        for segment in range(groups):
+                            row = (component * groups + segment) * radii * planes + at
+                            parts.append(held_ref[strip, row : row + quad // 2, :])
         lines.append(jnp.concatenate(parts, axis=0))
     top, rest = halves(jnp.concatenate(lines, axis=1))
     spectral = product(analysis_ref[...], jnp.concatenate([top, rest, top], axis=1), (1, 1))
@@ -271,7 +276,6 @@
 
 
 def later_phase_a(
-    members,
     count_ref,
     wire_ref,
     synthesis_ref,
@@ -279,52 +283,58 @@
     mode_ref,
     profile_ref,
     out_ref,
-    state_ref,
+    held_ref,
+    physical_ref,
 ):
     sources, tiles, ignored, ignored = wire_ref.shape
-    groups, ignored, ignored = state_ref.shape
+    halves_of_ax, pairs, ignored, ignored = held_ref.shape
     parts = out_ref.shape[2] // 8
-    pairs = 2 * groups
-    group = pl.program_id(0)
-
-    @pl.when(group == 0)
-    def _():
-        low = lax.broadcasted_iota(jnp.int32, (8 * pairs, 128), 1) & 16 == 0
-
-        @pl.loop(0, members, unroll=UNROLL[5])
-        def _(member):
-            first = member // 2 * 4 + lax.rem(member, 2)
-            both = [
-                gathered_list(pieces(wire_ref[source].reshape(tiles * 8, 128)), pairs * parts)
-                for source in (first, first + 2)
-            ]
+
+    def unpack():
+        @pl.loop(0, sources, unroll=UNROLL[5])
+        def _(source):
+            half = lax.rem(source, 4) // 2
+            member = source // 4 * 2 + lax.rem(source, 2)
+            blocks = gathered_list(pieces(wire_ref[source].reshape(tiles * 8, 128)), pairs * parts)
             for part in range(parts):
                 at = pl.ds(pl.multiple_of((member * parts + part) * 8, 8), 8)
-                one, two = (
-                    jnp.concatenate(blocks[part * pairs : (part + 1) * pairs], axis=0)
-                    for blocks in both
-                )
-                even = pieces(jnp.where(low, one, pltpu.roll(two, 16, 1)))
-                odd = pieces(jnp.where(low, pltpu.roll(one, 112, 1), two))
-                radii = [every(even, 0, 2), every(odd, 0, 2), every(even, 1, 2), every(odd, 1, 2)]
-                for tile, block in enumerate(spread(radii[:3], radii[3])):
-                    for place in range(groups):
-                        state_ref[place, at, tile * 128 : (tile + 1) * 128] = block[
-                            8 * place : 8 * place + 8
-                        ]
-
-    top, rest = halves(state_ref[group])
-    physical = product(synthesis_ref[...], jnp.concatenate([top, rest, top], axis=0), (1, 0))
-    physical = [physical[:, tile * 128 : (tile + 1) * 128] for tile in range(3)]
-    spectral = physical_to_spectral(physical, profile_ref[0], analysis_ref[...])
-    write_spectral(spectral, count_ref, mode_ref, out_ref)
+                for pair in range(pairs):
+                    held_ref[half, pair, at, :] = blocks[part * pairs + pair]
+
+    def begin(group):
+        radii = []
+        for pair in range(2):
+            one, two = (held_ref[half, 2 * group + pair] for half in range(halves_of_ax))
+            low = lane_index(one) & 8 == 0
+            radii.append(jnp.where(low, one, pltpu.roll(two, 8, 1)))
+            radii.append(jnp.where(low, pltpu.roll(one, 120, 1), two))
+        top, rest = halves(jnp.concatenate(spread(radii[:3], radii[3]), axis=1))
+        physical_ref[group % 2] = product(
+            synthesis_ref[...], jnp.concatenate([top, rest, top], axis=0), (1, 0)
+        )
+
+    def finish(group):
+        physical = [physical_ref[group % 2, :, tile * 128 : (tile + 1) * 128] for tile in range(3)]
+        spectral = physical_to_spectral(physical, profile_ref[group], analysis_ref[...])
+        write_spectral(spectral, count_ref, mode_ref, out_ref)
+
+    for step in range(pairs // 2 + 1):
+
+        @pl.when(pl.program_id(0) == step)
+        def _(step=step):
+            if step == 0:
+                unpack()
+            if step < pairs // 2:
+                begin(step)
+            if step > 0:
+                finish(step - 1)
 
 
 def unpack_quads(wire_ref, held_ref, peers):
     members, tiles, width, ignored = wire_ref.shape
     seg_places, rad_places, ignored = peers
     lane = lax.broadcasted_iota(jnp.int32, (4 * width, 128), 1)
-    eight, four = lane & 8 == 0, lane & 4 == 0
+    sixteen, four = lane & 16 == 0, lane & 4 == 0
 
     def swapped(mask, step, left, right):
         return (
@@ -347,8 +357,8 @@
             jnp.concatenate([quad[at : at + width] for quad in quads], axis=0)
             for at in range(0, 4 * width, width)
         )
-        one, three = swapped(eight, 8, one, three)
-        two, last = swapped(eight, 8, two, last)
+        one, three = swapped(sixteen, 16, one, three)
+        two, last = swapped(sixteen, 16, two, last)
         radii = swapped(four, 4, one, two) + swapped(four, 4, three, last)
         for place, block in enumerate(radii):
             for quad in range(4):
@@ -378,16 +388,28 @@
                 held_ref[pl.ds(at, width), :] = block[group * width : (group + 1) * width]
 
 
-def pack_inverse(place_ref, inverse_ref, out_ref, held_ref, sem):
+def pack_sent(
+    place_ref, offset_ref, inverse_ref, start_ref, out_ref, first_ref, held_ref, start_held_ref, sems
+):
     each, radii, ignored = held_ref.shape
-    copy = pltpu.make_async_copy(inverse_ref.at[pl.ds(place_ref[0] * each, each)], held_ref, sem)
+    copy = pltpu.make_async_copy(
+        inverse_ref.at[pl.ds(place_ref[0] * each, each)], held_ref, sems.at[0]
+    )
     copy.start()
+    first = pltpu.make_async_copy(start_ref.at[0], start_held_ref, sems.at[1])
+    first.start()
+    rows = first_ref.shape[0] - 8
+    for index in range(8):
+        offset = offset_ref[index % offset_ref.shape[0]].astype(jnp.float32)
+        first_ref[rows + index : rows + index + 1, :] = jnp.full((1, first_ref.shape[1]), offset)
     copy.wait()
     for index in range(each):
         out_ref[index] = held_ref[index, :, :128]
     for index in range(each // 2):
         out_ref[each + index, :, :64] = held_ref[index, :, 128:]
         out_ref[each + index, :, 64:] = held_ref[each // 2 + index, :, 128:]
+    first.wait()
+    first_ref[0:rows, :] = start_held_ref[...].reshape(rows, first_ref.shape[1])
 
 
 def ordered_inverse(place_ref, own_ref, other_ref, top_ref, rest_ref):
@@ -426,6 +448,10 @@
             [held_ref[pl.ds(2 * mode + part, radii, stride=width), :] for part in range(2)], axis=1
         )
         if transposed:
+            matrix_top, matrix_rest = (
+                jnp.concatenate([m[:96], m[:32], m[96:], m[:32]], axis=0)
+                for m in (matrix_top, matrix_rest)
+            )
             top, rest = halves(state.T)
             solved = product(top, matrix_top, (1, 1))
             solved += product(rest, matrix_top, (1, 1)) + product(top, matrix_rest, (1, 1))
@@ -455,7 +481,7 @@
 
     solved_modes(top_ref, rest_ref, held_ref, False, store)
     own = radii // members
-    low = lax.broadcasted_iota(jnp.int32, (own * width // 2, 128), 1) & 16 == 0
+    low = lax.broadcasted_iota(jnp.int32, (own * width // 2, 128), 1) & 8 == 0
 
     @pl.loop(0, members, unroll=UNROLL[3])
     def _(member):
@@ -472,9 +498,9 @@
                 for first in range(2)
             )
             if half == 0:
-                blocks = pieces(jnp.where(low, one, pltpu.roll(two, 16, 1)))
+                blocks = pieces(jnp.where(low, one, pltpu.roll(two, 8, 1)))
             else:
-                blocks = pieces(jnp.where(low, pltpu.roll(one, 112, 1), two))
+                blocks = pieces(jnp.where(low, pltpu.roll(one, 120, 1), two))
             parts = width // 8
             split = [block for part in range(parts) for block in blocks[part::parts]]
             target = member // 2 * ax_places + 2 * half + lax.rem(member, 2)
@@ -502,6 +528,10 @@
     seg_places, rad_places, ax_places = peers
     planes = 16 // ax_places
     each = radii // rad_places
+    half = place_ref[1]
+    rows = other_offset_ref.shape[0] - 8
+    others = [jnp.max(other_offset_ref[rows + i : rows + i + 1, :128]) for i in range(2)]
+    other_offset = jnp.where(half == 0, *others).astype(jnp.int32)
     copies = inverse_copies(top_hbm, rest_hbm, top_ref, rest_ref, sems)
     unpack_radii(wire_ref, held_ref)
     for copy in copies:
@@ -511,31 +541,22 @@
         for part in range(2):
             rows = pl.ds(2 * mode + part, 96, stride=width)
             block = solved[part * 128 : part * 128 + 96]
-            solved_ref[0, rows, :] = block[:, :128]
-            solved_ref[1, rows, 0 : radii - 128] = block[:, 128:]
+            for strip in range(2):
+                solved_ref[strip, rows, :] = block[:, strip * 128 : (strip + 1) * 128]
 
     solved_modes(top_ref, rest_ref, held_ref, True, store)
     lane = lax.broadcasted_iota(jnp.int32, (planes // 2 * width, 128), 1)
 
-    def radial_piece(low, high, rad, at):
-        first = rad * each
-        if first + each <= 128:
-            return pltpu.roll(low, (at - first) % 128, 1)
-        if first >= 128:
-            return pltpu.roll(high, (at - first) % 128, 1)
-        return pltpu.roll(jnp.where(lane >= first, low, high), (at - first) % 128, 1)
-
-    half = place_ref[1]
 
     @pl.loop(0, seg_places * ax_places, unroll=UNROLL[4])
     def _(index):
         seg, ax = index // ax_places, lax.rem(index, ax_places)
-        offset = jnp.where(place_ref[2] == seg, own_offset_ref[half], other_offset_ref[half])
+        offset = jnp.where(place_ref[2] == seg, own_offset_ref[half], other_offset)
         blocks = {}
         for component in range(3):
             for plane in range(planes):
                 source = lax.rem(ax * planes + plane - offset + 16, 16)
-                row = (component * 32 + source // 8 * 16 + seg * 8 + lax.rem(source, 8)) * width
+                row = (component * 32 + seg * 16 + source) * width
                 row = pl.multiple_of(row, 8)
                 blocks[component, plane] = row
         for rad in range(rad_places):
@@ -547,11 +568,12 @@
                     rows = [
                         pl.ds(blocks[component, plane], width) for plane in range(side, planes, 2)
                     ]
-                    low, high = (
-                        jnp.concatenate([solved_ref[strip, at, :] for at in rows], axis=0)
-                        for strip in range(2)
-                    )
-                    sides.append(radial_piece(low, high, rad, side * each))
+                    lines = [solved_ref[rad // 2, at, :] for at in rows]
+                    sides.append(jnp.concatenate(lines, axis=0))
+                if rad % 2 == 0:
+                    sides[1] = pltpu.roll(sides[1], each, 1)
+                else:
+                    sides[0] = pltpu.roll(sides[0], 128 - each, 1)
                 slots += pieces(jnp.where(lane < each, *sides))
             split = [block for part in range(parts) for block in slots[part::parts]]
             target = (seg * rad_places + rad) * ax_places + ax
@@ -561,37 +583,39 @@
 
 def residual_end(peers, wire_ref, start_ref, following_ref, out_ref, held_ref):
     seg_places, rad_places, ax_places = peers
-    groups, components, planes, each, columns = out_ref.shape
+    ignored, components, planes, each, columns = out_ref.shape
     shares = seg_places * rad_places
     width = columns // (2 * shares)
     chunk = width // 2
     count = (width // 8) * components * (planes // 2)
     slots = components * (planes // 2)
-    for half in range(2):
-
-        @pl.loop(0, 2 * shares, unroll=UNROLL[6])
-        def _(member):
-            share, low = member // 2, lax.rem(member, 2)
-            source = share * ax_places + 2 * half + low
-            split = gathered_list(pieces(wire_ref[source].reshape(-1, 128)), count)
-            for slot in range(slots):
-                parts = [split[part * slots + slot] for part in range(width // 8)]
-                rows = jnp.concatenate(parts, axis=0)
-                for high in range(2):
-                    at = (2 * high + low) * (columns // 4) + share * chunk
-                    held_ref[slot, pl.ds(at, chunk), :] = rows[high * chunk : (high + 1) * chunk]
-
-        @pl.loop(0, slots, unroll=UNROLL[7])
-        def _(slot):
-            component, pair = slot // (planes // 2), lax.rem(slot, planes // 2)
-            ending = held_ref[slot].T
-            for side in range(2):
-                plane = 2 * pair + side
-                if half + 1 < groups:
-                    upcoming = start_ref[half + 1, component, plane]
-                else:
-                    upcoming = following_ref[component, plane]
-                out_ref[half, component, plane] = ending[side * each : (side + 1) * each] - upcoming
+    half = pl.program_id(0)
+
+    @pl.loop(0, 2 * shares, unroll=UNROLL[6])
+    def _(member):
+        share, low = member // 2, lax.rem(member, 2)
+        source = share * ax_places + 2 * half + low
+        split = gathered_list(pieces(wire_ref[source].reshape(-1, 128)), count)
+        for slot in range(slots):
+            parts = [split[part * slots + slot] for part in range(width // 8)]
+            rows = jnp.concatenate(parts, axis=0)
+            for high in range(2):
+                at = (2 * high + low) * (columns // 4) + share * chunk
+                held_ref[slot, pl.ds(at, chunk), :] = rows[high * chunk : (high + 1) * chunk]
+
+    @pl.loop(0, slots, unroll=UNROLL[7])
+    def _(slot):
+        component, pair = slot // (planes // 2), lax.rem(slot, planes // 2)
+        ending = held_ref[slot].T
+        for side in range(2):
+            plane = 2 * pair + side
+            row = pl.multiple_of((component * planes + plane) * each, 8)
+            upcoming = jnp.where(
+                half + 1 < pl.num_programs(0),
+                start_ref[0, component, plane],
+                following_ref[pl.ds(row, each), :],
+            )
+            out_ref[0, component, plane] = ending[side * each : (side + 1) * each] - upcoming
 
 
 def in_place(value):
@@ -654,22 +678,28 @@
 
     share = seg * rad_places + rad
     place = jnp.stack([share, half, seg]).astype(jnp.int32)
-    with jax.named_scope("pack_inverse"):
-        dense_inverse = pl.pallas_call(
-            pack_inverse,
+    first_rows = components * axial_rows * radial_rows
+    with jax.named_scope("pack_sent"):
+        dense_inverse, first_start = pl.pallas_call(
+            pack_sent,
             in_specs=[
                 pl.BlockSpec(memory_space=pltpu.SMEM),
+                pl.BlockSpec(memory_space=pltpu.SMEM),
+                pl.BlockSpec(memory_space=pltpu.HBM),
                 pl.BlockSpec(memory_space=pltpu.HBM),
             ],
-            out_specs=pl.BlockSpec(memory_space=pltpu.VMEM),
-            out_shape=jax.ShapeDtypeStruct((own_modes * 3 // 2, radii, 128), jnp.float32),
+            out_specs=whole_blocks(2),
+            out_shape=[
+                jax.ShapeDtypeStruct((own_modes * 3 // 2, radii, 128), jnp.float32),
+                jax.ShapeDtypeStruct((first_rows + 8, columns), jnp.float32),
+            ],
             scratch_shapes=[
                 pltpu.VMEM((own_modes, radii, radii), jnp.float32),
-                pltpu.SemaphoreType.DMA,
+                pltpu.VMEM(start_states.shape[1:], jnp.float32),
+                pltpu.SemaphoreType.DMA((2,)),
             ],
             compiler_params=params,
-        )(place, in_place(radial_inverse))
-    other_offsets = passed_along(offsets, "seg", 1)
+        )(place, offsets, in_place(radial_inverse), in_place(start_states))
     first = rad * radial_rows + (seg * 2 + low) * own_radii
     tile_index = np.arange(tiles)[:, None]
     lane = np.arange(128)[None, :]
@@ -680,13 +710,72 @@
     own_radius = ((rad * radial_rows + jnp.arange(radial_rows)).astype(jnp.float32) + 0.5) / radii
     own_profile = jnp.broadcast_to((1.0 - own_radius * own_radius)[:, None], (radial_rows, 128))
 
-    following = passed_along(start_states[0], "seg", -1)
-    before, after, dense_inverse, following, other_offsets, profile, own_profile = (
-        lax.optimization_barrier(
-            (before, after, dense_inverse, following, other_offsets, profile, own_profile)
+    following = passed_along(first_start, "seg", -1)
+    synthesis_natural, synthesis, analysis = (
+        jnp.asarray(table) for table in (synthesis_natural, synthesis, analysis)
+    )
+    mode_rows = jnp.asarray(np.repeat(mode_of_row[:, None], 128, axis=1))
+    wire = jax.ShapeDtypeStruct((members, tiles, width, 128), jnp.float32)
+    wire_spec = pl.BlockSpec((members, 3, width, 128), lambda g: (0, g, 0, 0))
+    held = pltpu.VMEM((radii * width, 128), jnp.float32)
+    count = (width // 8) * components * (axial_rows // 2)
+    end_tiles = (count // 4) * 3 + count % 4
+    everyone = seg_places * rad_places * ax_places
+    spread_wire = jax.ShapeDtypeStruct((everyone, end_tiles, 8, 128), jnp.float32)
+
+    def exchanged(value):
+        return lax.all_to_all(
+            value, MESH_AXES, 0, 0, axis_index_groups=half_groups, tiled=True
         )
+
+    step = radial_rows // 3
+    halo_spec = pl.BlockSpec((groups, components, step, columns), lambda g: (0, 0, g, 0))
+    own_spec = pl.BlockSpec(
+        (groups, components, axial_rows, step, columns), lambda g: (0, 0, 0, g, 0)
+    )
+    with jax.named_scope("own_physical"):
+        physical = pl.pallas_call(
+            own_physical,
+            grid=(3,),
+            in_specs=[own_spec] + whole_blocks(1),
+            out_specs=own_spec,
+            out_shape=jax.ShapeDtypeStruct(start_states.shape, jnp.float32),
+            compiler_params=params,
+        )(start_states, synthesis_natural)
+    before, after, dense_inverse, physical, profile, own_profile = lax.optimization_barrier(
+        (before, after, dense_inverse, physical, profile, own_profile)
     )
     other_inverse = lax.ppermute(dense_inverse, "ax", mirror)
+    with jax.named_scope("phase_a_first"):
+        spectral = pl.pallas_call(
+            first_phase_a,
+            grid=(3,),
+            in_specs=[
+                pl.BlockSpec(memory_space=pltpu.SMEM),
+                halo_spec,
+                own_spec,
+                halo_spec,
+                *whole_blocks(3),
+                pl.BlockSpec((step, 128), lambda g: (g, 0)),
+            ],
+            out_specs=wire_spec,
+            out_shape=pltpu.HBM(wire.shape, wire.dtype),
+            scratch_shapes=[
+                pltpu.VMEM(
+                    (columns // 128, groups * components * axial_rows * step, 128), jnp.float32
+                )
+            ],
+            compiler_params=params,
+        )(
+            mode_count,
+            before,
+            physical,
+            after,
+            synthesis_natural,
+            analysis,
+            mode_rows,
+            own_profile,
+        )
     matrices = jax.ShapeDtypeStruct((2 * own_modes, radii, radii), jnp.bfloat16)
     in_hbm = [pl.BlockSpec(memory_space=pltpu.HBM)] * 2
     inverse_scratch = [pltpu.VMEM(matrices.shape, matrices.dtype)] * 2
@@ -702,59 +791,6 @@
                 flops=FLOPS, bytes_accessed=16 * own_modes * radii * radii, transcendentals=0
             ),
         )(place, dense_inverse, other_inverse)
-    synthesis_natural, synthesis, analysis = (
-        jnp.asarray(table) for table in (synthesis_natural, synthesis, analysis)
-    )
-    mode_rows = jnp.asarray(np.repeat(mode_of_row[:, None], 128, axis=1))
-    wire = jax.ShapeDtypeStruct((members, tiles, width, 128), jnp.float32)
-    wire_spec = pl.BlockSpec((members, 3, width, 128), lambda g: (0, g, 0, 0))
-    held = pltpu.VMEM((radii * width, 128), jnp.float32)
-    count = (width // 8) * components * (axial_rows // 2)
-    end_tiles = (count // 4) * 3 + count % 4
-    everyone = seg_places * rad_places * ax_places
-    spread_wire = jax.ShapeDtypeStruct((everyone, end_tiles, 8, 128), jnp.float32)
-
-    def exchanged(value):
-        return lax.all_to_all(
-            value, MESH_AXES, 0, 0, axis_index_groups=half_groups, tiled=True
-        )
-
-    step = radial_rows // 3
-    halo_spec = pl.BlockSpec((groups, components, step, columns), lambda g: (0, 0, g, 0))
-    with jax.named_scope("phase_a_first"):
-        spectral = pl.pallas_call(
-            first_phase_a,
-            grid=(3,),
-            in_specs=[
-                pl.BlockSpec(memory_space=pltpu.SMEM),
-                halo_spec,
-                pl.BlockSpec(
-                    (groups, components, axial_rows, step, columns), lambda g: (0, 0, 0, g, 0)
-                ),
-                halo_spec,
-                pl.BlockSpec((3 * columns, columns), lambda g: (0, 0)),
-                pl.BlockSpec((columns, 3 * columns), lambda g: (0, 0)),
-                pl.BlockSpec((columns, 128), lambda g: (0, 0)),
-                pl.BlockSpec((step, 128), lambda g: (g, 0)),
-            ],
-            out_specs=wire_spec,
-            out_shape=wire,
-            scratch_shapes=[
-                pltpu.VMEM(
-                    (columns // 128, groups * components * axial_rows * step, 128), jnp.float32
-                )
-            ],
-            compiler_params=params,
-        )(
-            mode_count,
-            before,
-            start_states,
-            after,
-            synthesis_natural,
-            analysis,
-            mode_rows,
-            own_profile,
-        )
     lines = exchanged(spectral)
     with jax.named_scope("phase_b_first"):
         solved = pl.pallas_call(
@@ -765,41 +801,52 @@
             scratch_shapes=[held, held] + inverse_scratch,
             compiler_params=params,
         )(*map(in_place, inverse), lines)
+    solved, following = lax.optimization_barrier((solved, following))
     state = lax.all_to_all(solved, MESH_AXES, 0, 0, tiled=True)
     with jax.named_scope("phase_a_later"):
         spectral = pl.pallas_call(
-            functools.partial(later_phase_a, members),
-            grid=(tiles // 3,),
+            later_phase_a,
+            grid=(tiles // 3 + 1,),
             in_specs=[
                 pl.BlockSpec(memory_space=pltpu.SMEM),
-                pl.BlockSpec(spread_wire.shape, lambda g: (0, 0, 0, 0)),
-                pl.BlockSpec((columns, 3 * columns), lambda g: (0, 0)),
-                pl.BlockSpec((columns, 3 * columns), lambda g: (0, 0)),
-                pl.BlockSpec((columns, 128), lambda g: (0, 0)),
-                pl.BlockSpec((1, 3, 128), lambda g: (g, 0, 0)),
+                *whole_blocks(4),
+                *whole_blocks(1),
             ],
-            out_specs=wire_spec,
+            out_specs=pl.BlockSpec(
+                wire_spec.block_shape, lambda g: (0, jnp.maximum(g - 1, 0), 0, 0)
+            ),
             out_shape=wire,
-            scratch_shapes=[pltpu.VMEM((tiles // 3, columns, 3 * 128), jnp.float32)],
+            scratch_shapes=[
+                pltpu.VMEM((2, own_radii // 2, columns, 128), jnp.float32),
+                pltpu.VMEM((2, columns, 3 * 128), jnp.float32),
+            ],
             compiler_params=params,
         )(mode_count, state, synthesis, analysis, mode_rows, profile)
     lines = exchanged(spectral)
     with jax.named_scope("phase_b_last"):
         ending = pl.pallas_call(
             functools.partial(last_phase_b, peers),
-            in_specs=[pl.BlockSpec(memory_space=pltpu.SMEM)] * 3 + in_hbm + whole_blocks(1),
+            in_specs=[pl.BlockSpec(memory_space=pltpu.SMEM)] * 2
+            + whole_blocks(1)
+            + in_hbm
+            + whole_blocks(1),
             out_specs=pl.BlockSpec(memory_space=pltpu.VMEM),
             out_shape=spread_wire,
             scratch_shapes=[held, pltpu.VMEM((2, 96 * width, 128), jnp.float32)]
             + inverse_scratch,
             compiler_params=params,
-        )(place, offsets, other_offsets, *map(in_place, inverse), lines)
+        )(place, offsets, following, *map(in_place, inverse), lines)
     ending = lax.all_to_all(ending, MESH_AXES, 0, 0, tiled=True)
     with jax.named_scope("residual_end"):
         return pl.pallas_call(
             functools.partial(residual_end, peers),
-            in_specs=whole_blocks(3),
-            out_specs=pl.BlockSpec(memory_space=pltpu.VMEM),
+            grid=(groups,),
+            in_specs=[
+                *whole_blocks(1),
+                pl.BlockSpec((1,) + start_states.shape[1:], lambda b: (groups - 1, 0, 0, 0, 0)),
+                *whole_blocks(1),
+            ],
+            out_specs=pl.BlockSpec((1,) + start_states.shape[1:], lambda b: (b, 0, 0, 0, 0)),
             out_shape=jax.ShapeDtypeStruct(start_states.shape, jnp.float32),
             scratch_shapes=[pltpu.VMEM((components * (axial_rows // 2), columns, 128), jnp.float32)],
             compiler_params=params,

time: 229 us -> 224 us (0.978)
    ppermute x2 -> x1, waiting for transfers between devices: 10.7 us -> 0.01 us  [passed_along(): return lax.ppermute(value, axis, pairs)]
    ppermute x1, waiting for transfers between devices: 3.79 us -> 10.3 us  [half_body(): before = lax.ppermute(start_states[:, :, axial_rows - 1], 'ax', up)]
    ppermute x1, waiting for transfers between devices: 0.01 us -> 2.36 us  [half_body(): after = lax.ppermute(start_states[:, :, 0], 'ax', down)]
    pallas_call x3 -> x4, Pallas kernels: 15.8 us -> 16.5 us  [the longest x1 7.7 us: half_body(): pl.pallas_call(later_phase_a, grid=(tiles // 3 + 1,), in_specs=[pl.BlockS...]
  transfers between devices with their start and end apart: 6 -> 5, of which waited for: 4 -> 4; matrix products, arithmetic and copies ran while one was open for 1% -> 0% of each run, Pallas kernels for 5% -> 9%
where the time goes in v4:
time: 224 us
  blocking collectives  121 us (54%)
  waiting for transfers between devices  48.4 us (22%)
  Pallas kernels  38.2 us (17%)
  starting transfers between devices  11.7 us (5%)
  local copies, waits for them, and re-layouts  3.52 us (2%)
    all_to_all x1, blocking collectives, half_body(): state = lax.all_to_all(solved, MESH_AXES, 0, 0, tiled=True)  48.8 us
    all_to_all x1, blocking collectives, half_body(): ending = lax.all_to_all(ending, MESH_AXES, 0, 0, tiled=True)  46.4 us
    ppermute x1, waiting for transfers between devices, half_body(): other_inverse = lax.ppermute(dense_inverse, 'ax', mirror)  27 us
    all_to_all x1, blocking collectives, exchanged(): lax.all_to_all(value, MESH_AXES, 0, 0, axis_index_groups=half_groups, til...  25.6 us
    ppermute x1, waiting for transfers between devices, half_body(): before = lax.ppermute(start_states[:, :, axial_rows - 1], 'ax', up)  10.3 us
    all_to_all x1, waiting for transfers between devices, exchanged(): lax.all_to_all(value, MESH_AXES, 0, 0, axis_index_groups=half_groups, til...  8.73 us
    pallas_call x1, Pallas kernels, half_body(): pl.pallas_call(later_phase_a, grid=(tiles // 3 + 1,), in_specs=[pl.BlockS...  7.7 us
    pallas_call x1, Pallas kernels, half_body(): pl.pallas_call(functools.partial(last_phase_b, peers), in_specs=[pl.Block...  6.68 us
  transfers between devices with their start and end apart: 5, of which 4 were waited for; matrix products, arithmetic and copies ran while one was open for 0% of the time, Pallas kernels for 9%

profile of v4, /device:TPU:1, one launch (start us, length us, event | category | flops | bytes accessed | tf_op | source)
XLA Modules:
  0.0 223.5 jit_solution(13022675909262619898)
XLA Ops:
  0.0 0.0 copy-start.10
  0.0 0.0 copy-start
  0.0 2.2 slice_bitcast_fusion
  2.2 4.2 %collective-permute-start.1 = (f32[2,3,48,384]{3,2,1,0:T(8,128)}, f32[2,3,48,384]{3,2,1,0:T(8,128)}, u32[]{:S(2)}, u32[]{:S(2)}) collective-permute-start(f32[2,3,48,384]{3,2,1,0:T(8,128)} %get-tuple-element.29), channel_id=1, source_target_pairs={{1,0},{2,1},{3,2},{0,3},{5,4},{6,5},{7,6},{4,7},{9,8},{10,9},{11,1... | collective-permute-start | bytes 1327112 | tf_op jit(solution)/shard_map/ppermute | solution.py:677
  6.4 0.0 collective-permute-start
  6.4 0.0 copy-done.10
  6.4 0.0 copy-done
  6.4 0.0 copy-start.4
  6.4 1.2 copy-done.4
  7.6 0.0 copy-start.9
  7.6 2.2 own_physical.1.own_ref
  9.8 0.1 pad_add_fusion.place_ref
  9.9 0.0 copy-done.9
  9.9 0.0 copy-start.2
  9.9 0.0 copy-start.5
  9.9 0.0 copy-start.7
  9.9 3.4 %pack_sent.1 = (f32[9,192,128]{2,1,0:T(8,128)}, f32[584,384]{1,0:T(8,128)}) custom-call(s32[3]{0:T(128)S(1)} %pad_add_fusion.place_ref, s32[2]{0:T(128)S(1)} %copy-done.9, f32[48,192,192]{2,1,0:T(8,128)} %inverse_ref.1, f32[2,3,4,48,384]{4,3,2,1,0:T(8,128)} %start_ref.3), custom_call_target="tpu_custom_call" | custom-call | tf_op jit(solution)/shard_map/pack_sent/pallas_call | solution.py:683
  13.3 2.4 %collective-permute-done.1.after_ref = f32[2,3,48,384]{3,2,1,0:T(8,128)} collective-permute-done((f32[2,3,48,384]{3,2,1,0:T(8,128)}, f32[2,3,48,384]{3,2,1,0:T(8,128)}, u32[]{:S(2)}, u32[]{:S(2)}) %collective-permute-start.1) | collective-permute-done | bytes 442400 | tf_op jit(solution)/shard_map/ppermute | solution.py:677
  15.6 10.3 %collective-permute-done.before_ref = f32[2,3,48,384]{3,2,1,0:T(8,128)} collective-permute-done((f32[2,3,48,384]{3,2,1,0:T(8,128)}, f32[2,3,48,384]{3,2,1,0:T(8,128)}, u32[]{:S(2)}, u32[]{:S(2)}) %collective-permute-start) | collective-permute-done | bytes 442400 | tf_op jit(solution)/shard_map/ppermute | solution.py:676
  25.9 0.1 broadcast_in_dim.2.profile_ref
  26.0 0.1 collective-permute-start.2
  26.1 1.2 collective-permute-start.3
  28.0 0.0 copy-done.2
  28.0 0.0 copy-done.5
  28.0 0.0 copy-done.7
  28.0 5.3 %phase_a_first.1 = f32[16,9,24,128]{3,2,1,0:T(8,128)} custom-call(s32[1]{0:T(128)S(6)} %copy.14.count_ref, f32[2,3,48,384]{3,2,1,0:T(8,128)} %collective-permute-done.before_ref, f32[2,3,4,48,384]{4,3,2,1,0:T(8,128)S(1)} %own_physical.1.own_ref, f32[2,3,48,384]{3,2,1,0:T(8,128)} %collective-permute-done.1.after_ref, bf16[1152,384]{1,0:T(8,128)(2,1)S(1)} %copy-done.5, ...), custom_call_target="tpu_custom_call" | custom-call | tf_op jit(solution)/shard_map/phase_a_first/pallas_call | solution.py:750
  33.4 6.2 %all-to-all-start = ((f32[16,9,24,128]{3,2,1,0:T(8,128)}), f32[16,9,24,128]{3,2,1,0:T(8,128)S(1)}, u32[]{:S(2)}, u32[]{:S(2)}) async-start(f32[16,9,24,128]{3,2,1,0:T(8,128)} %phase_a_first.1), calls=%async_computation | async-start | bytes 3538944 | tf_op jit(solution)/shard_map/all_to_all | solution.py:727
  39.6 27.0 %collective-permute-done.2.other_ref = f32[9,192,128]{2,1,0:T(8,128)} collective-permute-done((f32[9,192,128]{2,1,0:T(8,128)}, f32[9,192,128]{2,1,0:T(8,128)}, u32[]{:S(2)}, u32[]{:S(2)}) %collective-permute-start.2) | collective-permute-done | bytes 884768 | tf_op jit(solution)/shard_map/ppermute | solution.py:748
  66.6 3.3 %ordered_inverse.1 = (bf16[12,192,192]{2,1,0:T(8,128)(2,1)}, bf16[12,192,192]{2,1,0:T(8,128)(2,1)}) custom-call(s32[3]{0:T(128)S(1)} %pad_add_fusion.place_ref, f32[9,192,128]{2,1,0:T(8,128)} %get-tuple-element.18.own_ref, f32[9,192,128]{2,1,0:T(8,128)} %collective-permute-done.2.other_ref), custom_call_target="tpu_custom_call" | custom-call | flops 40000000000 | bytes 3538944 | tf_op jit(solution)/shard_map/ordered_inverse/pallas_call | solution.py:784
  70.0 8.7 %all-to-all-done.wire_ref = f32[16,9,24,128]{3,2,1,0:T(8,128)S(1)} async-done(((f32[16,9,24,128]{3,2,1,0:T(8,128)}), f32[16,9,24,128]{3,2,1,0:T(8,128)S(1)}, u32[]{:S(2)}, u32[]{:S(2)}) %all-to-all-start) | async-done | bytes 1769504 | tf_op jit(solution)/shard_map/all_to_all | solution.py:727
  78.7 6.3 %phase_b_first.1 = f32[32,14,8,128]{3,2,1,0:T(8,128)S(1)} custom-call(bf16[12,192,192]{2,1,0:T(8,128)(2,1)} %get-tuple-element.19.top_hbm, bf16[12,192,192]{2,1,0:T(8,128)(2,1)} %get-tuple-element.20.rest_hbm, f32[16,9,24,128]{3,2,1,0:T(8,128)S(1)} %all-to-all-done.wire_ref), custom_call_target="tpu_custom_call" | custom-call | tf_op jit(solution)/shard_map/phase_b_first/pallas_call | solution.py:796
  85.0 0.0 copy-start.3
  85.0 0.0 copy-start.6
  85.0 0.0 copy-start.8
  85.1 0.0 collective-permute-done.3.other_offset_ref.following_ref
  85.1 48.8 %all_to_all.20.wire_ref = f32[32,14,8,128]{3,2,1,0:T(8,128)S(1)} all-to-all(f32[32,14,8,128]{3,2,1,0:T(8,128)S(1)} %phase_b_first.1), channel_id=1, replica_groups=mesh['seg'=2,'rad'=4,'ax'=4] {'seg','rad','ax'}, dimensions={0} | all-to-all | bytes 3670016 | tf_op jit(solution)/shard_map/all_to_all | solution.py:805
  133.8 0.0 copy-done.3
  133.8 0.0 copy-done.6
  133.8 0.0 copy-done.8
  133.8 7.7 %phase_a_later.1 = f32[16,9,24,128]{3,2,1,0:T(8,128)S(1)} custom-call(s32[1]{0:T(128)S(6)} %copy.14.count_ref, f32[32,14,8,128]{3,2,1,0:T(8,128)S(1)} %all_to_all.20.wire_ref, bf16[384,1152]{1,0:T(8,128)(2,1)S(1)} %copy-done.6, bf16[384,1152]{1,0:T(8,128)(2,1)S(1)} %copy-done.3, s32[384,128]{1,0:T(8,128)S(1)} %copy-done.8, f32[3,3,128]{2,1,0:T(4,128)S(1)} %reshape.12.profile_ref), custom_call_target="tpu_custom_call" | custom-call | tf_op jit(solution)/shard_map/phase_a_later/pallas_call | solution.py:807
  141.5 25.6 %all_to_all.21.wire_ref = f32[16,9,24,128]{3,2,1,0:T(8,128)S(1)} all-to-all(f32[16,9,24,128]{3,2,1,0:T(8,128)S(1)} %phase_a_later.1), channel_id=1, replica_groups={{0,1,4,5,8,9,12,13,16,17,20,21,24,25,28,29},{2,3,6,7,10,11,14,15,18,19,..., dimensions={0} | all-to-all | bytes 3538944 | tf_op jit(solution)/shard_map/all_to_all | solution.py:727
  167.2 6.7 %phase_b_last.1 = f32[32,14,8,128]{3,2,1,0:T(8,128)S(1)} custom-call(s32[3]{0:T(128)S(1)} %pad_add_fusion.place_ref, s32[2]{0:T(128)S(1)} %copy-done.9, f32[584,384]{1,0:T(8,128)} %collective-permute-done.3.other_offset_ref.following_ref, bf16[12,192,192]{2,1,0:T(8,128)(2,1)} %get-tuple-element.19.top_hbm, bf16[12,192,192]{2,1,0:T(8,128)(2,1)} %get-tuple-element.20.rest_hbm, ...), custom_call_target="tpu_custom_call" | custom-call | tf_op jit(solution)/shard_map/phase_b_last/pallas_call | solution.py:827
  173.8 0.0 copy-start.1
  173.9 46.4 %all_to_all.22.wire_ref = f32[32,14,8,128]{3,2,1,0:T(8,128)S(1)} all-to-all(f32[32,14,8,128]{3,2,1,0:T(8,128)S(1)} %phase_b_last.1), channel_id=1, replica_groups=mesh['seg'=2,'rad'=4,'ax'=4] {'seg','rad','ax'}, dimensions={0} | all-to-all | bytes 3670016 | tf_op jit(solution)/shard_map/all_to_all | solution.py:839
  220.2 0.0 copy-done.1
  220.2 3.3 %residual_end.1 = f32[2,3,4,48,384]{4,3,2,1,0:T(8,128)} custom-call(f32[32,14,8,128]{3,2,1,0:T(8,128)S(1)} %all_to_all.22.wire_ref, f32[2,3,4,48,384]{4,3,2,1,0:T(8,128)S(1)} %copy-done.1, f32[584,384]{1,0:T(8,128)} %collective-permute-done.3.other_offset_ref.following_ref), custom_call_target="tpu_custom_call" | custom-call | tf_op jit(solution)/shard_map/residual_end/pallas_call | solution.py:841
  (3 shorter events, 0.0 us)
Async XLA Ops:
  0.0 6.4 %copy-start.10 = (s32[9,128]{1,0:T(8,128)S(1)}, s32[9,128]{1,0:T(8,128)}, u32[]{:S(2)}) copy-start(s32[9,128]{1,0:T(8,128)} %constant.64.clone) | copy-start | bytes 13828
  0.0 6.4 %copy-start = (f32[2,3,4,48,384]{4,3,2,1,0:T(8,128)S(1)}, f32[2,3,4,48,384]{4,3,2,1,0:T(8,128)}, u32[]{:S(2)}) copy-start(f32[2,3,4,48,384]{4,3,2,1,0:T(8,128)} %start_ref.3) | copy-start | bytes 5308420
  2.2 13.4 %collective-permute-start.1 = (f32[2,3,48,384]{3,2,1,0:T(8,128)}, f32[2,3,48,384]{3,2,1,0:T(8,128)}, u32[]{:S(2)}, u32[]{:S(2)}) collective-permute-start(f32[2,3,48,384]{3,2,1,0:T(8,128)} %get-tuple-element.29), channel_id=1, source_target_pairs={{1,0},{2,1},{3,2},{0,3},{5,4},{6,5},{7,6},{4,7},{9,8},{10,9},{11,1... | collective-permute-start | bytes 1327112 | tf_op jit(solution)/shard_map/ppermute | solution.py:677
  6.4 19.5 %collective-permute-start = (f32[2,3,48,384]{3,2,1,0:T(8,128)}, f32[2,3,48,384]{3,2,1,0:T(8,128)}, u32[]{:S(2)}, u32[]{:S(2)}) collective-permute-start(f32[2,3,48,384]{3,2,1,0:T(8,128)} %get-tuple-element.30), channel_id=1, source_target_pairs={{0,1},{1,2},{2,3},{3,0},{4,5},{5,6},{6,7},{7,4},{8,9},{9,10},{10,1... | collective-permute-start | bytes 1327112 | tf_op jit(solution)/shard_map/ppermute | solution.py:676
  6.4 1.2 copy-start.4
  7.6 2.3 %copy-start.9 = (s32[2]{0:T(128)S(1)}, s32[2]{0:T(128)}, u32[]{:S(2)}) copy-start(s32[2]{0:T(128)} %own_offset_ref.1) | copy-start | bytes 28
  9.9 18.1 %copy-start.2 = (bf16[384,1152]{1,0:T(8,128)(2,1)S(1)}, bf16[384,1152]{1,0:T(8,128)(2,1)}, u32[]{:S(2)}) copy-start(bf16[384,1152]{1,0:T(8,128)(2,1)} %constant.67.clone.analysis_ref) | copy-start | bytes 2654212
  9.9 18.1 %copy-start.5 = (bf16[1152,384]{1,0:T(8,128)(2,1)S(1)}, bf16[1152,384]{1,0:T(8,128)(2,1)}, u32[]{:S(2)}) copy-start(bf16[1152,384]{1,0:T(8,128)(2,1)} %constant.65.clone.synthesis_ref) | copy-start | bytes 2654212
  9.9 18.1 %copy-start.7 = (s32[384,128]{1,0:T(8,128)S(1)}, s32[384,128]{1,0:T(8,128)}, u32[]{:S(2)}) copy-start(s32[384,128]{1,0:T(8,128)} %constant.68.clone.mode_ref) | copy-start | bytes 589828
  26.0 40.6 %collective-permute-start.2 = (f32[9,192,128]{2,1,0:T(8,128)}, f32[9,192,128]{2,1,0:T(8,128)}, u32[]{:S(2)}, u32[]{:S(2)}) collective-permute-start(f32[9,192,128]{2,1,0:T(8,128)} %get-tuple-element.18.own_ref), channel_id=1, source_target_pairs={{0,2},{1,3},{2,0},{3,1},{4,6},{5,7},{6,4},{7,5},{8,10},{9,11},{10,... | collective-permute-start | bytes 2654216 | tf_op jit(solution)/shard_map/ppermute | solution.py:748
  26.1 58.9 %collective-permute-start.3 = (f32[584,384]{1,0:T(8,128)}, f32[584,384]{1,0:T(8,128)}, u32[]{:S(2)}, u32[]{:S(2)}) collective-permute-start(f32[584,384]{1,0:T(8,128)} %get-tuple-element.25), channel_id=1, source_target_pairs={{0,16},{16,0},{1,17},{17,1},{2,18},{18,2},{3,19},{19,3},{4,20},{20... | collective-permute-start | bytes 2691080 | tf_op jit(solution)/shard_map/ppermute | solution.py:25
  33.4 45.3 %all-to-all-start = ((f32[16,9,24,128]{3,2,1,0:T(8,128)}), f32[16,9,24,128]{3,2,1,0:T(8,128)S(1)}, u32[]{:S(2)}, u32[]{:S(2)}) async-start(f32[16,9,24,128]{3,2,1,0:T(8,128)} %phase_a_first.1), calls=%async_computation | async-start | bytes 3538944 | tf_op jit(solution)/shard_map/all_to_all | solution.py:727
  85.0 48.8 %copy-start.3 = (bf16[384,1152]{1,0:T(8,128)(2,1)S(1)}, bf16[384,1152]{1,0:T(8,128)(2,1)}, u32[]{:S(2)}) copy-start(bf16[384,1152]{1,0:T(8,128)(2,1)} %constant.67.clone.analysis_ref) | copy-start | bytes 2654212
  85.0 48.8 %copy-start.6 = (bf16[384,1152]{1,0:T(8,128)(2,1)S(1)}, bf16[384,1152]{1,0:T(8,128)(2,1)}, u32[]{:S(2)}) copy-start(bf16[384,1152]{1,0:T(8,128)(2,1)} %constant.66.clone.synthesis_ref) | copy-start | bytes 2654212
  85.0 48.8 %copy-start.8 = (s32[384,128]{1,0:T(8,128)S(1)}, s32[384,128]{1,0:T(8,128)}, u32[]{:S(2)}) copy-start(s32[384,128]{1,0:T(8,128)} %constant.68.clone.mode_ref) | copy-start | bytes 589828
  173.8 46.4 %copy-start.1 = (f32[2,3,4,48,384]{4,3,2,1,0:T(8,128)S(1)}, f32[2,3,4,48,384]{4,3,2,1,0:T(8,128)}, u32[]{:S(2)}) copy-start(f32[2,3,4,48,384]{4,3,2,1,0:T(8,128)} %start_ref.3) | copy-start | bytes 5308420

commit v5 on v4

--- a/solution.py
+++ b/solution.py
@@ -193,18 +193,26 @@
     return [block for group in zip(*blocks) for block in group] + full[whole:]
 
 
-def physical_to_spectral(physical, profile, analysis):
+def lane_moves():
+    lane = np.arange(128)
+    moves = np.zeros((128, 256), np.float32)
+    above = lane // 16 * 16 + (lane + 1) % 16
+    below = lane // 16 * 16 + (lane + 15) % 16
+    np.add.at(moves, (above, lane), 1.0)
+    np.add.at(moves, (below, lane), -1.0)
+    whole = lane[:96]
+    moves[64 + whole % 32, 128 + whole] = 1.0
+    return np.concatenate([moves, moves], axis=0).astype(ml_dtypes.bfloat16)
+
+
+def physical_to_spectral(physical, profile, analysis, moves):
     lane = lane_index(physical[0])
-    z = lane & 15
     forcing = []
     for tile in range(3):
         field = physical[tile]
-        above = jnp.where(z < 15, pltpu.roll(field, 127, 1), pltpu.roll(field, 15, 1))
-        below = jnp.where(z > 0, pltpu.roll(field, 1, 1), pltpu.roll(field, 113, 1))
-        speed = jnp.where(lane < 32, pltpu.roll(field, 64, 1), pltpu.roll(field, 96, 1))
-        speed = jnp.where(lane < 64, speed, field)
-        speed = jnp.where(lane < 96, speed, physical[2])
-        forcing.append(field - 0.4 * (profile[tile : tile + 1] + speed) * (above - below))
+        moved = product(jnp.concatenate(halves(field), axis=1), moves, (1, 0))
+        speed = jnp.where(lane < 96, moved[:, 128:], physical[2])
+        forcing.append(field - 0.4 * (profile[tile : tile + 1] + speed) * moved[:, :128])
     forcing = jnp.concatenate(forcing, axis=1)
     top, rest = halves(forcing)
     return product(analysis, jnp.concatenate([top, rest, top], axis=0), (1, 0))
@@ -216,6 +224,18 @@
     for tile in range(3):
         block = jnp.where(kept, spectral[:, tile * 128 : (tile + 1) * 128], 0.0)
         out_ref[:, tile] = block.reshape(members, width, 128)
+
+
+def pack_halos(start_ref, last_ref, leading_ref, sems):
+    planes = start_ref.shape[2]
+    copies = [
+        pltpu.make_async_copy(start_ref.at[:, :, planes - 1], last_ref, sems.at[0]),
+        pltpu.make_async_copy(start_ref.at[:, :, 0], leading_ref, sems.at[1]),
+    ]
+    for copy in copies:
+        copy.start()
+    for copy in copies:
+        copy.wait()
 
 
 def synthesized(rows, synthesis):
@@ -282,6 +302,7 @@
     analysis_ref,
     mode_ref,
     profile_ref,
+    moves_ref,
     out_ref,
     held_ref,
     physical_ref,
@@ -315,7 +336,9 @@
 
     def finish(group):
         physical = [physical_ref[group % 2, :, tile * 128 : (tile + 1) * 128] for tile in range(3)]
-        spectral = physical_to_spectral(physical, profile_ref[group], analysis_ref[...])
+        spectral = physical_to_spectral(
+            physical, profile_ref[group], analysis_ref[...], moves_ref[...]
+        )
         write_spectral(spectral, count_ref, mode_ref, out_ref)
 
     for step in range(pairs // 2 + 1):
@@ -673,8 +696,18 @@
     params = pltpu.CompilerParams(vmem_limit_bytes=VMEM_LIMIT)
     up = [(i, (i + 1) % ax_places) for i in range(ax_places)]
     down = [(j, i) for i, j in up]
-    before = lax.ppermute(start_states[:, :, axial_rows - 1], "ax", up)
-    after = lax.ppermute(start_states[:, :, 0], "ax", down)
+    halo = jax.ShapeDtypeStruct((groups, components, radial_rows, columns), jnp.float32)
+    with jax.named_scope("pack_halos"):
+        last, leading = pl.pallas_call(
+            pack_halos,
+            in_specs=[pl.BlockSpec(memory_space=pltpu.HBM)],
+            out_specs=whole_blocks(2),
+            out_shape=[halo, halo],
+            scratch_shapes=[pltpu.SemaphoreType.DMA((2,))],
+            compiler_params=params,
+        )(in_place(start_states))
+    before = lax.ppermute(last, "ax", up)
+    after = lax.ppermute(leading, "ax", down)
 
     share = seg * rad_places + rad
     place = jnp.stack([share, half, seg]).astype(jnp.int32)
@@ -710,7 +743,6 @@
     own_radius = ((rad * radial_rows + jnp.arange(radial_rows)).astype(jnp.float32) + 0.5) / radii
     own_profile = jnp.broadcast_to((1.0 - own_radius * own_radius)[:, None], (radial_rows, 128))
 
-    following = passed_along(first_start, "seg", -1)
     synthesis_natural, synthesis, analysis = (
         jnp.asarray(table) for table in (synthesis_natural, synthesis, analysis)
     )
@@ -791,6 +823,8 @@
                 flops=FLOPS, bytes_accessed=16 * own_modes * radii * radii, transcendentals=0
             ),
         )(place, dense_inverse, other_inverse)
+    spectral, first_start = lax.optimization_barrier((spectral, first_start))
+    following = passed_along(first_start, "seg", -1)
     lines = exchanged(spectral)
     with jax.named_scope("phase_b_first"):
         solved = pl.pallas_call(
@@ -809,8 +843,7 @@
             grid=(tiles // 3 + 1,),
             in_specs=[
                 pl.BlockSpec(memory_space=pltpu.SMEM),
-                *whole_blocks(4),
-                *whole_blocks(1),
+                *whole_blocks(6),
             ],
             out_specs=pl.BlockSpec(
                 wire_spec.block_shape, lambda g: (0, jnp.maximum(g - 1, 0), 0, 0)
@@ -821,7 +854,7 @@
                 pltpu.VMEM((2, columns, 3 * 128), jnp.float32),
             ],
             compiler_params=params,
-        )(mode_count, state, synthesis, analysis, mode_rows, profile)
+        )(mode_count, state, synthesis, analysis, mode_rows, profile, jnp.asarray(lane_moves()))
     lines = exchanged(spectral)
     with jax.named_scope("phase_b_last"):
         ending = pl.pallas_call(

time: 224 us -> 219 us (0.978)
  waiting for transfers between devices: 48.4 us -> 45.9 us
where the time goes in v5:
time: 219 us
  blocking collectives  120 us (55%)
  waiting for transfers between devices  45.9 us (21%)
  Pallas kernels  37.3 us (17%)
  starting transfers between devices  12.8 us (6%)
  local copies, waits for them, and re-layouts  2.23 us (1%)
    all_to_all x1, blocking collectives, half_body(): state = lax.all_to_all(solved, MESH_AXES, 0, 0, tiled=True)  47.8 us
    all_to_all x1, blocking collectives, half_body(): ending = lax.all_to_all(ending, MESH_AXES, 0, 0, tiled=True)  46.4 us
    ppermute x1, waiting for transfers between devices, half_body(): other_inverse = lax.ppermute(dense_inverse, 'ax', mirror)  25.9 us
    all_to_all x1, blocking collectives, exchanged(): lax.all_to_all(value, MESH_AXES, 0, 0, axis_index_groups=half_groups, til...  25.6 us
    ppermute x1, waiting for transfers between devices, half_body(): after = lax.ppermute(leading, 'ax', down)  8.98 us
    all_to_all x1, waiting for transfers between devices, exchanged(): lax.all_to_all(value, MESH_AXES, 0, 0, axis_index_groups=half_groups, til...  8.33 us
    pallas_call x1, Pallas kernels, half_body(): pl.pallas_call(later_phase_a, grid=(tiles // 3 + 1,), in_specs=[pl.BlockS...  6.63 us
    all_to_all x1, starting transfers between devices, exchanged(): lax.all_to_all(value, MESH_AXES, 0, 0, axis_index_groups=half_groups, til...  6.38 us
  transfers between devices with their start and end apart: 5, of which 4 were waited for; matrix products, arithmetic and copies ran while one was open for 0% of the time, Pallas kernels for 9%

profile of v5, /device:TPU:1, one launch (start us, length us, event | category | flops | bytes accessed | tf_op | source)
XLA Modules:
  0.0 219.0 jit_solution(13954843388874916500)
XLA Ops:
  0.0 0.0 copy-start.12
  0.0 2.2 %pack_halos.1 = (f32[2,3,48,384]{3,2,1,0:T(8,128)}, f32[2,3,48,384]{3,2,1,0:T(8,128)}) custom-call(f32[2,3,4,48,384]{4,3,2,1,0:T(8,128)} %start_ref.5), custom_call_target="tpu_custom_call" | custom-call | tf_op jit(solution)/shard_map/pack_halos/pallas_call | solution.py:701
  2.2 2.2 collective-permute-start
  4.4 2.1 collective-permute-start.1
  6.5 0.0 copy-done.12
  6.5 0.0 copy-done
  6.5 0.0 copy-start.4
  6.5 1.2 copy-done.4
  7.7 0.0 copy-start.10
  7.7 2.2 own_physical.1.own_ref
  9.9 0.1 pad_add_fusion.place_ref
  10.0 0.0 copy-done.10
  10.0 0.0 copy-start.2
  10.0 0.0 copy-start.5
  10.0 3.0 %pack_sent.1 = (f32[9,192,128]{2,1,0:T(8,128)}, f32[584,384]{1,0:T(8,128)S(1)}) custom-call(s32[3]{0:T(128)S(1)} %pad_add_fusion.place_ref, s32[2]{0:T(128)S(1)} %copy-done.10, f32[48,192,192]{2,1,0:T(8,128)} %inverse_ref.1, f32[2,3,4,48,384]{4,3,2,1,0:T(8,128)} %start_ref.5), custom_call_target="tpu_custom_call" | custom-call | tf_op jit(solution)/shard_map/pack_sent/pallas_call | solution.py:716
  13.0 0.0 copy-start.11
  13.1 0.9 copy-done.11
  14.0 2.7 %collective-permute-done.before_ref = f32[2,3,48,384]{3,2,1,0:T(8,128)} collective-permute-done((f32[2,3,48,384]{3,2,1,0:T(8,128)}, f32[2,3,48,384]{3,2,1,0:T(8,128)}, u32[]{:S(2)}, u32[]{:S(2)}) %collective-permute-start) | collective-permute-done | bytes 442400 | tf_op jit(solution)/shard_map/ppermute | solution.py:709
  16.7 9.0 %collective-permute-done.1.after_ref = f32[2,3,48,384]{3,2,1,0:T(8,128)} collective-permute-done((f32[2,3,48,384]{3,2,1,0:T(8,128)}, f32[2,3,48,384]{3,2,1,0:T(8,128)}, u32[]{:S(2)}, u32[]{:S(2)}) %collective-permute-start.1) | collective-permute-done | bytes 442400 | tf_op jit(solution)/shard_map/ppermute | solution.py:710
  25.7 0.1 broadcast_in_dim.2.profile_ref
  25.7 0.8 collective-permute-start.2
  27.2 0.0 copy-done.2
  27.2 0.0 copy-done.5
  27.2 0.0 copy-done.7
  27.2 5.3 %phase_a_first.1 = f32[16,9,24,128]{3,2,1,0:T(8,128)} custom-call(s32[1]{0:T(128)S(6)} %copy.11.count_ref, f32[2,3,48,384]{3,2,1,0:T(8,128)} %collective-permute-done.before_ref, f32[2,3,4,48,384]{4,3,2,1,0:T(8,128)S(1)} %own_physical.1.own_ref, f32[2,3,48,384]{3,2,1,0:T(8,128)} %collective-permute-done.1.after_ref, bf16[1152,384]{1,0:T(8,128)(2,1)S(1)} %copy-done.5, ...), custom_call_target="tpu_custom_call" | custom-call | tf_op jit(solution)/shard_map/phase_a_first/pallas_call | solution.py:782
  32.5 6.4 %all-to-all-start = ((f32[16,9,24,128]{3,2,1,0:T(8,128)}), f32[16,9,24,128]{3,2,1,0:T(8,128)S(1)}, u32[]{:S(2)}, u32[]{:S(2)}) async-start(f32[16,9,24,128]{3,2,1,0:T(8,128)} %phase_a_first.1), calls=%async_computation | async-start | bytes 3538944 | tf_op jit(solution)/shard_map/all_to_all | solution.py:759
  38.9 1.4 collective-permute-start.3
  40.3 25.9 %collective-permute-done.2.other_ref = f32[9,192,128]{2,1,0:T(8,128)} collective-permute-done((f32[9,192,128]{2,1,0:T(8,128)}, f32[9,192,128]{2,1,0:T(8,128)}, u32[]{:S(2)}, u32[]{:S(2)}) %collective-permute-start.2) | collective-permute-done | bytes 884768 | tf_op jit(solution)/shard_map/ppermute | solution.py:780
  66.3 3.4 %ordered_inverse.1 = (bf16[12,192,192]{2,1,0:T(8,128)(2,1)}, bf16[12,192,192]{2,1,0:T(8,128)(2,1)}) custom-call(s32[3]{0:T(128)S(1)} %pad_add_fusion.place_ref, f32[9,192,128]{2,1,0:T(8,128)} %get-tuple-element.24.own_ref, f32[9,192,128]{2,1,0:T(8,128)} %collective-permute-done.2.other_ref), custom_call_target="tpu_custom_call" | custom-call | flops 40000000000 | bytes 3538944 | tf_op jit(solution)/shard_map/ordered_inverse/pallas_call | solution.py:816
  69.6 8.3 %all-to-all-done.wire_ref = f32[16,9,24,128]{3,2,1,0:T(8,128)S(1)} async-done(((f32[16,9,24,128]{3,2,1,0:T(8,128)}), f32[16,9,24,128]{3,2,1,0:T(8,128)S(1)}, u32[]{:S(2)}, u32[]{:S(2)}) %all-to-all-start) | async-done | bytes 1769504 | tf_op jit(solution)/shard_map/all_to_all | solution.py:759
  78.0 6.3 %phase_b_first.1 = f32[32,14,8,128]{3,2,1,0:T(8,128)S(1)} custom-call(bf16[12,192,192]{2,1,0:T(8,128)(2,1)} %get-tuple-element.25.top_hbm, bf16[12,192,192]{2,1,0:T(8,128)(2,1)} %get-tuple-element.26.rest_hbm, f32[16,9,24,128]{3,2,1,0:T(8,128)S(1)} %all-to-all-done.wire_ref), custom_call_target="tpu_custom_call" | custom-call | tf_op jit(solution)/shard_map/phase_b_first/pallas_call | solution.py:830
  84.3 0.0 copy-start.3
  84.3 0.0 copy-start.6
  84.3 0.0 copy-start.8
  84.3 0.0 copy-start.9
  84.3 0.0 collective-permute-done.3.other_offset_ref.following_ref
  84.3 47.8 %all_to_all.20.wire_ref = f32[32,14,8,128]{3,2,1,0:T(8,128)S(1)} all-to-all(f32[32,14,8,128]{3,2,1,0:T(8,128)S(1)} %phase_b_first.1), channel_id=1, replica_groups=mesh['seg'=2,'rad'=4,'ax'=4] {'seg','rad','ax'}, dimensions={0} | all-to-all | bytes 3670016 | tf_op jit(solution)/shard_map/all_to_all | solution.py:839
  132.1 0.0 copy-done.3
  132.1 0.0 copy-done.6
  132.1 0.0 copy-done.8
  132.1 0.0 copy-done.9
  132.1 6.6 %phase_a_later.1 = f32[16,9,24,128]{3,2,1,0:T(8,128)S(1)} custom-call(s32[1]{0:T(128)S(6)} %copy.11.count_ref, f32[32,14,8,128]{3,2,1,0:T(8,128)S(1)} %all_to_all.20.wire_ref, bf16[384,1152]{1,0:T(8,128)(2,1)S(1)} %copy-done.6, bf16[384,1152]{1,0:T(8,128)(2,1)S(1)} %copy-done.3, s32[384,128]{1,0:T(8,128)S(1)} %copy-done.8, ...), custom_call_target="tpu_custom_call" | custom-call | tf_op jit(solution)/shard_map/phase_a_later/pallas_call | solution.py:841
  138.8 25.6 %all_to_all.21.wire_ref = f32[16,9,24,128]{3,2,1,0:T(8,128)S(1)} all-to-all(f32[16,9,24,128]{3,2,1,0:T(8,128)S(1)} %phase_a_later.1), channel_id=1, replica_groups={{0,1,4,5,8,9,12,13,16,17,20,21,24,25,28,29},{2,3,6,7,10,11,14,15,18,19,..., dimensions={0} | all-to-all | bytes 3538944 | tf_op jit(solution)/shard_map/all_to_all | solution.py:759
  164.4 6.0 %phase_b_last.1 = f32[32,14,8,128]{3,2,1,0:T(8,128)S(1)} custom-call(s32[3]{0:T(128)S(1)} %pad_add_fusion.place_ref, s32[2]{0:T(128)S(1)} %copy-done.10, f32[584,384]{1,0:T(8,128)S(1)} %collective-permute-done.3.other_offset_ref.following_ref, bf16[12,192,192]{2,1,0:T(8,128)(2,1)} %get-tuple-element.25.top_hbm, ...), custom_call_target="tpu_custom_call" | custom-call | tf_op jit(solution)/shard_map/phase_b_last/pallas_call | solution.py:860
  170.4 0.0 copy-start.1
  170.4 46.4 %all_to_all.22.wire_ref = f32[32,14,8,128]{3,2,1,0:T(8,128)S(1)} all-to-all(f32[32,14,8,128]{3,2,1,0:T(8,128)S(1)} %phase_b_last.1), channel_id=1, replica_groups=mesh['seg'=2,'rad'=4,'ax'=4] {'seg','rad','ax'}, dimensions={0} | all-to-all | bytes 3670016 | tf_op jit(solution)/shard_map/all_to_all | solution.py:872
  216.8 0.0 copy-done.1
  216.8 2.1 residual_end.1
  (5 shorter events, 0.0 us)
Async XLA Ops:
  0.0 6.5 %copy-start.12 = (s32[9,128]{1,0:T(8,128)S(1)}, s32[9,128]{1,0:T(8,128)}, u32[]{:S(2)}) copy-start(s32[9,128]{1,0:T(8,128)} %constant.66.clone) | copy-start | bytes 13828
  0.0 6.5 %copy-start = (f32[2,3,4,48,384]{4,3,2,1,0:T(8,128)S(1)}, f32[2,3,4,48,384]{4,3,2,1,0:T(8,128)}, u32[]{:S(2)}) copy-start(f32[2,3,4,48,384]{4,3,2,1,0:T(8,128)} %start_ref.5) | copy-start | bytes 5308420
  2.2 14.5 %collective-permute-start = (f32[2,3,48,384]{3,2,1,0:T(8,128)}, f32[2,3,48,384]{3,2,1,0:T(8,128)}, u32[]{:S(2)}, u32[]{:S(2)}) collective-permute-start(f32[2,3,48,384]{3,2,1,0:T(8,128)} %get-tuple-element.21), channel_id=1, source_target_pairs={{0,1},{1,2},{2,3},{3,0},{4,5},{5,6},{6,7},{7,4},{8,9},{9,10},{10,1... | collective-permute-start | bytes 1327112 | tf_op jit(solution)/shard_map/ppermute | solution.py:709
  4.4 21.3 %collective-permute-start.1 = (f32[2,3,48,384]{3,2,1,0:T(8,128)}, f32[2,3,48,384]{3,2,1,0:T(8,128)}, u32[]{:S(2)}, u32[]{:S(2)}) collective-permute-start(f32[2,3,48,384]{3,2,1,0:T(8,128)} %get-tuple-element.22), channel_id=1, source_target_pairs={{1,0},{2,1},{3,2},{0,3},{5,4},{6,5},{7,6},{4,7},{9,8},{10,9},{11,1... | collective-permute-start | bytes 1327112 | tf_op jit(solution)/shard_map/ppermute | solution.py:710
  6.5 1.2 copy-start.4
  7.7 2.3 %copy-start.10 = (s32[2]{0:T(128)S(1)}, s32[2]{0:T(128)}, u32[]{:S(2)}) copy-start(s32[2]{0:T(128)} %own_offset_ref.1) | copy-start | bytes 28
  10.0 17.2 %copy-start.2 = (bf16[384,1152]{1,0:T(8,128)(2,1)S(1)}, bf16[384,1152]{1,0:T(8,128)(2,1)}, u32[]{:S(2)}) copy-start(bf16[384,1152]{1,0:T(8,128)(2,1)} %constant.69.clone.analysis_ref) | copy-start | bytes 2654212
  10.0 17.2 %copy-start.5 = (bf16[1152,384]{1,0:T(8,128)(2,1)S(1)}, bf16[1152,384]{1,0:T(8,128)(2,1)}, u32[]{:S(2)}) copy-start(bf16[1152,384]{1,0:T(8,128)(2,1)} %constant.67.clone.synthesis_ref) | copy-start | bytes 2654212
  10.0 17.2 %copy-start.7 = (s32[384,128]{1,0:T(8,128)S(1)}, s32[384,128]{1,0:T(8,128)}, u32[]{:S(2)}) copy-start(s32[384,128]{1,0:T(8,128)} %constant.70.clone.mode_ref) | copy-start | bytes 589828
  13.0 0.9 copy-start.11
  25.7 40.5 %collective-permute-start.2 = (f32[9,192,128]{2,1,0:T(8,128)}, f32[9,192,128]{2,1,0:T(8,128)}, u32[]{:S(2)}, u32[]{:S(2)}) collective-permute-start(f32[9,192,128]{2,1,0:T(8,128)} %get-tuple-element.24.own_ref), channel_id=1, source_target_pairs={{0,2},{1,3},{2,0},{3,1},{4,6},{5,7},{6,4},{7,5},{8,10},{9,11},{10,... | collective-permute-start | bytes 2654216 | tf_op jit(solution)/shard_map/ppermute | solution.py:780
  32.5 45.4 %all-to-all-start = ((f32[16,9,24,128]{3,2,1,0:T(8,128)}), f32[16,9,24,128]{3,2,1,0:T(8,128)S(1)}, u32[]{:S(2)}, u32[]{:S(2)}) async-start(f32[16,9,24,128]{3,2,1,0:T(8,128)} %phase_a_first.1), calls=%async_computation | async-start | bytes 3538944 | tf_op jit(solution)/shard_map/all_to_all | solution.py:759
  38.9 45.4 %collective-permute-start.3 = (f32[584,384]{1,0:T(8,128)}, f32[584,384]{1,0:T(8,128)S(1)}, u32[]{:S(2)}, u32[]{:S(2)}) collective-permute-start(f32[584,384]{1,0:T(8,128)} %copy-done.11), channel_id=1, source_target_pairs={{0,16},{16,0},{1,17},{17,1},{2,18},{18,2},{3,19},{19,3},{4,20},{20... | collective-permute-start | bytes 2691080 | tf_op jit(solution)/shard_map/ppermute | solution.py:25
  84.3 47.8 %copy-start.3 = (bf16[384,1152]{1,0:T(8,128)(2,1)S(1)}, bf16[384,1152]{1,0:T(8,128)(2,1)}, u32[]{:S(2)}) copy-start(bf16[384,1152]{1,0:T(8,128)(2,1)} %constant.69.clone.analysis_ref) | copy-start | bytes 2654212
  84.3 47.8 %copy-start.6 = (bf16[384,1152]{1,0:T(8,128)(2,1)S(1)}, bf16[384,1152]{1,0:T(8,128)(2,1)}, u32[]{:S(2)}) copy-start(bf16[384,1152]{1,0:T(8,128)(2,1)} %constant.68.clone.synthesis_ref) | copy-start | bytes 2654212
  84.3 47.8 %copy-start.8 = (s32[384,128]{1,0:T(8,128)S(1)}, s32[384,128]{1,0:T(8,128)}, u32[]{:S(2)}) copy-start(s32[384,128]{1,0:T(8,128)} %constant.70.clone.mode_ref) | copy-start | bytes 589828
  84.3 47.8 %copy-start.9 = (bf16[256,256]{1,0:T(8,128)(2,1)S(1)}, bf16[256,256]{1,0:T(8,128)(2,1)}, u32[]{:S(2)}) copy-start(bf16[256,256]{1,0:T(8,128)(2,1)} %constant.71.clone.moves_ref) | copy-start | bytes 393220
  170.4 46.4 %copy-start.1 = (f32[2,3,4,48,384]{4,3,2,1,0:T(8,128)S(1)}, f32[2,3,4,48,384]{4,3,2,1,0:T(8,128)}, u32[]{:S(2)}) copy-start(f32[2,3,4,48,384]{4,3,2,1,0:T(8,128)} %start_ref.5) | copy-start | bytes 5308420

commit v6 on v5

--- a/solution.py
+++ b/solution.py
@@ -12,7 +12,7 @@
 
 STEPS = 2
 MESH_AXES = ("seg", "rad", "ax")
-UNROLL = [12, 2, 16, 2, 8, 4, 16, 6]
+UNROLL = [12, 12, 16, 16, 8, 32, 16, 6]
 VMEM_LIMIT = 24 * 1024 * 1024
 FLOPS = 40_000_000_000
 
@@ -353,18 +353,25 @@
                 finish(step - 1)
 
 
-def unpack_quads(wire_ref, held_ref, peers):
+def quad_moves():
+    moves = np.zeros((4, 128, 4, 128), np.float32)
+    for source in range(4):
+        for lane in range(96):
+            block, two, segment, one, z = (
+                lane // 32,
+                lane // 16 % 2,
+                lane // 8 % 2,
+                lane // 4 % 2,
+                lane % 4,
+            )
+            target = block * 32 + source // 2 * 16 + segment * 8 + source % 2 * 4 + z
+            moves[source, lane, 2 * two + one, target] = 1.0
+    return moves.reshape(512, 512).astype(ml_dtypes.bfloat16)
+
+
+def unpack_quads(wire_ref, moves_ref, held_ref, peers):
     members, tiles, width, ignored = wire_ref.shape
     seg_places, rad_places, ignored = peers
-    lane = lax.broadcasted_iota(jnp.int32, (4 * width, 128), 1)
-    sixteen, four = lane & 16 == 0, lane & 4 == 0
-
-    def swapped(mask, step, left, right):
-        return (
-            jnp.where(mask, left, pltpu.roll(right, step, 1)),
-            jnp.where(mask, pltpu.roll(left, 128 - step, 1), right),
-        )
-
     groups = tiles // 3
 
     @pl.loop(0, rad_places * groups, unroll=UNROLL[1])
@@ -376,17 +383,18 @@
             for tile in range(3)
         ]
         quads = gathered(waves)
-        one, two, three, last = (
+        lines = [
             jnp.concatenate([quad[at : at + width] for quad in quads], axis=0)
             for at in range(0, 4 * width, width)
-        )
-        one, three = swapped(sixteen, 16, one, three)
-        two, last = swapped(sixteen, 16, two, last)
-        radii = swapped(four, 4, one, two) + swapped(four, 4, three, last)
-        for place, block in enumerate(radii):
+        ]
+        top, rest = halves(jnp.concatenate(lines, axis=1))
+        radii = product(top, moves_ref[...], (1, 0)) + product(rest, moves_ref[...], (1, 0))
+        for place in range(4):
             for quad in range(4):
                 at = pl.multiple_of((index * 16 + 4 * quad + place) * width, 8)
-                held_ref[pl.ds(at, width), :] = block[quad * width : (quad + 1) * width]
+                held_ref[pl.ds(at, width), :] = radii[
+                    quad * width : (quad + 1) * width, place * 128 : (place + 1) * 128
+                ]
 
 
 def first_radius(member, own):
@@ -486,13 +494,27 @@
 
 
 def phase_b(
-    peers, top_hbm, rest_hbm, wire_ref, out_ref, held_ref, solved_ref, top_ref, rest_ref, sems
+    peers,
+    top_hbm,
+    rest_hbm,
+    moves_hbm,
+    wire_ref,
+    out_ref,
+    held_ref,
+    solved_ref,
+    moves_ref,
+    top_ref,
+    rest_ref,
+    sems,
 ):
     members, tiles, width, ignored = wire_ref.shape
     radii = top_ref.shape[1]
     ax_places = peers[2]
+    first = pltpu.make_async_copy(moves_hbm, moves_ref, sems.at[2])
+    first.start()
     copies = inverse_copies(top_hbm, rest_hbm, top_ref, rest_ref, sems)
-    unpack_quads(wire_ref, held_ref, peers)
+    first.wait()
+    unpack_quads(wire_ref, moves_ref, held_ref, peers)
     for copy in copies:
         copy.wait()
 
@@ -811,7 +833,7 @@
     matrices = jax.ShapeDtypeStruct((2 * own_modes, radii, radii), jnp.bfloat16)
     in_hbm = [pl.BlockSpec(memory_space=pltpu.HBM)] * 2
     inverse_scratch = [pltpu.VMEM(matrices.shape, matrices.dtype)] * 2
-    inverse_scratch += [pltpu.SemaphoreType.DMA((2,))]
+    inverse_scratch += [pltpu.SemaphoreType.DMA((3,))]
     with jax.named_scope("ordered_inverse"):
         inverse = pl.pallas_call(
             ordered_inverse,
@@ -826,15 +848,16 @@
     spectral, first_start = lax.optimization_barrier((spectral, first_start))
     following = passed_along(first_start, "seg", -1)
     lines = exchanged(spectral)
+    moves = jnp.asarray(quad_moves())
     with jax.named_scope("phase_b_first"):
         solved = pl.pallas_call(
             functools.partial(phase_b, peers),
-            in_specs=in_hbm + whole_blocks(1),
+            in_specs=in_hbm + [pl.BlockSpec(memory_space=pltpu.HBM)] + whole_blocks(1),
             out_specs=pl.BlockSpec(memory_space=pltpu.VMEM),
             out_shape=spread_wire,
-            scratch_shapes=[held, held] + inverse_scratch,
+            scratch_shapes=[held, held, pltpu.VMEM(moves.shape, moves.dtype)] + inverse_scratch,
             compiler_params=params,
-        )(*map(in_place, inverse), lines)
+        )(*map(in_place, (*inverse, moves)), lines)
     solved, following = lax.optimization_barrier((solved, following))
     state = lax.all_to_all(solved, MESH_AXES, 0, 0, tiled=True)
     with jax.named_scope("phase_a_later"):

time: 219 us -> 218 us (level)
  no operation moved by 1% of the time
where the time goes in v6:
time: 218 us; the launch traced here: 217 us
  blocking collectives  120 us (55%)
  waiting for transfers between devices  45.9 us (21%)
  Pallas kernels  35.5 us (16%)
  starting transfers between devices  12.8 us (6%)
  local copies, waits for them, and re-layouts  2.23 us (1%)
    all_to_all x1, blocking collectives, half_body(): state = lax.all_to_all(solved, MESH_AXES, 0, 0, tiled=True)  47.8 us
    all_to_all x1, blocking collectives, half_body(): ending = lax.all_to_all(ending, MESH_AXES, 0, 0, tiled=True)  46.4 us
    ppermute x1, waiting for transfers between devices, half_body(): other_inverse = lax.ppermute(dense_inverse, 'ax', mirror)  25.9 us
    all_to_all x1, blocking collectives, exchanged(): lax.all_to_all(value, MESH_AXES, 0, 0, axis_index_groups=half_groups, til...  25.6 us
    ppermute x1, waiting for transfers between devices, half_body(): after = lax.ppermute(leading, 'ax', down)  8.98 us
    all_to_all x1, waiting for transfers between devices, exchanged(): lax.all_to_all(value, MESH_AXES, 0, 0, axis_index_groups=half_groups, til...  8.33 us
    all_to_all x1, starting transfers between devices, exchanged(): lax.all_to_all(value, MESH_AXES, 0, 0, axis_index_groups=half_groups, til...  6.38 us
    pallas_call x1, Pallas kernels, half_body(): pl.pallas_call(functools.partial(last_phase_b, peers), in_specs=[pl.Block...  6.05 us
  transfers between devices with their start and end apart: 5, of which 4 were waited for; matrix products, arithmetic and copies ran while one was open for 0% of the time, Pallas kernels for 9%

profile of v6, /device:TPU:1, one launch (start us, length us, event | category | flops | bytes accessed | tf_op | source)
XLA Modules:
  0.0 217.2 jit_solution(13447532149838580641)
XLA Ops:
  0.0 0.0 copy-start.12
  0.0 2.2 %pack_halos.1 = (f32[2,3,48,384]{3,2,1,0:T(8,128)}, f32[2,3,48,384]{3,2,1,0:T(8,128)}) custom-call(f32[2,3,4,48,384]{4,3,2,1,0:T(8,128)} %start_ref.5), custom_call_target="tpu_custom_call" | custom-call | tf_op jit(solution)/shard_map/pack_halos/pallas_call | solution.py:723
  2.2 2.2 %collective-permute-start = (f32[2,3,48,384]{3,2,1,0:T(8,128)}, f32[2,3,48,384]{3,2,1,0:T(8,128)}, u32[]{:S(2)}, u32[]{:S(2)}) collective-permute-start(f32[2,3,48,384]{3,2,1,0:T(8,128)} %get-tuple-element.21), channel_id=1, source_target_pairs={{0,1},{1,2},{2,3},{3,0},{4,5},{5,6},{6,7},{7,4},{8,9},{9,10},{10,1... | collective-permute-start | bytes 1327112 | tf_op jit(solution)/shard_map/ppermute | solution.py:731
  4.4 2.1 collective-permute-start.1
  6.5 0.0 copy-done.12
  6.5 0.0 copy-done
  6.5 0.0 copy-start.4
  6.5 1.2 copy-done.4
  7.7 0.0 copy-start.10
  7.7 2.2 %own_physical.1.own_ref = f32[2,3,4,48,384]{4,3,2,1,0:T(8,128)S(1)} custom-call(f32[2,3,4,48,384]{4,3,2,1,0:T(8,128)S(1)} %copy-done, bf16[1152,384]{1,0:T(8,128)(2,1)S(1)} %copy-done.4), custom_call_target="tpu_custom_call" | custom-call | tf_op jit(solution)/shard_map/own_physical/pallas_call | solution.py:791
  9.9 0.1 pad_add_fusion.place_ref
  10.0 0.0 copy-done.10
  10.0 0.0 copy-start.2
  10.0 0.0 copy-start.5
  10.0 3.0 %pack_sent.1 = (f32[9,192,128]{2,1,0:T(8,128)}, f32[584,384]{1,0:T(8,128)S(1)}) custom-call(s32[3]{0:T(128)S(1)} %pad_add_fusion.place_ref, s32[2]{0:T(128)S(1)} %copy-done.10, f32[48,192,192]{2,1,0:T(8,128)} %inverse_ref.1, f32[2,3,4,48,384]{4,3,2,1,0:T(8,128)} %start_ref.5), custom_call_target="tpu_custom_call" | custom-call | tf_op jit(solution)/shard_map/pack_sent/pallas_call | solution.py:738
  13.0 0.0 copy-start.11
  13.1 0.9 copy-done.11
  14.0 2.7 %collective-permute-done.before_ref = f32[2,3,48,384]{3,2,1,0:T(8,128)} collective-permute-done((f32[2,3,48,384]{3,2,1,0:T(8,128)}, f32[2,3,48,384]{3,2,1,0:T(8,128)}, u32[]{:S(2)}, u32[]{:S(2)}) %collective-permute-start) | collective-permute-done | bytes 442400 | tf_op jit(solution)/shard_map/ppermute | solution.py:731
  16.7 9.0 %collective-permute-done.1.after_ref = f32[2,3,48,384]{3,2,1,0:T(8,128)} collective-permute-done((f32[2,3,48,384]{3,2,1,0:T(8,128)}, f32[2,3,48,384]{3,2,1,0:T(8,128)}, u32[]{:S(2)}, u32[]{:S(2)}) %collective-permute-start.1) | collective-permute-done | bytes 442400 | tf_op jit(solution)/shard_map/ppermute | solution.py:732
  25.7 0.1 broadcast_in_dim.2.profile_ref
  25.7 0.8 collective-permute-start.2
  27.2 0.0 copy-done.2
  27.2 0.0 copy-done.5
  27.2 0.0 copy-done.7
  27.2 5.3 %phase_a_first.1 = f32[16,9,24,128]{3,2,1,0:T(8,128)} custom-call(s32[1]{0:T(128)S(6)} %copy.12.count_ref, f32[2,3,48,384]{3,2,1,0:T(8,128)} %collective-permute-done.before_ref, f32[2,3,4,48,384]{4,3,2,1,0:T(8,128)S(1)} %own_physical.1.own_ref, f32[2,3,48,384]{3,2,1,0:T(8,128)} %collective-permute-done.1.after_ref, bf16[1152,384]{1,0:T(8,128)(2,1)S(1)} %copy-done.5, ...), custom_call_target="tpu_custom_call" | custom-call | tf_op jit(solution)/shard_map/phase_a_first/pallas_call | solution.py:804
  32.5 6.4 %all-to-all-start = ((f32[16,9,24,128]{3,2,1,0:T(8,128)}), f32[16,9,24,128]{3,2,1,0:T(8,128)S(1)}, u32[]{:S(2)}, u32[]{:S(2)}) async-start(f32[16,9,24,128]{3,2,1,0:T(8,128)} %phase_a_first.1), calls=%async_computation | async-start | bytes 3538944 | tf_op jit(solution)/shard_map/all_to_all | solution.py:781
  38.9 1.4 collective-permute-start.3
  40.3 25.9 %collective-permute-done.2.other_ref = f32[9,192,128]{2,1,0:T(8,128)} collective-permute-done((f32[9,192,128]{2,1,0:T(8,128)}, f32[9,192,128]{2,1,0:T(8,128)}, u32[]{:S(2)}, u32[]{:S(2)}) %collective-permute-start.2) | collective-permute-done | bytes 884768 | tf_op jit(solution)/shard_map/ppermute | solution.py:802
  66.3 3.4 %ordered_inverse.1 = (bf16[12,192,192]{2,1,0:T(8,128)(2,1)}, bf16[12,192,192]{2,1,0:T(8,128)(2,1)}) custom-call(s32[3]{0:T(128)S(1)} %pad_add_fusion.place_ref, f32[9,192,128]{2,1,0:T(8,128)} %get-tuple-element.24.own_ref, f32[9,192,128]{2,1,0:T(8,128)} %collective-permute-done.2.other_ref), custom_call_target="tpu_custom_call" | custom-call | flops 40000000000 | bytes 3538944 | tf_op jit(solution)/shard_map/ordered_inverse/pallas_call | solution.py:838
  69.6 8.3 %all-to-all-done.wire_ref = f32[16,9,24,128]{3,2,1,0:T(8,128)S(1)} async-done(((f32[16,9,24,128]{3,2,1,0:T(8,128)}), f32[16,9,24,128]{3,2,1,0:T(8,128)S(1)}, u32[]{:S(2)}, u32[]{:S(2)}) %all-to-all-start) | async-done | bytes 1769504 | tf_op jit(solution)/shard_map/all_to_all | solution.py:781
  78.0 5.4 %phase_b_first.1 = f32[32,14,8,128]{3,2,1,0:T(8,128)S(1)} custom-call(bf16[12,192,192]{2,1,0:T(8,128)(2,1)} %get-tuple-element.25.top_hbm, bf16[12,192,192]{2,1,0:T(8,128)(2,1)} %get-tuple-element.26.rest_hbm, bf16[512,512]{1,0:T(8,128)(2,1)} %constant.73.clone.moves_hbm, f32[16,9,24,128]{3,2,1,0:T(8,128)S(1)} %all-to-all-done.wire_ref), custom_call_target="tpu_custom_call" | custom-call | tf_op jit(solution)/shard_map/phase_b_first/pallas_call | solution.py:853
  83.3 0.0 copy-start.3
  83.3 0.0 copy-start.6
  83.3 0.0 copy-start.8
  83.4 0.0 copy-start.9
  83.4 0.0 collective-permute-done.3.other_offset_ref.following_ref
  83.4 47.8 %all_to_all.20.wire_ref = f32[32,14,8,128]{3,2,1,0:T(8,128)S(1)} all-to-all(f32[32,14,8,128]{3,2,1,0:T(8,128)S(1)} %phase_b_first.1), channel_id=1, replica_groups=mesh['seg'=2,'rad'=4,'ax'=4] {'seg','rad','ax'}, dimensions={0} | all-to-all | bytes 3670016 | tf_op jit(solution)/shard_map/all_to_all | solution.py:862
  131.2 0.0 copy-done.3
  131.2 0.0 copy-done.6
  131.2 0.0 copy-done.8
  131.2 0.0 copy-done.9
  131.2 5.8 %phase_a_later.1 = f32[16,9,24,128]{3,2,1,0:T(8,128)S(1)} custom-call(s32[1]{0:T(128)S(6)} %copy.12.count_ref, f32[32,14,8,128]{3,2,1,0:T(8,128)S(1)} %all_to_all.20.wire_ref, bf16[384,1152]{1,0:T(8,128)(2,1)S(1)} %copy-done.6, bf16[384,1152]{1,0:T(8,128)(2,1)S(1)} %copy-done.3, s32[384,128]{1,0:T(8,128)S(1)} %copy-done.8, ...), custom_call_target="tpu_custom_call" | custom-call | tf_op jit(solution)/shard_map/phase_a_later/pallas_call | solution.py:864
  137.0 25.6 %all_to_all.21.wire_ref = f32[16,9,24,128]{3,2,1,0:T(8,128)S(1)} all-to-all(f32[16,9,24,128]{3,2,1,0:T(8,128)S(1)} %phase_a_later.1), channel_id=1, replica_groups={{0,1,4,5,8,9,12,13,16,17,20,21,24,25,28,29},{2,3,6,7,10,11,14,15,18,19,..., dimensions={0} | all-to-all | bytes 3538944 | tf_op jit(solution)/shard_map/all_to_all | solution.py:781
  162.6 6.1 %phase_b_last.1 = f32[32,14,8,128]{3,2,1,0:T(8,128)S(1)} custom-call(s32[3]{0:T(128)S(1)} %pad_add_fusion.place_ref, s32[2]{0:T(128)S(1)} %copy-done.10, f32[584,384]{1,0:T(8,128)S(1)} %collective-permute-done.3.other_offset_ref.following_ref, bf16[12,192,192]{2,1,0:T(8,128)(2,1)} %get-tuple-element.25.top_hbm, ...), custom_call_target="tpu_custom_call" | custom-call | tf_op jit(solution)/shard_map/phase_b_last/pallas_call | solution.py:883
  168.7 0.0 copy-start.1
  168.7 46.4 %all_to_all.22.wire_ref = f32[32,14,8,128]{3,2,1,0:T(8,128)S(1)} all-to-all(f32[32,14,8,128]{3,2,1,0:T(8,128)S(1)} %phase_b_last.1), channel_id=1, replica_groups=mesh['seg'=2,'rad'=4,'ax'=4] {'seg','rad','ax'}, dimensions={0} | all-to-all | bytes 3670016 | tf_op jit(solution)/shard_map/all_to_all | solution.py:895
  215.1 0.0 copy-done.1
  215.1 2.1 residual_end.1
  (5 shorter events, 0.0 us)
Async XLA Ops:
  0.0 6.5 %copy-start.12 = (s32[9,128]{1,0:T(8,128)S(1)}, s32[9,128]{1,0:T(8,128)}, u32[]{:S(2)}) copy-start(s32[9,128]{1,0:T(8,128)} %constant.68.clone) | copy-start | bytes 13828
  0.0 6.5 %copy-start = (f32[2,3,4,48,384]{4,3,2,1,0:T(8,128)S(1)}, f32[2,3,4,48,384]{4,3,2,1,0:T(8,128)}, u32[]{:S(2)}) copy-start(f32[2,3,4,48,384]{4,3,2,1,0:T(8,128)} %start_ref.5) | copy-start | bytes 5308420
  2.2 14.5 %collective-permute-start = (f32[2,3,48,384]{3,2,1,0:T(8,128)}, f32[2,3,48,384]{3,2,1,0:T(8,128)}, u32[]{:S(2)}, u32[]{:S(2)}) collective-permute-start(f32[2,3,48,384]{3,2,1,0:T(8,128)} %get-tuple-element.21), channel_id=1, source_target_pairs={{0,1},{1,2},{2,3},{3,0},{4,5},{5,6},{6,7},{7,4},{8,9},{9,10},{10,1... | collective-permute-start | bytes 1327112 | tf_op jit(solution)/shard_map/ppermute | solution.py:731
  4.4 21.3 %collective-permute-start.1 = (f32[2,3,48,384]{3,2,1,0:T(8,128)}, f32[2,3,48,384]{3,2,1,0:T(8,128)}, u32[]{:S(2)}, u32[]{:S(2)}) collective-permute-start(f32[2,3,48,384]{3,2,1,0:T(8,128)} %get-tuple-element.22), channel_id=1, source_target_pairs={{1,0},{2,1},{3,2},{0,3},{5,4},{6,5},{7,6},{4,7},{9,8},{10,9},{11,1... | collective-permute-start | bytes 1327112 | tf_op jit(solution)/shard_map/ppermute | solution.py:732
  6.5 1.2 copy-start.4
  7.7 2.3 %copy-start.10 = (s32[2]{0:T(128)S(1)}, s32[2]{0:T(128)}, u32[]{:S(2)}) copy-start(s32[2]{0:T(128)} %own_offset_ref.1) | copy-start | bytes 28
  10.0 17.2 %copy-start.2 = (bf16[384,1152]{1,0:T(8,128)(2,1)S(1)}, bf16[384,1152]{1,0:T(8,128)(2,1)}, u32[]{:S(2)}) copy-start(bf16[384,1152]{1,0:T(8,128)(2,1)} %constant.71.clone.analysis_ref) | copy-start | bytes 2654212
  10.0 17.2 %copy-start.5 = (bf16[1152,384]{1,0:T(8,128)(2,1)S(1)}, bf16[1152,384]{1,0:T(8,128)(2,1)}, u32[]{:S(2)}) copy-start(bf16[1152,384]{1,0:T(8,128)(2,1)} %constant.69.clone.synthesis_ref) | copy-start | bytes 2654212
  10.0 17.2 %copy-start.7 = (s32[384,128]{1,0:T(8,128)S(1)}, s32[384,128]{1,0:T(8,128)}, u32[]{:S(2)}) copy-start(s32[384,128]{1,0:T(8,128)} %constant.72.clone.mode_ref) | copy-start | bytes 589828
  13.0 0.9 copy-start.11
  25.7 40.5 %collective-permute-start.2 = (f32[9,192,128]{2,1,0:T(8,128)}, f32[9,192,128]{2,1,0:T(8,128)}, u32[]{:S(2)}, u32[]{:S(2)}) collective-permute-start(f32[9,192,128]{2,1,0:T(8,128)} %get-tuple-element.24.own_ref), channel_id=1, source_target_pairs={{0,2},{1,3},{2,0},{3,1},{4,6},{5,7},{6,4},{7,5},{8,10},{9,11},{10,... | collective-permute-start | bytes 2654216 | tf_op jit(solution)/shard_map/ppermute | solution.py:802
  32.5 45.4 %all-to-all-start = ((f32[16,9,24,128]{3,2,1,0:T(8,128)}), f32[16,9,24,128]{3,2,1,0:T(8,128)S(1)}, u32[]{:S(2)}, u32[]{:S(2)}) async-start(f32[16,9,24,128]{3,2,1,0:T(8,128)} %phase_a_first.1), calls=%async_computation | async-start | bytes 3538944 | tf_op jit(solution)/shard_map/all_to_all | solution.py:781
  38.9 44.4 %collective-permute-start.3 = (f32[584,384]{1,0:T(8,128)}, f32[584,384]{1,0:T(8,128)S(1)}, u32[]{:S(2)}, u32[]{:S(2)}) collective-permute-start(f32[584,384]{1,0:T(8,128)} %copy-done.11), channel_id=1, source_target_pairs={{0,16},{16,0},{1,17},{17,1},{2,18},{18,2},{3,19},{19,3},{4,20},{20... | collective-permute-start | bytes 2691080 | tf_op jit(solution)/shard_map/ppermute | solution.py:25
  83.3 47.8 %copy-start.3 = (bf16[384,1152]{1,0:T(8,128)(2,1)S(1)}, bf16[384,1152]{1,0:T(8,128)(2,1)}, u32[]{:S(2)}) copy-start(bf16[384,1152]{1,0:T(8,128)(2,1)} %constant.71.clone.analysis_ref) | copy-start | bytes 2654212
  83.3 47.8 %copy-start.6 = (bf16[384,1152]{1,0:T(8,128)(2,1)S(1)}, bf16[384,1152]{1,0:T(8,128)(2,1)}, u32[]{:S(2)}) copy-start(bf16[384,1152]{1,0:T(8,128)(2,1)} %constant.70.clone.synthesis_ref) | copy-start | bytes 2654212
  83.3 47.8 %copy-start.8 = (s32[384,128]{1,0:T(8,128)S(1)}, s32[384,128]{1,0:T(8,128)}, u32[]{:S(2)}) copy-start(s32[384,128]{1,0:T(8,128)} %constant.72.clone.mode_ref) | copy-start | bytes 589828
  83.4 47.8 %copy-start.9 = (bf16[256,256]{1,0:T(8,128)(2,1)S(1)}, bf16[256,256]{1,0:T(8,128)(2,1)}, u32[]{:S(2)}) copy-start(bf16[256,256]{1,0:T(8,128)(2,1)} %constant.74.clone.moves_ref) | copy-start | bytes 393220
  168.7 46.4 %copy-start.1 = (f32[2,3,4,48,384]{4,3,2,1,0:T(8,128)S(1)}, f32[2,3,4,48,384]{4,3,2,1,0:T(8,128)}, u32[]{:S(2)}) copy-start(f32[2,3,4,48,384]{4,3,2,1,0:T(8,128)} %start_ref.5) | copy-start | bytes 5308420

commit v7 on v6

--- a/solution.py
+++ b/solution.py
@@ -429,9 +429,9 @@
     copy.start()
     first = pltpu.make_async_copy(start_ref.at[0], start_held_ref, sems.at[1])
     first.start()
-    rows = first_ref.shape[0] - 8
-    for index in range(8):
-        offset = offset_ref[index % offset_ref.shape[0]].astype(jnp.float32)
+    rows = first_ref.shape[0] - 16
+    for index in range(offset_ref.shape[0]):
+        offset = offset_ref[index].astype(jnp.float32)
         first_ref[rows + index : rows + index + 1, :] = jnp.full((1, first_ref.shape[1]), offset)
     copy.wait()
     for index in range(each):
@@ -574,7 +574,7 @@
     planes = 16 // ax_places
     each = radii // rad_places
     half = place_ref[1]
-    rows = other_offset_ref.shape[0] - 8
+    rows = other_offset_ref.shape[0] - 16
     others = [jnp.max(other_offset_ref[rows + i : rows + i + 1, :128]) for i in range(2)]
     other_offset = jnp.where(half == 0, *others).astype(jnp.int32)
     copies = inverse_copies(top_hbm, rest_hbm, top_ref, rest_ref, sems)
@@ -651,7 +651,7 @@
     @pl.loop(0, slots, unroll=UNROLL[7])
     def _(slot):
         component, pair = slot // (planes // 2), lax.rem(slot, planes // 2)
-        ending = held_ref[slot].T
+        ending = held_ref[slot, :columns].T
         for side in range(2):
             plane = 2 * pair + side
             row = pl.multiple_of((component * planes + plane) * each, 8)
@@ -746,7 +746,7 @@
             out_specs=whole_blocks(2),
             out_shape=[
                 jax.ShapeDtypeStruct((own_modes * 3 // 2, radii, 128), jnp.float32),
-                jax.ShapeDtypeStruct((first_rows + 8, columns), jnp.float32),
+                jax.ShapeDtypeStruct((first_rows + 16, columns), jnp.float32),
             ],
             scratch_shapes=[
                 pltpu.VMEM((own_modes, radii, radii), jnp.float32),
@@ -904,7 +904,9 @@
             ],
             out_specs=pl.BlockSpec((1,) + start_states.shape[1:], lambda b: (b, 0, 0, 0, 0)),
             out_shape=jax.ShapeDtypeStruct(start_states.shape, jnp.float32),
-            scratch_shapes=[pltpu.VMEM((components * (axial_rows // 2), columns, 128), jnp.float32)],
+            scratch_shapes=[
+                pltpu.VMEM((components * (axial_rows // 2), columns + 8, 128), jnp.float32)
+            ],
             compiler_params=params,
         )(ending, start_states, following)
 

time: 218 us -> 218 us (level)
  no operation moved by 1% of the time
where the time goes in v7:
time: 218 us; the launch traced here: 217 us
  blocking collectives  120 us (55%)
  waiting for transfers between devices  46 us (21%)
  Pallas kernels  35.5 us (16%)
  starting transfers between devices  12.8 us (6%)
  local copies, waits for them, and re-layouts  2.23 us (1%)
    all_to_all x1, blocking collectives, half_body(): state = lax.all_to_all(solved, MESH_AXES, 0, 0, tiled=True)  47.8 us
    all_to_all x1, blocking collectives, half_body(): ending = lax.all_to_all(ending, MESH_AXES, 0, 0, tiled=True)  46.4 us
    ppermute x1, waiting for transfers between devices, half_body(): other_inverse = lax.ppermute(dense_inverse, 'ax', mirror)  25.9 us
    all_to_all x1, blocking collectives, exchanged(): lax.all_to_all(value, MESH_AXES, 0, 0, axis_index_groups=half_groups, til...  25.6 us
    ppermute x1, waiting for transfers between devices, half_body(): after = lax.ppermute(leading, 'ax', down)  8.98 us
    all_to_all x1, waiting for transfers between devices, exchanged(): lax.all_to_all(value, MESH_AXES, 0, 0, axis_index_groups=half_groups, til...  8.33 us
    all_to_all x1, starting transfers between devices, exchanged(): lax.all_to_all(value, MESH_AXES, 0, 0, axis_index_groups=half_groups, til...  6.38 us
    pallas_call x1, Pallas kernels, half_body(): pl.pallas_call(functools.partial(last_phase_b, peers), in_specs=[pl.Block...  6.06 us
  transfers between devices with their start and end apart: 5, of which 4 were waited for; matrix products, arithmetic and copies ran while one was open for 0% of the time, Pallas kernels for 9%

profile of v7, /device:TPU:1, one launch (start us, length us, event | category | flops | bytes accessed | tf_op | source)
XLA Modules:
  0.0 217.2 jit_solution(3820449672111664906)
XLA Ops:
  0.0 0.0 copy-start.12
  0.0 2.2 %pack_halos.1 = (f32[2,3,48,384]{3,2,1,0:T(8,128)}, f32[2,3,48,384]{3,2,1,0:T(8,128)}) custom-call(f32[2,3,4,48,384]{4,3,2,1,0:T(8,128)} %start_ref.5), custom_call_target="tpu_custom_call" | custom-call | tf_op jit(solution)/shard_map/pack_halos/pallas_call | solution.py:723
  2.2 2.2 %collective-permute-start = (f32[2,3,48,384]{3,2,1,0:T(8,128)}, f32[2,3,48,384]{3,2,1,0:T(8,128)}, u32[]{:S(2)}, u32[]{:S(2)}) collective-permute-start(f32[2,3,48,384]{3,2,1,0:T(8,128)} %get-tuple-element.21), channel_id=1, source_target_pairs={{0,1},{1,2},{2,3},{3,0},{4,5},{5,6},{6,7},{7,4},{8,9},{9,10},{10,1... | collective-permute-start | bytes 1327112 | tf_op jit(solution)/shard_map/ppermute | solution.py:731
  4.4 2.1 collective-permute-start.1
  6.5 0.0 copy-done.12
  6.5 0.0 copy-done
  6.5 0.0 copy-start.4
  6.5 1.2 copy-done.4
  7.7 0.0 copy-start.10
  7.7 2.2 %own_physical.1.own_ref = f32[2,3,4,48,384]{4,3,2,1,0:T(8,128)S(1)} custom-call(f32[2,3,4,48,384]{4,3,2,1,0:T(8,128)S(1)} %copy-done, bf16[1152,384]{1,0:T(8,128)(2,1)S(1)} %copy-done.4), custom_call_target="tpu_custom_call" | custom-call | tf_op jit(solution)/shard_map/own_physical/pallas_call | solution.py:791
  9.9 0.1 pad_add_fusion.place_ref
  10.0 0.0 copy-done.10
  10.0 0.0 copy-start.2
  10.0 0.0 copy-start.5
  10.0 3.0 %pack_sent.1 = (f32[9,192,128]{2,1,0:T(8,128)}, f32[592,384]{1,0:T(8,128)S(1)}) custom-call(s32[3]{0:T(128)S(1)} %pad_add_fusion.place_ref, s32[2]{0:T(128)S(1)} %copy-done.10, f32[48,192,192]{2,1,0:T(8,128)} %inverse_ref.1, f32[2,3,4,48,384]{4,3,2,1,0:T(8,128)} %start_ref.5), custom_call_target="tpu_custom_call" | custom-call | tf_op jit(solution)/shard_map/pack_sent/pallas_call | solution.py:738
  13.0 0.0 copy-start.11
  13.0 0.9 copy-done.11
  14.0 2.7 %collective-permute-done.before_ref = f32[2,3,48,384]{3,2,1,0:T(8,128)} collective-permute-done((f32[2,3,48,384]{3,2,1,0:T(8,128)}, f32[2,3,48,384]{3,2,1,0:T(8,128)}, u32[]{:S(2)}, u32[]{:S(2)}) %collective-permute-start) | collective-permute-done | bytes 442400 | tf_op jit(solution)/shard_map/ppermute | solution.py:731
  16.7 9.0 %collective-permute-done.1.after_ref = f32[2,3,48,384]{3,2,1,0:T(8,128)} collective-permute-done((f32[2,3,48,384]{3,2,1,0:T(8,128)}, f32[2,3,48,384]{3,2,1,0:T(8,128)}, u32[]{:S(2)}, u32[]{:S(2)}) %collective-permute-start.1) | collective-permute-done | bytes 442400 | tf_op jit(solution)/shard_map/ppermute | solution.py:732
  25.7 0.1 broadcast_in_dim.2.profile_ref
  25.7 0.8 collective-permute-start.2
  27.2 0.0 copy-done.2
  27.2 0.0 copy-done.5
  27.2 0.0 copy-done.7
  27.2 5.3 %phase_a_first.1 = f32[16,9,24,128]{3,2,1,0:T(8,128)} custom-call(s32[1]{0:T(128)S(6)} %copy.12.count_ref, f32[2,3,48,384]{3,2,1,0:T(8,128)} %collective-permute-done.before_ref, f32[2,3,4,48,384]{4,3,2,1,0:T(8,128)S(1)} %own_physical.1.own_ref, f32[2,3,48,384]{3,2,1,0:T(8,128)} %collective-permute-done.1.after_ref, bf16[1152,384]{1,0:T(8,128)(2,1)S(1)} %copy-done.5, ...), custom_call_target="tpu_custom_call" | custom-call | tf_op jit(solution)/shard_map/phase_a_first/pallas_call | solution.py:804
  32.5 6.4 %all-to-all-start = ((f32[16,9,24,128]{3,2,1,0:T(8,128)}), f32[16,9,24,128]{3,2,1,0:T(8,128)S(1)}, u32[]{:S(2)}, u32[]{:S(2)}) async-start(f32[16,9,24,128]{3,2,1,0:T(8,128)} %phase_a_first.1), calls=%async_computation | async-start | bytes 3538944 | tf_op jit(solution)/shard_map/all_to_all | solution.py:781
  38.9 1.4 collective-permute-start.3
  40.3 25.9 %collective-permute-done.2.other_ref = f32[9,192,128]{2,1,0:T(8,128)} collective-permute-done((f32[9,192,128]{2,1,0:T(8,128)}, f32[9,192,128]{2,1,0:T(8,128)}, u32[]{:S(2)}, u32[]{:S(2)}) %collective-permute-start.2) | collective-permute-done | bytes 884768 | tf_op jit(solution)/shard_map/ppermute | solution.py:802
  66.3 3.4 %ordered_inverse.1 = (bf16[12,192,192]{2,1,0:T(8,128)(2,1)}, bf16[12,192,192]{2,1,0:T(8,128)(2,1)}) custom-call(s32[3]{0:T(128)S(1)} %pad_add_fusion.place_ref, f32[9,192,128]{2,1,0:T(8,128)} %get-tuple-element.24.own_ref, f32[9,192,128]{2,1,0:T(8,128)} %collective-permute-done.2.other_ref), custom_call_target="tpu_custom_call" | custom-call | flops 40000000000 | bytes 3538944 | tf_op jit(solution)/shard_map/ordered_inverse/pallas_call | solution.py:838
  69.6 8.3 %all-to-all-done.wire_ref = f32[16,9,24,128]{3,2,1,0:T(8,128)S(1)} async-done(((f32[16,9,24,128]{3,2,1,0:T(8,128)}), f32[16,9,24,128]{3,2,1,0:T(8,128)S(1)}, u32[]{:S(2)}, u32[]{:S(2)}) %all-to-all-start) | async-done | bytes 1769504 | tf_op jit(solution)/shard_map/all_to_all | solution.py:781
  78.0 5.4 %phase_b_first.1 = f32[32,14,8,128]{3,2,1,0:T(8,128)S(1)} custom-call(bf16[12,192,192]{2,1,0:T(8,128)(2,1)} %get-tuple-element.25.top_hbm, bf16[12,192,192]{2,1,0:T(8,128)(2,1)} %get-tuple-element.26.rest_hbm, bf16[512,512]{1,0:T(8,128)(2,1)} %constant.73.clone.moves_hbm, f32[16,9,24,128]{3,2,1,0:T(8,128)S(1)} %all-to-all-done.wire_ref), custom_call_target="tpu_custom_call" | custom-call | tf_op jit(solution)/shard_map/phase_b_first/pallas_call | solution.py:853
  83.3 0.0 copy-start.3
  83.3 0.0 copy-start.6
  83.3 0.0 copy-start.8
  83.4 0.0 copy-start.9
  83.4 0.0 collective-permute-done.3.other_offset_ref.following_ref
  83.4 47.8 %all_to_all.20.wire_ref = f32[32,14,8,128]{3,2,1,0:T(8,128)S(1)} all-to-all(f32[32,14,8,128]{3,2,1,0:T(8,128)S(1)} %phase_b_first.1), channel_id=1, replica_groups=mesh['seg'=2,'rad'=4,'ax'=4] {'seg','rad','ax'}, dimensions={0} | all-to-all | bytes 3670016 | tf_op jit(solution)/shard_map/all_to_all | solution.py:862
  131.2 0.0 copy-done.3
  131.2 0.0 copy-done.6
  131.2 0.0 copy-done.8
  131.2 0.0 copy-done.9
  131.2 5.8 %phase_a_later.1 = f32[16,9,24,128]{3,2,1,0:T(8,128)S(1)} custom-call(s32[1]{0:T(128)S(6)} %copy.12.count_ref, f32[32,14,8,128]{3,2,1,0:T(8,128)S(1)} %all_to_all.20.wire_ref, bf16[384,1152]{1,0:T(8,128)(2,1)S(1)} %copy-done.6, bf16[384,1152]{1,0:T(8,128)(2,1)S(1)} %copy-done.3, s32[384,128]{1,0:T(8,128)S(1)} %copy-done.8, ...), custom_call_target="tpu_custom_call" | custom-call | tf_op jit(solution)/shard_map/phase_a_later/pallas_call | solution.py:864
  137.0 25.6 %all_to_all.21.wire_ref = f32[16,9,24,128]{3,2,1,0:T(8,128)S(1)} all-to-all(f32[16,9,24,128]{3,2,1,0:T(8,128)S(1)} %phase_a_later.1), channel_id=1, replica_groups={{0,1,4,5,8,9,12,13,16,17,20,21,24,25,28,29},{2,3,6,7,10,11,14,15,18,19,..., dimensions={0} | all-to-all | bytes 3538944 | tf_op jit(solution)/shard_map/all_to_all | solution.py:781
  162.6 6.1 %phase_b_last.1 = f32[32,14,8,128]{3,2,1,0:T(8,128)S(1)} custom-call(s32[3]{0:T(128)S(1)} %pad_add_fusion.place_ref, s32[2]{0:T(128)S(1)} %copy-done.10, f32[592,384]{1,0:T(8,128)S(1)} %collective-permute-done.3.other_offset_ref.following_ref, bf16[12,192,192]{2,1,0:T(8,128)(2,1)} %get-tuple-element.25.top_hbm, ...), custom_call_target="tpu_custom_call" | custom-call | tf_op jit(solution)/shard_map/phase_b_last/pallas_call | solution.py:883
  168.7 0.0 copy-start.1
  168.7 46.4 %all_to_all.22.wire_ref = f32[32,14,8,128]{3,2,1,0:T(8,128)S(1)} all-to-all(f32[32,14,8,128]{3,2,1,0:T(8,128)S(1)} %phase_b_last.1), channel_id=1, replica_groups=mesh['seg'=2,'rad'=4,'ax'=4] {'seg','rad','ax'}, dimensions={0} | all-to-all | bytes 3670016 | tf_op jit(solution)/shard_map/all_to_all | solution.py:895
  215.1 0.0 copy-done.1
  215.1 2.1 residual_end.1
  (5 shorter events, 0.0 us)
Async XLA Ops:
  0.0 6.5 %copy-start.12 = (s32[9,128]{1,0:T(8,128)S(1)}, s32[9,128]{1,0:T(8,128)}, u32[]{:S(2)}) copy-start(s32[9,128]{1,0:T(8,128)} %constant.68.clone) | copy-start | bytes 13828
  0.0 6.5 %copy-start = (f32[2,3,4,48,384]{4,3,2,1,0:T(8,128)S(1)}, f32[2,3,4,48,384]{4,3,2,1,0:T(8,128)}, u32[]{:S(2)}) copy-start(f32[2,3,4,48,384]{4,3,2,1,0:T(8,128)} %start_ref.5) | copy-start | bytes 5308420
  2.2 14.5 %collective-permute-start = (f32[2,3,48,384]{3,2,1,0:T(8,128)}, f32[2,3,48,384]{3,2,1,0:T(8,128)}, u32[]{:S(2)}, u32[]{:S(2)}) collective-permute-start(f32[2,3,48,384]{3,2,1,0:T(8,128)} %get-tuple-element.21), channel_id=1, source_target_pairs={{0,1},{1,2},{2,3},{3,0},{4,5},{5,6},{6,7},{7,4},{8,9},{9,10},{10,1... | collective-permute-start | bytes 1327112 | tf_op jit(solution)/shard_map/ppermute | solution.py:731
  4.4 21.3 %collective-permute-start.1 = (f32[2,3,48,384]{3,2,1,0:T(8,128)}, f32[2,3,48,384]{3,2,1,0:T(8,128)}, u32[]{:S(2)}, u32[]{:S(2)}) collective-permute-start(f32[2,3,48,384]{3,2,1,0:T(8,128)} %get-tuple-element.22), channel_id=1, source_target_pairs={{1,0},{2,1},{3,2},{0,3},{5,4},{6,5},{7,6},{4,7},{9,8},{10,9},{11,1... | collective-permute-start | bytes 1327112 | tf_op jit(solution)/shard_map/ppermute | solution.py:732
  6.5 1.2 copy-start.4
  7.7 2.3 %copy-start.10 = (s32[2]{0:T(128)S(1)}, s32[2]{0:T(128)}, u32[]{:S(2)}) copy-start(s32[2]{0:T(128)} %own_offset_ref.1) | copy-start | bytes 28
  10.0 17.2 %copy-start.2 = (bf16[384,1152]{1,0:T(8,128)(2,1)S(1)}, bf16[384,1152]{1,0:T(8,128)(2,1)}, u32[]{:S(2)}) copy-start(bf16[384,1152]{1,0:T(8,128)(2,1)} %constant.71.clone.analysis_ref) | copy-start | bytes 2654212
  10.0 17.2 %copy-start.5 = (bf16[1152,384]{1,0:T(8,128)(2,1)S(1)}, bf16[1152,384]{1,0:T(8,128)(2,1)}, u32[]{:S(2)}) copy-start(bf16[1152,384]{1,0:T(8,128)(2,1)} %constant.69.clone.synthesis_ref) | copy-start | bytes 2654212
  10.0 17.2 %copy-start.7 = (s32[384,128]{1,0:T(8,128)S(1)}, s32[384,128]{1,0:T(8,128)}, u32[]{:S(2)}) copy-start(s32[384,128]{1,0:T(8,128)} %constant.72.clone.mode_ref) | copy-start | bytes 589828
  13.0 0.9 copy-start.11
  25.7 40.5 %collective-permute-start.2 = (f32[9,192,128]{2,1,0:T(8,128)}, f32[9,192,128]{2,1,0:T(8,128)}, u32[]{:S(2)}, u32[]{:S(2)}) collective-permute-start(f32[9,192,128]{2,1,0:T(8,128)} %get-tuple-element.24.own_ref), channel_id=1, source_target_pairs={{0,2},{1,3},{2,0},{3,1},{4,6},{5,7},{6,4},{7,5},{8,10},{9,11},{10,... | collective-permute-start | bytes 2654216 | tf_op jit(solution)/shard_map/ppermute | solution.py:802
  32.5 45.4 %all-to-all-start = ((f32[16,9,24,128]{3,2,1,0:T(8,128)}), f32[16,9,24,128]{3,2,1,0:T(8,128)S(1)}, u32[]{:S(2)}, u32[]{:S(2)}) async-start(f32[16,9,24,128]{3,2,1,0:T(8,128)} %phase_a_first.1), calls=%async_computation | async-start | bytes 3538944 | tf_op jit(solution)/shard_map/all_to_all | solution.py:781
  38.9 44.4 %collective-permute-start.3 = (f32[592,384]{1,0:T(8,128)}, f32[592,384]{1,0:T(8,128)S(1)}, u32[]{:S(2)}, u32[]{:S(2)}) collective-permute-start(f32[592,384]{1,0:T(8,128)} %copy-done.11), channel_id=1, source_target_pairs={{0,16},{16,0},{1,17},{17,1},{2,18},{18,2},{3,19},{19,3},{4,20},{20... | collective-permute-start | bytes 2727944 | tf_op jit(solution)/shard_map/ppermute | solution.py:25
  83.3 47.8 %copy-start.3 = (bf16[384,1152]{1,0:T(8,128)(2,1)S(1)}, bf16[384,1152]{1,0:T(8,128)(2,1)}, u32[]{:S(2)}) copy-start(bf16[384,1152]{1,0:T(8,128)(2,1)} %constant.71.clone.analysis_ref) | copy-start | bytes 2654212
  83.3 47.8 %copy-start.6 = (bf16[384,1152]{1,0:T(8,128)(2,1)S(1)}, bf16[384,1152]{1,0:T(8,128)(2,1)}, u32[]{:S(2)}) copy-start(bf16[384,1152]{1,0:T(8,128)(2,1)} %constant.70.clone.synthesis_ref) | copy-start | bytes 2654212
  83.3 47.8 %copy-start.8 = (s32[384,128]{1,0:T(8,128)S(1)}, s32[384,128]{1,0:T(8,128)}, u32[]{:S(2)}) copy-start(s32[384,128]{1,0:T(8,128)} %constant.72.clone.mode_ref) | copy-start | bytes 589828
  83.4 47.8 %copy-start.9 = (bf16[256,256]{1,0:T(8,128)(2,1)S(1)}, bf16[256,256]{1,0:T(8,128)(2,1)}, u32[]{:S(2)}) copy-start(bf16[256,256]{1,0:T(8,128)(2,1)} %constant.74.clone.moves_ref) | copy-start | bytes 393220
  168.7 46.4 %copy-start.1 = (f32[2,3,4,48,384]{4,3,2,1,0:T(8,128)S(1)}, f32[2,3,4,48,384]{4,3,2,1,0:T(8,128)}, u32[]{:S(2)}) copy-start(f32[2,3,4,48,384]{4,3,2,1,0:T(8,128)} %start_ref.5) | copy-start | bytes 5308420

commit v8 on v7

--- a/solution.py
+++ b/solution.py
@@ -264,35 +264,54 @@
     groups, components, planes, radii, columns = own_ref.shape
     strips = columns // 128
     count = groups * components
-    sides = [ref[...].reshape(count * radii, columns) for ref in (before_ref, after_ref)]
-    sides = synthesized(sides, synthesis_ref[...]).reshape(2, groups, components, radii, columns)
-    profile = jnp.concatenate([profile_ref[...]] * strips, axis=1)
-    for segment in range(groups):
-        for plane in range(planes):
-            speed = 0.4 * (profile + own_ref[segment, 2, plane])
-            for component in range(components):
-                line = [own_ref[segment, component, i] for i in range(planes)]
-                line = [sides[0, segment, component], *line, sides[1, segment, component]]
-                forcing = line[plane + 1] - speed * (line[plane + 2] - line[plane])
-                first = (component * groups + segment) * radii * planes
-                at = pl.ds(first + plane, radii, stride=planes)
-                for strip in range(strips):
-                    held_ref[strip, at, :] = forcing[:, strip * 128 : (strip + 1) * 128]
     quad = 4 * planes
-    lines = []
-    for strip in range(strips):
-        parts = []
-        for tile in range(3):
-            for four, members in ((tile, range(components)), (3, (tile,))):
-                for component in members:
-                    for at in range(four * quad, (four + 1) * quad, quad // 2):
-                        for segment in range(groups):
-                            row = (component * groups + segment) * radii * planes + at
-                            parts.append(held_ref[strip, row : row + quad // 2, :])
-        lines.append(jnp.concatenate(parts, axis=0))
-    top, rest = halves(jnp.concatenate(lines, axis=1))
-    spectral = product(analysis_ref[...], jnp.concatenate([top, rest, top], axis=1), (1, 1))
-    write_spectral(spectral, count_ref, mode_ref, out_ref)
+
+    def begin(step):
+        sides = [ref[...].reshape(count * radii, columns) for ref in (before_ref, after_ref)]
+        sides = synthesized(sides, synthesis_ref[...])
+        sides = sides.reshape(2, groups, components, radii, columns)
+        profile = jnp.concatenate([profile_ref[...]] * strips, axis=1)
+        for segment in range(groups):
+            for plane in range(planes):
+                speed = 0.4 * (profile + own_ref[segment, 2, plane])
+                for component in range(components):
+                    line = [own_ref[segment, component, i] for i in range(planes)]
+                    line = [sides[0, segment, component], *line, sides[1, segment, component]]
+                    forcing = line[plane + 1] - speed * (line[plane + 2] - line[plane])
+                    first = (component * groups + segment) * radii * planes
+                    at = pl.ds(first + plane, radii, stride=planes)
+                    for strip in range(strips):
+                        held_ref[step % 2, strip, at, :] = forcing[
+                            :, strip * 128 : (strip + 1) * 128
+                        ]
+
+    def finish(step):
+        lines = []
+        for strip in range(strips):
+            parts = []
+            for tile in range(3):
+                for four, members in ((tile, range(components)), (3, (tile,))):
+                    for component in members:
+                        for at in range(four * quad, (four + 1) * quad, quad // 2):
+                            for segment in range(groups):
+                                row = (component * groups + segment) * radii * planes + at
+                                parts.append(
+                                    held_ref[step % 2, strip, row : row + quad // 2, :]
+                                )
+            lines.append(jnp.concatenate(parts, axis=0))
+        top, rest = halves(jnp.concatenate(lines, axis=1))
+        spectral = product(analysis_ref[...], jnp.concatenate([top, rest, top], axis=1), (1, 1))
+        write_spectral(spectral, count_ref, mode_ref, out_ref)
+
+    steps = out_ref.shape[2] // 8
+    for step in range(steps + 1):
+
+        @pl.when(pl.program_id(0) == step)
+        def _(step=step):
+            if step < steps:
+                begin(step)
+            if step > 0:
+                finish(step - 1)
 
 
 def later_phase_a(
@@ -483,7 +502,7 @@
                 jnp.concatenate([m[:96], m[:32], m[96:], m[:32]], axis=0)
                 for m in (matrix_top, matrix_rest)
             )
-            top, rest = halves(state.T)
+            top, rest = (part.T for part in halves(state))
             solved = product(top, matrix_top, (1, 1))
             solved += product(rest, matrix_top, (1, 1)) + product(top, matrix_rest, (1, 1))
         else:
@@ -783,7 +802,9 @@
         )
 
     step = radial_rows // 3
-    halo_spec = pl.BlockSpec((groups, components, step, columns), lambda g: (0, 0, g, 0))
+    late_halo_spec = pl.BlockSpec(
+        (groups, components, step, columns), lambda g: (0, 0, jnp.minimum(g, 2), 0)
+    )
     own_spec = pl.BlockSpec(
         (groups, components, axial_rows, step, columns), lambda g: (0, 0, 0, g, 0)
     )
@@ -803,20 +824,24 @@
     with jax.named_scope("phase_a_first"):
         spectral = pl.pallas_call(
             first_phase_a,
-            grid=(3,),
+            grid=(4,),
             in_specs=[
                 pl.BlockSpec(memory_space=pltpu.SMEM),
-                halo_spec,
-                own_spec,
-                halo_spec,
+                late_halo_spec,
+                pl.BlockSpec(
+                    own_spec.block_shape, lambda g: (0, 0, 0, jnp.minimum(g, 2), 0)
+                ),
+                late_halo_spec,
                 *whole_blocks(3),
-                pl.BlockSpec((step, 128), lambda g: (g, 0)),
+                pl.BlockSpec((step, 128), lambda g: (jnp.minimum(g, 2), 0)),
             ],
-            out_specs=wire_spec,
+            out_specs=pl.BlockSpec(
+                wire_spec.block_shape, lambda g: (0, jnp.maximum(g - 1, 0), 0, 0)
+            ),
             out_shape=pltpu.HBM(wire.shape, wire.dtype),
             scratch_shapes=[
                 pltpu.VMEM(
-                    (columns // 128, groups * components * axial_rows * step, 128), jnp.float32
+                    (2, columns // 128, groups * components * axial_rows * step, 128), jnp.float32
                 )
             ],
             compiler_params=params,

time: 218 us -> 217 us (level)
  no operation moved by 1% of the time
where the time goes in v8:
time: 217 us
  blocking collectives  120 us (55%)
  waiting for transfers between devices  46 us (21%)
  Pallas kernels  35.1 us (16%)
  starting transfers between devices  12.8 us (6%)
  local copies, waits for them, and re-layouts  2.23 us (1%)
    all_to_all x1, blocking collectives, half_body(): state = lax.all_to_all(solved, MESH_AXES, 0, 0, tiled=True)  47.8 us
    all_to_all x1, blocking collectives, half_body(): ending = lax.all_to_all(ending, MESH_AXES, 0, 0, tiled=True)  46.4 us
    ppermute x1, waiting for transfers between devices, half_body(): other_inverse = lax.ppermute(dense_inverse, 'ax', mirror)  26.1 us
    all_to_all x1, blocking collectives, exchanged(): lax.all_to_all(value, MESH_AXES, 0, 0, axis_index_groups=half_groups, til...  25.6 us
    ppermute x1, waiting for transfers between devices, half_body(): after = lax.ppermute(leading, 'ax', down)  8.98 us
    all_to_all x1, waiting for transfers between devices, exchanged(): lax.all_to_all(value, MESH_AXES, 0, 0, axis_index_groups=half_groups, til...  8.14 us
    all_to_all x1, starting transfers between devices, exchanged(): lax.all_to_all(value, MESH_AXES, 0, 0, axis_index_groups=half_groups, til...  6.38 us
    pallas_call x1, Pallas kernels, half_body(): pl.pallas_call(functools.partial(last_phase_b, peers), in_specs=[pl.Block...  5.9 us
  transfers between devices with their start and end apart: 5, of which 4 were waited for; matrix products, arithmetic and copies ran while one was open for 0% of the time, Pallas kernels for 9%

profile of v8, /device:TPU:1, one launch (start us, length us, event | category | flops | bytes accessed | tf_op | source)
XLA Modules:
  0.0 216.8 jit_solution(17809596295302676078)
XLA Ops:
  0.0 0.0 copy-start.12
  0.0 2.2 %pack_halos.1 = (f32[2,3,48,384]{3,2,1,0:T(8,128)}, f32[2,3,48,384]{3,2,1,0:T(8,128)}) custom-call(f32[2,3,4,48,384]{4,3,2,1,0:T(8,128)} %start_ref.5), custom_call_target="tpu_custom_call" | custom-call | tf_op jit(solution)/shard_map/pack_halos/pallas_call | solution.py:742
  2.2 2.2 %collective-permute-start = (f32[2,3,48,384]{3,2,1,0:T(8,128)}, f32[2,3,48,384]{3,2,1,0:T(8,128)}, u32[]{:S(2)}, u32[]{:S(2)}) collective-permute-start(f32[2,3,48,384]{3,2,1,0:T(8,128)} %get-tuple-element.21), channel_id=1, source_target_pairs={{0,1},{1,2},{2,3},{3,0},{4,5},{5,6},{6,7},{7,4},{8,9},{9,10},{10,1... | collective-permute-start | bytes 1327112 | tf_op jit(solution)/shard_map/ppermute | solution.py:750
  4.4 2.1 collective-permute-start.1
  6.5 0.0 copy-done.12
  6.5 0.0 copy-done
  6.5 0.0 copy-start.4
  6.5 1.2 copy-done.4
  7.7 0.0 copy-start.10
  7.7 2.2 %own_physical.1.own_ref = f32[2,3,4,48,384]{4,3,2,1,0:T(8,128)S(1)} custom-call(f32[2,3,4,48,384]{4,3,2,1,0:T(8,128)S(1)} %copy-done, bf16[1152,384]{1,0:T(8,128)(2,1)S(1)} %copy-done.4), custom_call_target="tpu_custom_call" | custom-call | tf_op jit(solution)/shard_map/own_physical/pallas_call | solution.py:812
  9.9 0.1 pad_add_fusion.place_ref
  10.0 0.0 copy-done.10
  10.0 0.0 copy-start.2
  10.0 0.0 copy-start.5
  10.0 3.0 %pack_sent.1 = (f32[9,192,128]{2,1,0:T(8,128)}, f32[592,384]{1,0:T(8,128)S(1)}) custom-call(s32[3]{0:T(128)S(1)} %pad_add_fusion.place_ref, s32[2]{0:T(128)S(1)} %copy-done.10, f32[48,192,192]{2,1,0:T(8,128)} %inverse_ref.1, f32[2,3,4,48,384]{4,3,2,1,0:T(8,128)} %start_ref.5), custom_call_target="tpu_custom_call" | custom-call | tf_op jit(solution)/shard_map/pack_sent/pallas_call | solution.py:757
  13.0 0.0 copy-start.11
  13.0 0.9 copy-done.11
  14.0 2.7 %collective-permute-done.before_ref = f32[2,3,48,384]{3,2,1,0:T(8,128)} collective-permute-done((f32[2,3,48,384]{3,2,1,0:T(8,128)}, f32[2,3,48,384]{3,2,1,0:T(8,128)}, u32[]{:S(2)}, u32[]{:S(2)}) %collective-permute-start) | collective-permute-done | bytes 442400 | tf_op jit(solution)/shard_map/ppermute | solution.py:750
  16.7 9.0 %collective-permute-done.1.after_ref = f32[2,3,48,384]{3,2,1,0:T(8,128)} collective-permute-done((f32[2,3,48,384]{3,2,1,0:T(8,128)}, f32[2,3,48,384]{3,2,1,0:T(8,128)}, u32[]{:S(2)}, u32[]{:S(2)}) %collective-permute-start.1) | collective-permute-done | bytes 442400 | tf_op jit(solution)/shard_map/ppermute | solution.py:751
  25.7 0.1 broadcast_in_dim.2.profile_ref
  25.7 0.8 collective-permute-start.2
  27.2 0.0 copy-done.2
  27.2 0.0 copy-done.5
  27.2 0.0 copy-done.7
  27.2 5.2 %phase_a_first.1 = f32[16,9,24,128]{3,2,1,0:T(8,128)} custom-call(s32[1]{0:T(128)S(6)} %copy.12.count_ref, f32[2,3,48,384]{3,2,1,0:T(8,128)} %collective-permute-done.before_ref, f32[2,3,4,48,384]{4,3,2,1,0:T(8,128)S(1)} %own_physical.1.own_ref, f32[2,3,48,384]{3,2,1,0:T(8,128)} %collective-permute-done.1.after_ref, bf16[1152,384]{1,0:T(8,128)(2,1)S(1)} %copy-done.5, ...), custom_call_target="tpu_custom_call" | custom-call | tf_op jit(solution)/shard_map/phase_a_first/pallas_call | solution.py:825
  32.4 6.4 %all-to-all-start = ((f32[16,9,24,128]{3,2,1,0:T(8,128)}), f32[16,9,24,128]{3,2,1,0:T(8,128)S(1)}, u32[]{:S(2)}, u32[]{:S(2)}) async-start(f32[16,9,24,128]{3,2,1,0:T(8,128)} %phase_a_first.1), calls=%async_computation | async-start | bytes 3538944 | tf_op jit(solution)/shard_map/all_to_all | solution.py:800
  38.7 1.4 collective-permute-start.3
  40.1 26.1 %collective-permute-done.2.other_ref = f32[9,192,128]{2,1,0:T(8,128)} collective-permute-done((f32[9,192,128]{2,1,0:T(8,128)}, f32[9,192,128]{2,1,0:T(8,128)}, u32[]{:S(2)}, u32[]{:S(2)}) %collective-permute-start.2) | collective-permute-done | bytes 884768 | tf_op jit(solution)/shard_map/ppermute | solution.py:823
  66.3 3.4 %ordered_inverse.1 = (bf16[12,192,192]{2,1,0:T(8,128)(2,1)}, bf16[12,192,192]{2,1,0:T(8,128)(2,1)}) custom-call(s32[3]{0:T(128)S(1)} %pad_add_fusion.place_ref, f32[9,192,128]{2,1,0:T(8,128)} %get-tuple-element.24.own_ref, f32[9,192,128]{2,1,0:T(8,128)} %collective-permute-done.2.other_ref), custom_call_target="tpu_custom_call" | custom-call | flops 40000000000 | bytes 3538944 | tf_op jit(solution)/shard_map/ordered_inverse/pallas_call | solution.py:863
  69.6 8.1 %all-to-all-done.wire_ref = f32[16,9,24,128]{3,2,1,0:T(8,128)S(1)} async-done(((f32[16,9,24,128]{3,2,1,0:T(8,128)}), f32[16,9,24,128]{3,2,1,0:T(8,128)S(1)}, u32[]{:S(2)}, u32[]{:S(2)}) %all-to-all-start) | async-done | bytes 1769504 | tf_op jit(solution)/shard_map/all_to_all | solution.py:800
  77.8 5.4 %phase_b_first.1 = f32[32,14,8,128]{3,2,1,0:T(8,128)S(1)} custom-call(bf16[12,192,192]{2,1,0:T(8,128)(2,1)} %get-tuple-element.25.top_hbm, bf16[12,192,192]{2,1,0:T(8,128)(2,1)} %get-tuple-element.26.rest_hbm, bf16[512,512]{1,0:T(8,128)(2,1)} %constant.73.clone.moves_hbm, f32[16,9,24,128]{3,2,1,0:T(8,128)S(1)} %all-to-all-done.wire_ref), custom_call_target="tpu_custom_call" | custom-call | tf_op jit(solution)/shard_map/phase_b_first/pallas_call | solution.py:878
  83.1 0.0 copy-start.3
  83.2 0.0 copy-start.6
  83.2 0.0 copy-start.8
  83.2 0.0 copy-start.9
  83.2 0.0 collective-permute-done.3.other_offset_ref.following_ref
  83.2 47.8 %all_to_all.20.wire_ref = f32[32,14,8,128]{3,2,1,0:T(8,128)S(1)} all-to-all(f32[32,14,8,128]{3,2,1,0:T(8,128)S(1)} %phase_b_first.1), channel_id=1, replica_groups=mesh['seg'=2,'rad'=4,'ax'=4] {'seg','rad','ax'}, dimensions={0} | all-to-all | bytes 3670016 | tf_op jit(solution)/shard_map/all_to_all | solution.py:887
  131.0 0.0 copy-done.3
  131.0 0.0 copy-done.6
  131.0 0.0 copy-done.8
  131.0 0.0 copy-done.9
  131.0 5.8 %phase_a_later.1 = f32[16,9,24,128]{3,2,1,0:T(8,128)S(1)} custom-call(s32[1]{0:T(128)S(6)} %copy.12.count_ref, f32[32,14,8,128]{3,2,1,0:T(8,128)S(1)} %all_to_all.20.wire_ref, bf16[384,1152]{1,0:T(8,128)(2,1)S(1)} %copy-done.6, bf16[384,1152]{1,0:T(8,128)(2,1)S(1)} %copy-done.3, s32[384,128]{1,0:T(8,128)S(1)} %copy-done.8, ...), custom_call_target="tpu_custom_call" | custom-call | tf_op jit(solution)/shard_map/phase_a_later/pallas_call | solution.py:889
  136.8 25.6 %all_to_all.21.wire_ref = f32[16,9,24,128]{3,2,1,0:T(8,128)S(1)} all-to-all(f32[16,9,24,128]{3,2,1,0:T(8,128)S(1)} %phase_a_later.1), channel_id=1, replica_groups={{0,1,4,5,8,9,12,13,16,17,20,21,24,25,28,29},{2,3,6,7,10,11,14,15,18,19,..., dimensions={0} | all-to-all | bytes 3538944 | tf_op jit(solution)/shard_map/all_to_all | solution.py:800
  162.4 5.9 %phase_b_last.1 = f32[32,14,8,128]{3,2,1,0:T(8,128)S(1)} custom-call(s32[3]{0:T(128)S(1)} %pad_add_fusion.place_ref, s32[2]{0:T(128)S(1)} %copy-done.10, f32[592,384]{1,0:T(8,128)S(1)} %collective-permute-done.3.other_offset_ref.following_ref, bf16[12,192,192]{2,1,0:T(8,128)(2,1)} %get-tuple-element.25.top_hbm, ...), custom_call_target="tpu_custom_call" | custom-call | tf_op jit(solution)/shard_map/phase_b_last/pallas_call | solution.py:908
  168.3 0.0 copy-start.1
  168.3 46.4 %all_to_all.22.wire_ref = f32[32,14,8,128]{3,2,1,0:T(8,128)S(1)} all-to-all(f32[32,14,8,128]{3,2,1,0:T(8,128)S(1)} %phase_b_last.1), channel_id=1, replica_groups=mesh['seg'=2,'rad'=4,'ax'=4] {'seg','rad','ax'}, dimensions={0} | all-to-all | bytes 3670016 | tf_op jit(solution)/shard_map/all_to_all | solution.py:920
  214.7 0.0 copy-done.1
  214.7 2.1 residual_end.1
  (5 shorter events, 0.0 us)
Async XLA Ops:
  0.0 6.5 %copy-start.12 = (s32[9,128]{1,0:T(8,128)S(1)}, s32[9,128]{1,0:T(8,128)}, u32[]{:S(2)}) copy-start(s32[9,128]{1,0:T(8,128)} %constant.68.clone) | copy-start | bytes 13828
  0.0 6.5 %copy-start = (f32[2,3,4,48,384]{4,3,2,1,0:T(8,128)S(1)}, f32[2,3,4,48,384]{4,3,2,1,0:T(8,128)}, u32[]{:S(2)}) copy-start(f32[2,3,4,48,384]{4,3,2,1,0:T(8,128)} %start_ref.5) | copy-start | bytes 5308420
  2.2 14.5 %collective-permute-start = (f32[2,3,48,384]{3,2,1,0:T(8,128)}, f32[2,3,48,384]{3,2,1,0:T(8,128)}, u32[]{:S(2)}, u32[]{:S(2)}) collective-permute-start(f32[2,3,48,384]{3,2,1,0:T(8,128)} %get-tuple-element.21), channel_id=1, source_target_pairs={{0,1},{1,2},{2,3},{3,0},{4,5},{5,6},{6,7},{7,4},{8,9},{9,10},{10,1... | collective-permute-start | bytes 1327112 | tf_op jit(solution)/shard_map/ppermute | solution.py:750
  4.4 21.3 %collective-permute-start.1 = (f32[2,3,48,384]{3,2,1,0:T(8,128)}, f32[2,3,48,384]{3,2,1,0:T(8,128)}, u32[]{:S(2)}, u32[]{:S(2)}) collective-permute-start(f32[2,3,48,384]{3,2,1,0:T(8,128)} %get-tuple-element.22), channel_id=1, source_target_pairs={{1,0},{2,1},{3,2},{0,3},{5,4},{6,5},{7,6},{4,7},{9,8},{10,9},{11,1... | collective-permute-start | bytes 1327112 | tf_op jit(solution)/shard_map/ppermute | solution.py:751
  6.5 1.2 copy-start.4
  7.7 2.3 %copy-start.10 = (s32[2]{0:T(128)S(1)}, s32[2]{0:T(128)}, u32[]{:S(2)}) copy-start(s32[2]{0:T(128)} %own_offset_ref.1) | copy-start | bytes 28
  10.0 17.2 %copy-start.2 = (bf16[384,1152]{1,0:T(8,128)(2,1)S(1)}, bf16[384,1152]{1,0:T(8,128)(2,1)}, u32[]{:S(2)}) copy-start(bf16[384,1152]{1,0:T(8,128)(2,1)} %constant.71.clone.analysis_ref) | copy-start | bytes 2654212
  10.0 17.2 %copy-start.5 = (bf16[1152,384]{1,0:T(8,128)(2,1)S(1)}, bf16[1152,384]{1,0:T(8,128)(2,1)}, u32[]{:S(2)}) copy-start(bf16[1152,384]{1,0:T(8,128)(2,1)} %constant.69.clone.synthesis_ref) | copy-start | bytes 2654212
  10.0 17.2 %copy-start.7 = (s32[384,128]{1,0:T(8,128)S(1)}, s32[384,128]{1,0:T(8,128)}, u32[]{:S(2)}) copy-start(s32[384,128]{1,0:T(8,128)} %constant.72.clone.mode_ref) | copy-start | bytes 589828
  13.0 0.9 copy-start.11
  25.7 40.5 %collective-permute-start.2 = (f32[9,192,128]{2,1,0:T(8,128)}, f32[9,192,128]{2,1,0:T(8,128)}, u32[]{:S(2)}, u32[]{:S(2)}) collective-permute-start(f32[9,192,128]{2,1,0:T(8,128)} %get-tuple-element.24.own_ref), channel_id=1, source_target_pairs={{0,2},{1,3},{2,0},{3,1},{4,6},{5,7},{6,4},{7,5},{8,10},{9,11},{10,... | collective-permute-start | bytes 2654216 | tf_op jit(solution)/shard_map/ppermute | solution.py:823
  32.4 45.4 %all-to-all-start = ((f32[16,9,24,128]{3,2,1,0:T(8,128)}), f32[16,9,24,128]{3,2,1,0:T(8,128)S(1)}, u32[]{:S(2)}, u32[]{:S(2)}) async-start(f32[16,9,24,128]{3,2,1,0:T(8,128)} %phase_a_first.1), calls=%async_computation | async-start | bytes 3538944 | tf_op jit(solution)/shard_map/all_to_all | solution.py:800
  38.7 44.5 %collective-permute-start.3 = (f32[592,384]{1,0:T(8,128)}, f32[592,384]{1,0:T(8,128)S(1)}, u32[]{:S(2)}, u32[]{:S(2)}) collective-permute-start(f32[592,384]{1,0:T(8,128)} %copy-done.11), channel_id=1, source_target_pairs={{0,16},{16,0},{1,17},{17,1},{2,18},{18,2},{3,19},{19,3},{4,20},{20... | collective-permute-start | bytes 2727944 | tf_op jit(solution)/shard_map/ppermute | solution.py:25
  83.1 47.8 %copy-start.3 = (bf16[384,1152]{1,0:T(8,128)(2,1)S(1)}, bf16[384,1152]{1,0:T(8,128)(2,1)}, u32[]{:S(2)}) copy-start(bf16[384,1152]{1,0:T(8,128)(2,1)} %constant.71.clone.analysis_ref) | copy-start | bytes 2654212
  83.2 47.8 %copy-start.6 = (bf16[384,1152]{1,0:T(8,128)(2,1)S(1)}, bf16[384,1152]{1,0:T(8,128)(2,1)}, u32[]{:S(2)}) copy-start(bf16[384,1152]{1,0:T(8,128)(2,1)} %constant.70.clone.synthesis_ref) | copy-start | bytes 2654212
  83.2 47.8 %copy-start.8 = (s32[384,128]{1,0:T(8,128)S(1)}, s32[384,128]{1,0:T(8,128)}, u32[]{:S(2)}) copy-start(s32[384,128]{1,0:T(8,128)} %constant.72.clone.mode_ref) | copy-start | bytes 589828
  83.2 47.8 %copy-start.9 = (bf16[256,256]{1,0:T(8,128)(2,1)S(1)}, bf16[256,256]{1,0:T(8,128)(2,1)}, u32[]{:S(2)}) copy-start(bf16[256,256]{1,0:T(8,128)(2,1)} %constant.74.clone.moves_ref) | copy-start | bytes 393220
  168.3 46.4 %copy-start.1 = (f32[2,3,4,48,384]{4,3,2,1,0:T(8,128)S(1)}, f32[2,3,4,48,384]{4,3,2,1,0:T(8,128)}, u32[]{:S(2)}) copy-start(f32[2,3,4,48,384]{4,3,2,1,0:T(8,128)} %start_ref.5) | copy-start | bytes 5308420

commit v9 on v8

--- a/solution.py
+++ b/solution.py
@@ -262,26 +262,29 @@
     held_ref,
 ):
     groups, components, planes, radii, columns = own_ref.shape
+    steps = 3
+    radii //= steps
     strips = columns // 128
     count = groups * components
     quad = 4 * planes
 
     def begin(step):
-        sides = [ref[...].reshape(count * radii, columns) for ref in (before_ref, after_ref)]
+        at = slice(step * radii, (step + 1) * radii)
+        sides = [ref[:, :, at].reshape(count * radii, columns) for ref in (before_ref, after_ref)]
         sides = synthesized(sides, synthesis_ref[...])
         sides = sides.reshape(2, groups, components, radii, columns)
-        profile = jnp.concatenate([profile_ref[...]] * strips, axis=1)
+        profile = jnp.concatenate([profile_ref[at]] * strips, axis=1)
         for segment in range(groups):
             for plane in range(planes):
-                speed = 0.4 * (profile + own_ref[segment, 2, plane])
+                speed = 0.4 * (profile + own_ref[segment, 2, plane, at])
                 for component in range(components):
-                    line = [own_ref[segment, component, i] for i in range(planes)]
+                    line = [own_ref[segment, component, i, at] for i in range(planes)]
                     line = [sides[0, segment, component], *line, sides[1, segment, component]]
                     forcing = line[plane + 1] - speed * (line[plane + 2] - line[plane])
                     first = (component * groups + segment) * radii * planes
-                    at = pl.ds(first + plane, radii, stride=planes)
+                    spot = pl.ds(first + plane, radii, stride=planes)
                     for strip in range(strips):
-                        held_ref[step % 2, strip, at, :] = forcing[
+                        held_ref[step % 2, strip, spot, :] = forcing[
                             :, strip * 128 : (strip + 1) * 128
                         ]
 
@@ -303,7 +306,6 @@
         spectral = product(analysis_ref[...], jnp.concatenate([top, rest, top], axis=1), (1, 1))
         write_spectral(spectral, count_ref, mode_ref, out_ref)
 
-    steps = out_ref.shape[2] // 8
     for step in range(steps + 1):
 
         @pl.when(pl.program_id(0) == step)
@@ -802,9 +804,6 @@
         )
 
     step = radial_rows // 3
-    late_halo_spec = pl.BlockSpec(
-        (groups, components, step, columns), lambda g: (0, 0, jnp.minimum(g, 2), 0)
-    )
     own_spec = pl.BlockSpec(
         (groups, components, axial_rows, step, columns), lambda g: (0, 0, 0, g, 0)
     )
@@ -827,13 +826,7 @@
             grid=(4,),
             in_specs=[
                 pl.BlockSpec(memory_space=pltpu.SMEM),
-                late_halo_spec,
-                pl.BlockSpec(
-                    own_spec.block_shape, lambda g: (0, 0, 0, jnp.minimum(g, 2), 0)
-                ),
-                late_halo_spec,
-                *whole_blocks(3),
-                pl.BlockSpec((step, 128), lambda g: (jnp.minimum(g, 2), 0)),
+                *whole_blocks(7),
             ],
             out_specs=pl.BlockSpec(
                 wire_spec.block_shape, lambda g: (0, jnp.maximum(g - 1, 0), 0, 0)

time: 217 us -> 217 us (level)
  no operation moved by 1% of the time
where the time goes in v9:
time: 217 us
  blocking collectives  120 us (55%)
  waiting for transfers between devices  46 us (21%)
  Pallas kernels  35.3 us (16%)
  starting transfers between devices  12.8 us (6%)
  local copies, waits for them, and re-layouts  2.23 us (1%)
    all_to_all x1, blocking collectives, half_body(): state = lax.all_to_all(solved, MESH_AXES, 0, 0, tiled=True)  47.8 us
    all_to_all x1, blocking collectives, half_body(): ending = lax.all_to_all(ending, MESH_AXES, 0, 0, tiled=True)  46.4 us
    ppermute x1, waiting for transfers between devices, half_body(): other_inverse = lax.ppermute(dense_inverse, 'ax', mirror)  26 us
    all_to_all x1, blocking collectives, exchanged(): lax.all_to_all(value, MESH_AXES, 0, 0, axis_index_groups=half_groups, til...  25.6 us
    ppermute x1, waiting for transfers between devices, half_body(): after = lax.ppermute(leading, 'ax', down)  8.98 us
    all_to_all x1, waiting for transfers between devices, exchanged(): lax.all_to_all(value, MESH_AXES, 0, 0, axis_index_groups=half_groups, til...  8.26 us
    all_to_all x1, starting transfers between devices, exchanged(): lax.all_to_all(value, MESH_AXES, 0, 0, axis_index_groups=half_groups, til...  6.38 us
    pallas_call x1, Pallas kernels, half_body(): pl.pallas_call(functools.partial(last_phase_b, peers), in_specs=[pl.Block...  5.91 us
  transfers between devices with their start and end apart: 5, of which 4 were waited for; matrix products, arithmetic and copies ran while one was open for 0% of the time, Pallas kernels for 9%

profile of v9, /device:TPU:1, one launch (start us, length us, event | category | flops | bytes accessed | tf_op | source)
XLA Modules:
  0.0 217.0 jit_solution(9019288537697918123)
XLA Ops:
  0.0 0.0 copy-start.12
  0.0 2.2 %pack_halos.1 = (f32[2,3,48,384]{3,2,1,0:T(8,128)}, f32[2,3,48,384]{3,2,1,0:T(8,128)}) custom-call(f32[2,3,4,48,384]{4,3,2,1,0:T(8,128)} %start_ref.5), custom_call_target="tpu_custom_call" | custom-call | tf_op jit(solution)/shard_map/pack_halos/pallas_call | solution.py:744
  2.2 2.2 %collective-permute-start = (f32[2,3,48,384]{3,2,1,0:T(8,128)}, f32[2,3,48,384]{3,2,1,0:T(8,128)}, u32[]{:S(2)}, u32[]{:S(2)}) collective-permute-start(f32[2,3,48,384]{3,2,1,0:T(8,128)} %get-tuple-element.21), channel_id=1, source_target_pairs={{0,1},{1,2},{2,3},{3,0},{4,5},{5,6},{6,7},{7,4},{8,9},{9,10},{10,1... | collective-permute-start | bytes 1327112 | tf_op jit(solution)/shard_map/ppermute | solution.py:752
  4.4 2.1 collective-permute-start.1
  6.5 0.0 copy-done.12
  6.5 0.0 copy-done
  6.5 0.0 copy-start.4
  6.5 1.2 copy-done.4
  7.7 0.0 copy-start.10
  7.7 2.2 %own_physical.1.own_ref = f32[2,3,4,48,384]{4,3,2,1,0:T(8,128)S(1)} custom-call(f32[2,3,4,48,384]{4,3,2,1,0:T(8,128)S(1)} %copy-done, bf16[1152,384]{1,0:T(8,128)(2,1)S(1)} %copy-done.4), custom_call_target="tpu_custom_call" | custom-call | tf_op jit(solution)/shard_map/own_physical/pallas_call | solution.py:811
  9.9 0.1 pad_add_fusion.place_ref
  10.0 0.0 copy-done.10
  10.0 0.0 copy-start.2
  10.0 0.0 copy-start.5
  10.0 3.0 %pack_sent.1 = (f32[9,192,128]{2,1,0:T(8,128)}, f32[592,384]{1,0:T(8,128)S(1)}) custom-call(s32[3]{0:T(128)S(1)} %pad_add_fusion.place_ref, s32[2]{0:T(128)S(1)} %copy-done.10, f32[48,192,192]{2,1,0:T(8,128)} %inverse_ref.1, f32[2,3,4,48,384]{4,3,2,1,0:T(8,128)} %start_ref.5), custom_call_target="tpu_custom_call" | custom-call | tf_op jit(solution)/shard_map/pack_sent/pallas_call | solution.py:759
  13.0 0.0 copy-start.11
  13.0 0.9 copy-done.11
  14.0 2.7 %collective-permute-done.before_ref = f32[2,3,48,384]{3,2,1,0:T(8,128)} collective-permute-done((f32[2,3,48,384]{3,2,1,0:T(8,128)}, f32[2,3,48,384]{3,2,1,0:T(8,128)}, u32[]{:S(2)}, u32[]{:S(2)}) %collective-permute-start) | collective-permute-done | bytes 442400 | tf_op jit(solution)/shard_map/ppermute | solution.py:752
  16.7 9.0 %collective-permute-done.1.after_ref = f32[2,3,48,384]{3,2,1,0:T(8,128)} collective-permute-done((f32[2,3,48,384]{3,2,1,0:T(8,128)}, f32[2,3,48,384]{3,2,1,0:T(8,128)}, u32[]{:S(2)}, u32[]{:S(2)}) %collective-permute-start.1) | collective-permute-done | bytes 442400 | tf_op jit(solution)/shard_map/ppermute | solution.py:753
  25.7 0.1 broadcast_in_dim.2.profile_ref
  25.7 0.8 collective-permute-start.2
  27.2 0.0 copy-done.2
  27.2 0.0 copy-done.5
  27.2 0.0 copy-done.7
  27.2 5.3 %phase_a_first.1 = f32[16,9,24,128]{3,2,1,0:T(8,128)} custom-call(s32[1]{0:T(128)S(6)} %copy.12.count_ref, f32[2,3,48,384]{3,2,1,0:T(8,128)} %collective-permute-done.before_ref, f32[2,3,4,48,384]{4,3,2,1,0:T(8,128)S(1)} %own_physical.1.own_ref, f32[2,3,48,384]{3,2,1,0:T(8,128)} %collective-permute-done.1.after_ref, bf16[1152,384]{1,0:T(8,128)(2,1)S(1)} %copy-done.5, ...), custom_call_target="tpu_custom_call" | custom-call | tf_op jit(solution)/shard_map/phase_a_first/pallas_call | solution.py:824
  32.5 6.4 %all-to-all-start = ((f32[16,9,24,128]{3,2,1,0:T(8,128)}), f32[16,9,24,128]{3,2,1,0:T(8,128)S(1)}, u32[]{:S(2)}, u32[]{:S(2)}) async-start(f32[16,9,24,128]{3,2,1,0:T(8,128)} %phase_a_first.1), calls=%async_computation | async-start | bytes 3538944 | tf_op jit(solution)/shard_map/all_to_all | solution.py:802
  38.9 1.4 collective-permute-start.3
  40.2 26.0 %collective-permute-done.2.other_ref = f32[9,192,128]{2,1,0:T(8,128)} collective-permute-done((f32[9,192,128]{2,1,0:T(8,128)}, f32[9,192,128]{2,1,0:T(8,128)}, u32[]{:S(2)}, u32[]{:S(2)}) %collective-permute-start.2) | collective-permute-done | bytes 884768 | tf_op jit(solution)/shard_map/ppermute | solution.py:822
  66.3 3.4 %ordered_inverse.1 = (bf16[12,192,192]{2,1,0:T(8,128)(2,1)}, bf16[12,192,192]{2,1,0:T(8,128)(2,1)}) custom-call(s32[3]{0:T(128)S(1)} %pad_add_fusion.place_ref, f32[9,192,128]{2,1,0:T(8,128)} %get-tuple-element.24.own_ref, f32[9,192,128]{2,1,0:T(8,128)} %collective-permute-done.2.other_ref), custom_call_target="tpu_custom_call" | custom-call | flops 40000000000 | bytes 3538944 | tf_op jit(solution)/shard_map/ordered_inverse/pallas_call | solution.py:856
  69.6 8.3 %all-to-all-done.wire_ref = f32[16,9,24,128]{3,2,1,0:T(8,128)S(1)} async-done(((f32[16,9,24,128]{3,2,1,0:T(8,128)}), f32[16,9,24,128]{3,2,1,0:T(8,128)S(1)}, u32[]{:S(2)}, u32[]{:S(2)}) %all-to-all-start) | async-done | bytes 1769504 | tf_op jit(solution)/shard_map/all_to_all | solution.py:802
  77.9 5.4 %phase_b_first.1 = f32[32,14,8,128]{3,2,1,0:T(8,128)S(1)} custom-call(bf16[12,192,192]{2,1,0:T(8,128)(2,1)} %get-tuple-element.25.top_hbm, bf16[12,192,192]{2,1,0:T(8,128)(2,1)} %get-tuple-element.26.rest_hbm, bf16[512,512]{1,0:T(8,128)(2,1)} %constant.73.clone.moves_hbm, f32[16,9,24,128]{3,2,1,0:T(8,128)S(1)} %all-to-all-done.wire_ref), custom_call_target="tpu_custom_call" | custom-call | tf_op jit(solution)/shard_map/phase_b_first/pallas_call | solution.py:871
  83.3 0.0 copy-start.3
  83.3 0.0 copy-start.6
  83.3 0.0 copy-start.8
  83.3 0.0 copy-start.9
  83.3 0.0 collective-permute-done.3.other_offset_ref.following_ref
  83.3 47.8 %all_to_all.20.wire_ref = f32[32,14,8,128]{3,2,1,0:T(8,128)S(1)} all-to-all(f32[32,14,8,128]{3,2,1,0:T(8,128)S(1)} %phase_b_first.1), channel_id=1, replica_groups=mesh['seg'=2,'rad'=4,'ax'=4] {'seg','rad','ax'}, dimensions={0} | all-to-all | bytes 3670016 | tf_op jit(solution)/shard_map/all_to_all | solution.py:880
  131.1 0.0 copy-done.3
  131.1 0.0 copy-done.6
  131.1 0.0 copy-done.8
  131.1 0.0 copy-done.9
  131.1 5.8 %phase_a_later.1 = f32[16,9,24,128]{3,2,1,0:T(8,128)S(1)} custom-call(s32[1]{0:T(128)S(6)} %copy.12.count_ref, f32[32,14,8,128]{3,2,1,0:T(8,128)S(1)} %all_to_all.20.wire_ref, bf16[384,1152]{1,0:T(8,128)(2,1)S(1)} %copy-done.6, bf16[384,1152]{1,0:T(8,128)(2,1)S(1)} %copy-done.3, s32[384,128]{1,0:T(8,128)S(1)} %copy-done.8, ...), custom_call_target="tpu_custom_call" | custom-call | tf_op jit(solution)/shard_map/phase_a_later/pallas_call | solution.py:882
  136.9 25.6 %all_to_all.21.wire_ref = f32[16,9,24,128]{3,2,1,0:T(8,128)S(1)} all-to-all(f32[16,9,24,128]{3,2,1,0:T(8,128)S(1)} %phase_a_later.1), channel_id=1, replica_groups={{0,1,4,5,8,9,12,13,16,17,20,21,24,25,28,29},{2,3,6,7,10,11,14,15,18,19,..., dimensions={0} | all-to-all | bytes 3538944 | tf_op jit(solution)/shard_map/all_to_all | solution.py:802
  162.5 5.9 %phase_b_last.1 = f32[32,14,8,128]{3,2,1,0:T(8,128)S(1)} custom-call(s32[3]{0:T(128)S(1)} %pad_add_fusion.place_ref, s32[2]{0:T(128)S(1)} %copy-done.10, f32[592,384]{1,0:T(8,128)S(1)} %collective-permute-done.3.other_offset_ref.following_ref, bf16[12,192,192]{2,1,0:T(8,128)(2,1)} %get-tuple-element.25.top_hbm, ...), custom_call_target="tpu_custom_call" | custom-call | tf_op jit(solution)/shard_map/phase_b_last/pallas_call | solution.py:901
  168.5 0.0 copy-start.1
  168.5 46.4 %all_to_all.22.wire_ref = f32[32,14,8,128]{3,2,1,0:T(8,128)S(1)} all-to-all(f32[32,14,8,128]{3,2,1,0:T(8,128)S(1)} %phase_b_last.1), channel_id=1, replica_groups=mesh['seg'=2,'rad'=4,'ax'=4] {'seg','rad','ax'}, dimensions={0} | all-to-all | bytes 3670016 | tf_op jit(solution)/shard_map/all_to_all | solution.py:913
  214.8 0.0 copy-done.1
  214.8 2.1 residual_end.1
  (5 shorter events, 0.0 us)
Async XLA Ops:
  0.0 6.5 %copy-start.12 = (s32[9,128]{1,0:T(8,128)S(1)}, s32[9,128]{1,0:T(8,128)}, u32[]{:S(2)}) copy-start(s32[9,128]{1,0:T(8,128)} %constant.68.clone) | copy-start | bytes 13828
  0.0 6.5 %copy-start = (f32[2,3,4,48,384]{4,3,2,1,0:T(8,128)S(1)}, f32[2,3,4,48,384]{4,3,2,1,0:T(8,128)}, u32[]{:S(2)}) copy-start(f32[2,3,4,48,384]{4,3,2,1,0:T(8,128)} %start_ref.5) | copy-start | bytes 5308420
  2.2 14.5 %collective-permute-start = (f32[2,3,48,384]{3,2,1,0:T(8,128)}, f32[2,3,48,384]{3,2,1,0:T(8,128)}, u32[]{:S(2)}, u32[]{:S(2)}) collective-permute-start(f32[2,3,48,384]{3,2,1,0:T(8,128)} %get-tuple-element.21), channel_id=1, source_target_pairs={{0,1},{1,2},{2,3},{3,0},{4,5},{5,6},{6,7},{7,4},{8,9},{9,10},{10,1... | collective-permute-start | bytes 1327112 | tf_op jit(solution)/shard_map/ppermute | solution.py:752
  4.4 21.3 %collective-permute-start.1 = (f32[2,3,48,384]{3,2,1,0:T(8,128)}, f32[2,3,48,384]{3,2,1,0:T(8,128)}, u32[]{:S(2)}, u32[]{:S(2)}) collective-permute-start(f32[2,3,48,384]{3,2,1,0:T(8,128)} %get-tuple-element.22), channel_id=1, source_target_pairs={{1,0},{2,1},{3,2},{0,3},{5,4},{6,5},{7,6},{4,7},{9,8},{10,9},{11,1... | collective-permute-start | bytes 1327112 | tf_op jit(solution)/shard_map/ppermute | solution.py:753
  6.5 1.2 copy-start.4
  7.7 2.3 %copy-start.10 = (s32[2]{0:T(128)S(1)}, s32[2]{0:T(128)}, u32[]{:S(2)}) copy-start(s32[2]{0:T(128)} %own_offset_ref.1) | copy-start | bytes 28
  10.0 17.2 %copy-start.2 = (bf16[384,1152]{1,0:T(8,128)(2,1)S(1)}, bf16[384,1152]{1,0:T(8,128)(2,1)}, u32[]{:S(2)}) copy-start(bf16[384,1152]{1,0:T(8,128)(2,1)} %constant.71.clone.analysis_ref) | copy-start | bytes 2654212
  10.0 17.2 %copy-start.5 = (bf16[1152,384]{1,0:T(8,128)(2,1)S(1)}, bf16[1152,384]{1,0:T(8,128)(2,1)}, u32[]{:S(2)}) copy-start(bf16[1152,384]{1,0:T(8,128)(2,1)} %constant.69.clone.synthesis_ref) | copy-start | bytes 2654212
  10.0 17.2 %copy-start.7 = (s32[384,128]{1,0:T(8,128)S(1)}, s32[384,128]{1,0:T(8,128)}, u32[]{:S(2)}) copy-start(s32[384,128]{1,0:T(8,128)} %constant.72.clone.mode_ref) | copy-start | bytes 589828
  13.0 0.9 copy-start.11
  25.7 40.5 %collective-permute-start.2 = (f32[9,192,128]{2,1,0:T(8,128)}, f32[9,192,128]{2,1,0:T(8,128)}, u32[]{:S(2)}, u32[]{:S(2)}) collective-permute-start(f32[9,192,128]{2,1,0:T(8,128)} %get-tuple-element.24.own_ref), channel_id=1, source_target_pairs={{0,2},{1,3},{2,0},{3,1},{4,6},{5,7},{6,4},{7,5},{8,10},{9,11},{10,... | collective-permute-start | bytes 2654216 | tf_op jit(solution)/shard_map/ppermute | solution.py:822
  32.5 45.4 %all-to-all-start = ((f32[16,9,24,128]{3,2,1,0:T(8,128)}), f32[16,9,24,128]{3,2,1,0:T(8,128)S(1)}, u32[]{:S(2)}, u32[]{:S(2)}) async-start(f32[16,9,24,128]{3,2,1,0:T(8,128)} %phase_a_first.1), calls=%async_computation | async-start | bytes 3538944 | tf_op jit(solution)/shard_map/all_to_all | solution.py:802
  38.9 44.5 %collective-permute-start.3 = (f32[592,384]{1,0:T(8,128)}, f32[592,384]{1,0:T(8,128)S(1)}, u32[]{:S(2)}, u32[]{:S(2)}) collective-permute-start(f32[592,384]{1,0:T(8,128)} %copy-done.11), channel_id=1, source_target_pairs={{0,16},{16,0},{1,17},{17,1},{2,18},{18,2},{3,19},{19,3},{4,20},{20... | collective-permute-start | bytes 2727944 | tf_op jit(solution)/shard_map/ppermute | solution.py:25
  83.3 47.8 %copy-start.3 = (bf16[384,1152]{1,0:T(8,128)(2,1)S(1)}, bf16[384,1152]{1,0:T(8,128)(2,1)}, u32[]{:S(2)}) copy-start(bf16[384,1152]{1,0:T(8,128)(2,1)} %constant.71.clone.analysis_ref) | copy-start | bytes 2654212
  83.3 47.8 %copy-start.6 = (bf16[384,1152]{1,0:T(8,128)(2,1)S(1)}, bf16[384,1152]{1,0:T(8,128)(2,1)}, u32[]{:S(2)}) copy-start(bf16[384,1152]{1,0:T(8,128)(2,1)} %constant.70.clone.synthesis_ref) | copy-start | bytes 2654212
  83.3 47.8 %copy-start.8 = (s32[384,128]{1,0:T(8,128)S(1)}, s32[384,128]{1,0:T(8,128)}, u32[]{:S(2)}) copy-start(s32[384,128]{1,0:T(8,128)} %constant.72.clone.mode_ref) | copy-start | bytes 589828
  83.3 47.8 %copy-start.9 = (bf16[256,256]{1,0:T(8,128)(2,1)S(1)}, bf16[256,256]{1,0:T(8,128)(2,1)}, u32[]{:S(2)}) copy-start(bf16[256,256]{1,0:T(8,128)(2,1)} %constant.74.clone.moves_ref) | copy-start | bytes 393220
  168.5 46.4 %copy-start.1 = (f32[2,3,4,48,384]{4,3,2,1,0:T(8,128)S(1)}, f32[2,3,4,48,384]{4,3,2,1,0:T(8,128)}, u32[]{:S(2)}) copy-start(f32[2,3,4,48,384]{4,3,2,1,0:T(8,128)} %start_ref.5) | copy-start | bytes 5308420
